TPU v7x, 512 devices: a whole 4x8x8 slice. The times are simulated.
512 devices in a mesh: outer: 8 (over y_hi, core), inner: 8 (over x, y_lo), tensor: 8 (over z).
Axes of the slice: x: 4, y: 8 (y_hi: 4, y_lo: 2; y = y_hi * 2 + y_lo), z: 8, core: 2. Of those that a mesh axis runs over, the one named last changes fastest.
Arguments:
- queries: bfloat16 [8192, 48, 128], P(('outer', 'inner'), 'tensor'), may hold values from -6 to 6
- keys: bfloat16 [8192, 8, 128], P(('outer', 'inner')), may hold values from -6 to 6
- values: bfloat16 [8192, 8, 128], P(('outer', 'inner')), may hold values from -6 to 6
- outputs: bfloat16 [8192, 48, 128], P(('outer', 'inner'), 'tensor'), may hold values from -6 to 6
- out_grad: bfloat16 [8192, 48, 128], P(('outer', 'inner'), 'tensor'), may hold values from -6 to 6
- log_norm: float32 [48, 8192], P('tensor', ('outer', 'inner')), may hold values from 3 to 8
- parents: int32 [64], replicated, may hold values from 0 to 62, as said below
Outputs:
- query_grad: bfloat16 [8192, 48, 128], P(('outer', 'inner'), 'tensor')
- key_grad: bfloat16 [8192, 8, 128], P(('outer', 'inner'))
- value_grad: bfloat16 [8192, 8, 128], P(('outer', 'inner'))
Inputs may be any that keep to these rules, and one draw needn't show every extreme that they name: parents[b] <= b for every block b; a block with parents[b] = b starts a new rollout, every other block continues the prefix of its parent; the last block continues the block before it.
All inputs are finite; a program needn't handle non-finite values.
Results may differ from a plain program's by a relative error of at most 0.0049.
Values may be sent and summed in bfloat16 or wider, within the bound.
No kernel may reach another device: no remote copies, remote signals or barrier semaphores. Data moves between devices by JAX's collectives and lax.ppermute only.
A program may use at most 64 MiB of HBM per device.

v0:
```python
import jax
import jax.numpy as jnp
from jax import lax
from jax.sharding import PartitionSpec as P

BLK = 128


def from_behind(block, axis, distance):
    devices = range(lax.axis_size(axis))
    route = [((i - distance) % len(devices), i) for i in devices]
    return lax.ppermute(block, axis, route)


def ancestors(parents):
    block_count = parents.shape[0]
    block_ids = jnp.arange(block_count, dtype=jnp.int32)
    reach_table = (
        (parents[:, None] == block_ids[None, :]) | (block_ids[:, None] == block_ids[None, :])
    ).astype(jnp.int32)
    for rounds in range(max(block_count.bit_length(), 1)):
        reach_table = jnp.minimum(jnp.dot(reach_table, reach_table), 1)
    return reach_table


def attend(
    queries, out_grad, log_norms, row_dots, key_rows, value_rows, allowed, scaling, carry_state
):
    key_acc, value_acc, query_acc = carry_state
    scores = (
        jnp.einsum("thd,kd->thk", queries, key_rows, preferred_element_type=jnp.float32) * scaling
    )
    probabilities = jnp.where(
        allowed[:, None, :], jnp.exp(scores - log_norms[:, :, None]), jnp.float32(0.0)
    )
    probs_low = probabilities.astype(jnp.bfloat16)
    dprobs = jnp.einsum("thd,kd->thk", out_grad, value_rows, preferred_element_type=jnp.float32)
    dscores = (probabilities * (dprobs - row_dots[:, :, None]) * scaling).astype(jnp.bfloat16)
    query_acc = query_acc + jnp.einsum(
        "thk,kd->thd", dscores, key_rows, preferred_element_type=jnp.float32
    )
    key_acc = key_acc + jnp.einsum(
        "thk,thd->kd", dscores, queries, preferred_element_type=jnp.float32
    )
    value_acc = value_acc + jnp.einsum(
        "thk,thd->kd", probs_low, out_grad, preferred_element_type=jnp.float32
    )
    return (key_acc, value_acc, query_acc)


def body(queries, keys, values, outputs, out_grad, log_norm, parents):
    rows_dev, head_count, head_width = queries.shape
    n_outer = lax.axis_size("outer")
    n_inner = lax.axis_size("inner")
    outer_pos = lax.axis_index("outer")
    inner_pos = lax.axis_index("inner")
    kv_head = lax.axis_index("tensor")
    scaling = head_width ** (-0.5)
    key_own = lax.dynamic_index_in_dim(keys, kv_head, 1, keepdims=False)
    value_own = lax.dynamic_index_in_dim(values, kv_head, 1, keepdims=False)
    reach_table = ancestors(parents).astype(jnp.float32)
    block_ids = jnp.arange(parents.shape[0], dtype=jnp.int32)
    offsets = jnp.arange(rows_dev, dtype=jnp.int32)
    query_pos = (outer_pos * n_inner + inner_pos) * rows_dev + offsets
    query_select = ((query_pos // BLK)[:, None] == block_ids[None, :]).astype(jnp.float32)
    query_reach = jnp.dot(query_select, reach_table, precision=lax.Precision.HIGHEST)
    log_norms = log_norm.T
    row_dots = jnp.sum(out_grad.astype(jnp.float32) * outputs.astype(jnp.float32), axis=-1)
    query_acc = jnp.zeros((rows_dev, head_count, head_width), jnp.float32)
    key_rows, value_rows = (
        lax.all_gather(key_own, "inner", axis=0, tiled=True),
        lax.all_gather(value_own, "inner", axis=0, tiled=True),
    )
    span_rows = key_rows.shape[0]
    key_acc = jnp.zeros((span_rows, head_width), jnp.float32)
    value_acc = jnp.zeros((span_rows, head_width), jnp.float32)
    for turn in range(n_outer):
        group_index = (outer_pos + turn) % n_outer
        key_pos = group_index * span_rows + jnp.arange(span_rows, dtype=jnp.int32)
        key_select = ((key_pos // BLK)[:, None] == block_ids[None, :]).astype(jnp.float32)
        linked = jnp.dot(query_reach, key_select.T, precision=lax.Precision.HIGHEST)
        allowed = (linked > 0.5) & (query_pos[:, None] >= key_pos[None, :])
        active = jnp.min(key_pos) <= jnp.max(query_pos)

        def compute(state_in):
            return attend(
                queries,
                out_grad,
                log_norms,
                row_dots,
                key_rows,
                value_rows,
                allowed,
                scaling,
                state_in,
            )

        def keep(state_in):
            return state_in

        key_acc, value_acc, query_acc = lax.cond(
            active, compute, keep, (key_acc, value_acc, query_acc)
        )
        if turn + 1 < n_outer:
            key_rows, value_rows = from_behind((key_rows, value_rows), ("outer", "inner"), -n_inner)
            key_acc, value_acc = from_behind((key_acc, value_acc), ("outer", "inner"), -n_inner)
    key_part, value_part = (
        lax.psum_scatter(key_acc, "inner", scatter_dimension=0, tiled=True),
        lax.psum_scatter(value_acc, "inner", scatter_dimension=0, tiled=True),
    )
    key_final, value_final = (
        from_behind(key_part.astype(jnp.bfloat16), ("outer", "inner"), -n_inner).astype(
            key_part.dtype
        ),
        from_behind(value_part.astype(jnp.bfloat16), ("outer", "inner"), -n_inner).astype(
            value_part.dtype
        ),
    )
    head_slots = (jnp.arange(keys.shape[1], dtype=jnp.int32) == kv_head).astype(jnp.float32)
    key_terms = head_slots[None, :, None] * key_final[:, None, :]
    value_terms = head_slots[None, :, None] * value_final[:, None, :]
    key_total, value_total = (
        lax.psum(key_terms.astype(jnp.bfloat16), "tensor").astype(jnp.float32),
        lax.psum(value_terms.astype(jnp.bfloat16), "tensor").astype(jnp.float32),
    )
    key_grad = key_total.astype(jnp.bfloat16)
    value_grad = value_total.astype(jnp.bfloat16)
    return (query_acc.astype(jnp.bfloat16), key_grad, value_grad)


def solution(mesh):
    in_specs = (
        P(("outer", "inner"), "tensor", None),
        P(("outer", "inner"), None, None),
        P(("outer", "inner"), None, None),
        P(("outer", "inner"), "tensor", None),
        P(("outer", "inner"), "tensor", None),
        P("tensor", ("outer", "inner")),
        P(),
    )
    out_specs = (
        P(("outer", "inner"), "tensor", None),
        P(("outer", "inner"), None, None),
        P(("outer", "inner"), None, None),
    )
    return jax.shard_map(body, mesh=mesh, in_specs=in_specs, out_specs=out_specs, check_vma=False)
```

profile of v0, /device:TPU:6, one launch (start us, length us, event | category | flops | bytes accessed | tf_op | source)
XLA Modules:
  0.0 582.2 jit_solution(4722396955379101616)
XLA Ops:
  10.9 31.9 %all-gather = bf16[1024,1,128]{2,0,1:T(8,128)(2,1)S(1)} all-gather(bf16[128,1,128]{2,0,1:T(8,128)(2,1)S(1)} %copy.44), channel_id=2, replica_groups=mesh['outer'=8,'inner'=8,'tensor'=8] {'inner'}, dimensions={0}, use_global_device_ids=true | all-gather | bytes 294912 | tf_op jit(solution)/shard_map/all_gather | solution.py:71
  43.8 30.7 %all-gather.1 = bf16[1024,1,128]{2,0,1:T(8,128)(2,1)} all-gather(bf16[128,1,128]{2,0,1:T(8,128)(2,1)S(1)} %copy.45), channel_id=3, replica_groups=mesh['outer'=8,'inner'=8,'tensor'=8] {'inner'}, dimensions={0}, use_global_device_ids=true | all-gather | bytes 294912 | tf_op jit(solution)/shard_map/all_gather | solution.py:72
  78.0 6.1 %conditional.8 = (f32[1024,128]{1,0:T(8,128)S(1)}, f32[1024,128]{1,0:T(8,128)S(1)}, f32[128,6,128]{2,0,1:T(8,128)S(1)}) conditional(s32[]{:T(128)} %convert_element_type.136, () %tuple.75, (f32[128,1024]{1,0:T(8,128)S(1)}, bf16[128,6,128]{2,0,1:T(8,128)(2,1)}, bf16[1024,128]{1,0:T(8,128)(2,1)S(1)}, f32[128,6]{0,1:T(8,128)}, ...), branch_computations={%region_10.11_spmd, %region_11.12_spmd} | conditional | flops 1015676928 | bytes 20211308 | solution.py:101
  79.8 2.1 multiply_convert_fusion
  84.1 1.9 collective-permute-start
  86.0 1.9 collective-permute-start.1
  87.9 1.9 collective-permute-start.2
  89.8 3.3 collective-permute-start.3
  95.7 2.3 collective-permute-done
  98.1 10.9 %collective-permute-done.1 = f32[1024,128]{1,0:T(8,128)} collective-permute-done((f32[1024,128]{1,0:T(8,128)S(1)}, f32[1024,128]{1,0:T(8,128)}, u32[]{:S(2)}, u32[]{:S(2)}) %collective-permute-start.1) | collective-permute-done | bytes 524320 | tf_op jit(solution)/shard_map/ppermute | solution.py:12
  109.0 9.1 %collective-permute-done.2 = bf16[1024,128]{1,0:T(8,128)(2,1)S(1)} collective-permute-done((bf16[1024,128]{1,0:T(8,128)(2,1)S(1)}, bf16[1024,128]{1,0:T(8,128)(2,1)S(1)}, u32[]{:S(2)}, u32[]{:S(2)}) %collective-permute-start.2) | collective-permute-done | bytes 262176 | tf_op jit(solution)/shard_map/ppermute | solution.py:12
  118.1 2.9 collective-permute-done.3
  120.9 14.6 %collective-permute-start.4 = (f32[1024,128]{1,0:T(8,128)}, f32[1024,128]{1,0:T(8,128)S(1)}, u32[]{:S(2)}, u32[]{:S(2)}) collective-permute-start(f32[1024,128]{1,0:T(8,128)} %get-tuple-element.317), channel_id=1, source_target_pairs={{64,0},{72,8},{80,16},{88,24},{96,32},{104,40},{112,48},{120,56},{... | collective-permute-start | bytes 1572872 | tf_op jit(solution)/shard_map/ppermute | solution.py:12
  135.6 1.9 collective-permute-start.5
  137.5 1.9 collective-permute-start.6
  139.5 2.4 collective-permute-start.7
  144.4 5.2 collective-permute-done.4
  149.6 5.8 collective-permute-done.5
  155.4 8.4 %collective-permute-done.6 = bf16[1024,128]{1,0:T(8,128)(2,1)S(1)} collective-permute-done((bf16[1024,128]{1,0:T(8,128)(2,1)S(1)}, bf16[1024,128]{1,0:T(8,128)(2,1)S(1)}, u32[]{:S(2)}, u32[]{:S(2)}) %collective-permute-start.6) | collective-permute-done | bytes 262176 | tf_op jit(solution)/shard_map/ppermute | solution.py:12
  163.8 2.8 collective-permute-done.7
  166.6 13.0 %collective-permute-start.8 = (f32[1024,128]{1,0:T(8,128)S(1)}, f32[1024,128]{1,0:T(8,128)S(1)}, u32[]{:S(2)}, u32[]{:S(2)}) collective-permute-start(f32[1024,128]{1,0:T(8,128)S(1)} %get-tuple-element.320), channel_id=1, source_target_pairs={{64,0},{72,8},{80,16},{88,24},{96,32},{104,40},{112,48},{120,56},{... | collective-permute-start | bytes 1572872 | tf_op jit(solution)/shard_map/ppermute | solution.py:12
  179.7 1.9 collective-permute-start.9
  181.6 1.9 collective-permute-start.10
  183.5 1.9 collective-permute-start.11
  188.1 16.2 %collective-permute-done.9 = f32[1024,128]{1,0:T(8,128)} collective-permute-done((f32[1024,128]{1,0:T(8,128)}, f32[1024,128]{1,0:T(8,128)}, u32[]{:S(2)}, u32[]{:S(2)}) %collective-permute-start.9) | collective-permute-done | bytes 524320 | tf_op jit(solution)/shard_map/ppermute | solution.py:12
  204.2 2.7 collective-permute-done.10
  206.9 7.6 %collective-permute-done.11 = bf16[1024,128]{1,0:T(8,128)(2,1)} collective-permute-done((bf16[1024,128]{1,0:T(8,128)(2,1)S(1)}, bf16[1024,128]{1,0:T(8,128)(2,1)}, u32[]{:S(2)}, u32[]{:S(2)}) %collective-permute-start.11) | collective-permute-done | bytes 262176 | tf_op jit(solution)/shard_map/ppermute | solution.py:12
  214.5 14.1 %collective-permute-start.12 = (f32[1024,128]{1,0:T(8,128)S(1)}, f32[1024,128]{1,0:T(8,128)S(1)}, u32[]{:S(2)}, u32[]{:S(2)}) collective-permute-start(f32[1024,128]{1,0:T(8,128)S(1)} %get-tuple-element.323), channel_id=1, source_target_pairs={{64,0},{72,8},{80,16},{88,24},{96,32},{104,40},{112,48},{120,56},{... | collective-permute-start | bytes 1572872 | tf_op jit(solution)/shard_map/ppermute | solution.py:12
  228.6 1.9 collective-permute-start.13
  230.5 1.9 collective-permute-start.14
  232.5 1.9 collective-permute-start.15
  237.0 11.8 %collective-permute-done.12 = f32[1024,128]{1,0:T(8,128)S(1)} collective-permute-done((f32[1024,128]{1,0:T(8,128)S(1)}, f32[1024,128]{1,0:T(8,128)S(1)}, u32[]{:S(2)}, u32[]{:S(2)}) %collective-permute-start.12) | collective-permute-done | bytes 524320 | tf_op jit(solution)/shard_map/ppermute | solution.py:12
  248.7 9.1 %collective-permute-done.13 = f32[1024,128]{1,0:T(8,128)} collective-permute-done((f32[1024,128]{1,0:T(8,128)}, f32[1024,128]{1,0:T(8,128)}, u32[]{:S(2)}, u32[]{:S(2)}) %collective-permute-start.13) | collective-permute-done | bytes 524320 | tf_op jit(solution)/shard_map/ppermute | solution.py:12
  257.8 2.7 collective-permute-done.14
  260.5 2.9 collective-permute-done.15
  263.6 12.9 %collective-permute-start.16 = (f32[1024,128]{1,0:T(8,128)S(1)}, f32[1024,128]{1,0:T(8,128)S(1)}, u32[]{:S(2)}, u32[]{:S(2)}) collective-permute-start(f32[1024,128]{1,0:T(8,128)S(1)} %get-tuple-element.326), channel_id=1, source_target_pairs={{64,0},{72,8},{80,16},{88,24},{96,32},{104,40},{112,48},{120,56},{... | collective-permute-start | bytes 1572872 | tf_op jit(solution)/shard_map/ppermute | solution.py:12
  276.5 1.9 collective-permute-start.17
  278.4 1.9 collective-permute-start.18
  280.4 1.9 collective-permute-start.19
  284.9 11.3 %collective-permute-done.17 = f32[1024,128]{1,0:T(8,128)} collective-permute-done((f32[1024,128]{1,0:T(8,128)}, f32[1024,128]{1,0:T(8,128)}, u32[]{:S(2)}, u32[]{:S(2)}) %collective-permute-start.17) | collective-permute-done | bytes 524320 | tf_op jit(solution)/shard_map/ppermute | solution.py:12
  296.1 2.7 collective-permute-done.18
  298.9 2.8 collective-permute-done.19
  301.7 14.1 %collective-permute-start.20 = (f32[1024,128]{1,0:T(8,128)S(1)}, f32[1024,128]{1,0:T(8,128)}, u32[]{:S(2)}, u32[]{:S(2)}) collective-permute-start(f32[1024,128]{1,0:T(8,128)S(1)} %get-tuple-element.329), channel_id=1, source_target_pairs={{64,0},{72,8},{80,16},{88,24},{96,32},{104,40},{112,48},{120,56},{... | collective-permute-start | bytes 1572872 | tf_op jit(solution)/shard_map/ppermute | solution.py:12
  315.8 1.9 collective-permute-start.21
  317.7 1.9 collective-permute-start.22
  319.6 1.9 collective-permute-start.23
  324.1 1.8 collective-permute-done.20
  325.9 12.7 %collective-permute-done.21 = f32[1024,128]{1,0:T(8,128)S(1)} collective-permute-done((f32[1024,128]{1,0:T(8,128)}, f32[1024,128]{1,0:T(8,128)S(1)}, u32[]{:S(2)}, u32[]{:S(2)}) %collective-permute-start.21) | collective-permute-done | bytes 524320 | tf_op jit(solution)/shard_map/ppermute | solution.py:12
  338.6 2.7 collective-permute-done.22
  341.3 2.9 collective-permute-done.23
  344.5 12.9 %collective-permute-start.24 = (f32[1024,128]{1,0:T(8,128)}, f32[1024,128]{1,0:T(8,128)S(1)}, u32[]{:S(2)}, u32[]{:S(2)}) collective-permute-start(f32[1024,128]{1,0:T(8,128)} %get-tuple-element.332), channel_id=1, source_target_pairs={{64,0},{72,8},{80,16},{88,24},{96,32},{104,40},{112,48},{120,56},{... | collective-permute-start | bytes 1572872 | tf_op jit(solution)/shard_map/ppermute | solution.py:12
  357.4 1.9 collective-permute-start.25
  359.3 1.9 collective-permute-start.26
  361.3 1.9 collective-permute-start.27
  365.7 3.8 collective-permute-done.24
  369.5 14.1 %collective-permute-done.25 = f32[1024,128]{1,0:T(8,128)S(1)} collective-permute-done((f32[1024,128]{1,0:T(8,128)}, f32[1024,128]{1,0:T(8,128)S(1)}, u32[]{:S(2)}, u32[]{:S(2)}) %collective-permute-start.25) | collective-permute-done | bytes 524320 | tf_op jit(solution)/shard_map/ppermute | solution.py:12
  383.6 2.7 collective-permute-done.26
  386.3 2.8 collective-permute-done.27
  390.8 50.1 %reduce-scatter.3.cloned.1.call-done = f32[128,128]{1,0:T(8,128)} async-done(((f32[1024,128]{1,0:T(8,128)}), f32[128,128]{1,0:T(8,128)}) %reduce-scatter.3.cloned.1.call-update) | async-done | bytes 65552 | tf_op jit(solution)/shard_map/reduce_scatter | solution.py:108
  441.7 1.9 collective-permute-start.28
  443.6 41.9 %reduce-scatter.5.cloned.1.call-done = f32[128,128]{1,0:T(8,128)} async-done(((f32[1024,128]{1,0:T(8,128)}), f32[128,128]{1,0:T(8,128)}) %reduce-scatter.5.cloned.1.call-update) | async-done | bytes 65552 | tf_op jit(solution)/shard_map/reduce_scatter | solution.py:109
  486.4 1.9 collective-permute-start.29
  491.5 80.5 %all-reduce.3.cloned.1.call-done = (bf16[128,8,128]{2,1,0:T(8,128)(2,1)}, bf16[128,8,128]{2,1,0:T(8,128)(2,1)}) async-done(((bf16[128,8,128]{2,1,0:T(8,128)(2,1)}, bf16[128,8,128]{2,1,0:T(8,128)(2,1)}), (bf16[128,8,128]{2,1,0:T(8,128)(2,1)}, bf16[128,8,128]{2,1,0:T(8,128)(2,1)})) %all-reduce.3.cloned.1.call-update) | async-done | bytes 524304 | tf_op jit(solution)/shard_map/psum | solution.py:123
  572.1 1.7 copy.96
  (87 shorter events, 28.0 us)
Async XLA Ops:
  7.2 3.6 copy-start
  7.2 433.7 %reduce-scatter.3.cloned.1.call-start = ((), (), s32[]{:S(2)}) async-start(), calls=%async_computation.2 | async-start | bytes 589824 | tf_op jit(solution)/shard_map/reduce_scatter | solution.py:108
  78.0 1.7 copy-start.11
  78.0 1.7 copy-start.20
  79.7 2.2 copy-start.1
  84.1 14.0 %collective-permute-start = (f32[1024,128]{1,0:T(8,128)S(1)}, f32[1024,128]{1,0:T(8,128)}, u32[]{:S(2)}, u32[]{:S(2)}) collective-permute-start(f32[1024,128]{1,0:T(8,128)S(1)} %get-tuple-element.314), channel_id=1, source_target_pairs={{64,0},{72,8},{80,16},{88,24},{96,32},{104,40},{112,48},{120,56},{... | collective-permute-start | bytes 1572872 | tf_op jit(solution)/shard_map/ppermute | solution.py:12
  86.0 23.0 %collective-permute-start.1 = (f32[1024,128]{1,0:T(8,128)S(1)}, f32[1024,128]{1,0:T(8,128)}, u32[]{:S(2)}, u32[]{:S(2)}) collective-permute-start(f32[1024,128]{1,0:T(8,128)S(1)} %get-tuple-element.315), channel_id=1, source_target_pairs={{64,0},{72,8},{80,16},{88,24},{96,32},{104,40},{112,48},{120,56},{... | collective-permute-start | bytes 1572872 | tf_op jit(solution)/shard_map/ppermute | solution.py:12
  87.9 30.1 %collective-permute-start.2 = (bf16[1024,128]{1,0:T(8,128)(2,1)S(1)}, bf16[1024,128]{1,0:T(8,128)(2,1)S(1)}, u32[]{:S(2)}, u32[]{:S(2)}) collective-permute-start(bf16[1024,128]{1,0:T(8,128)(2,1)S(1)} %bitcast.191), channel_id=1, source_target_pairs={{64,0},{72,8},{80,16},{88,24},{96,32},{104,40},{112,48},{120,56},{... | collective-permute-start | bytes 786440 | tf_op jit(solution)/shard_map/ppermute | solution.py:12
  89.8 31.1 %collective-permute-start.3 = (bf16[1024,128]{1,0:T(8,128)(2,1)}, bf16[1024,128]{1,0:T(8,128)(2,1)S(1)}, u32[]{:S(2)}, u32[]{:S(2)}) collective-permute-start(bf16[1024,128]{1,0:T(8,128)(2,1)} %bitcast.34), channel_id=1, source_target_pairs={{64,0},{72,8},{80,16},{88,24},{96,32},{104,40},{112,48},{120,56},{... | collective-permute-start | bytes 786440 | tf_op jit(solution)/shard_map/ppermute | solution.py:12
  120.9 28.7 %collective-permute-start.4 = (f32[1024,128]{1,0:T(8,128)}, f32[1024,128]{1,0:T(8,128)S(1)}, u32[]{:S(2)}, u32[]{:S(2)}) collective-permute-start(f32[1024,128]{1,0:T(8,128)} %get-tuple-element.317), channel_id=1, source_target_pairs={{64,0},{72,8},{80,16},{88,24},{96,32},{104,40},{112,48},{120,56},{... | collective-permute-start | bytes 1572872 | tf_op jit(solution)/shard_map/ppermute | solution.py:12
  135.6 19.8 %collective-permute-start.5 = (f32[1024,128]{1,0:T(8,128)}, f32[1024,128]{1,0:T(8,128)}, u32[]{:S(2)}, u32[]{:S(2)}) collective-permute-start(f32[1024,128]{1,0:T(8,128)} %get-tuple-element.318), channel_id=1, source_target_pairs={{64,0},{72,8},{80,16},{88,24},{96,32},{104,40},{112,48},{120,56},{... | collective-permute-start | bytes 1572872 | tf_op jit(solution)/shard_map/ppermute | solution.py:12
  137.5 26.3 %collective-permute-start.6 = (bf16[1024,128]{1,0:T(8,128)(2,1)S(1)}, bf16[1024,128]{1,0:T(8,128)(2,1)S(1)}, u32[]{:S(2)}, u32[]{:S(2)}) collective-permute-start(bf16[1024,128]{1,0:T(8,128)(2,1)S(1)} %collective-permute-done.2), channel_id=1, source_target_pairs={{64,0},{72,8},{80,16},{88,24},{96,32},{104,40},{112,48},{120,56},{... | collective-permute-start | bytes 786440 | tf_op jit(solution)/shard_map/ppermute | solution.py:12
  139.5 27.1 %collective-permute-start.7 = (bf16[1024,128]{1,0:T(8,128)(2,1)S(1)}, bf16[1024,128]{1,0:T(8,128)(2,1)S(1)}, u32[]{:S(2)}, u32[]{:S(2)}) collective-permute-start(bf16[1024,128]{1,0:T(8,128)(2,1)S(1)} %collective-permute-done.3), channel_id=1, source_target_pairs={{64,0},{72,8},{80,16},{88,24},{96,32},{104,40},{112,48},{120,56},{... | collective-permute-start | bytes 786440 | tf_op jit(solution)/shard_map/ppermute | solution.py:12
  166.6 21.5 %collective-permute-start.8 = (f32[1024,128]{1,0:T(8,128)S(1)}, f32[1024,128]{1,0:T(8,128)S(1)}, u32[]{:S(2)}, u32[]{:S(2)}) collective-permute-start(f32[1024,128]{1,0:T(8,128)S(1)} %get-tuple-element.320), channel_id=1, source_target_pairs={{64,0},{72,8},{80,16},{88,24},{96,32},{104,40},{112,48},{120,56},{... | collective-permute-start | bytes 1572872 | tf_op jit(solution)/shard_map/ppermute | solution.py:12
  179.7 24.6 %collective-permute-start.9 = (f32[1024,128]{1,0:T(8,128)}, f32[1024,128]{1,0:T(8,128)}, u32[]{:S(2)}, u32[]{:S(2)}) collective-permute-start(f32[1024,128]{1,0:T(8,128)} %get-tuple-element.321), channel_id=1, source_target_pairs={{64,0},{72,8},{80,16},{88,24},{96,32},{104,40},{112,48},{120,56},{... | collective-permute-start | bytes 1572872 | tf_op jit(solution)/shard_map/ppermute | solution.py:12
  181.6 25.3 %collective-permute-start.10 = (bf16[1024,128]{1,0:T(8,128)(2,1)S(1)}, bf16[1024,128]{1,0:T(8,128)(2,1)S(1)}, u32[]{:S(2)}, u32[]{:S(2)}) collective-permute-start(bf16[1024,128]{1,0:T(8,128)(2,1)S(1)} %collective-permute-done.6), channel_id=1, source_target_pairs={{64,0},{72,8},{80,16},{88,24},{96,32},{104,40},{112,48},{120,56},{... | collective-permute-start | bytes 786440 | tf_op jit(solution)/shard_map/ppermute | solution.py:12
  183.5 31.0 %collective-permute-start.11 = (bf16[1024,128]{1,0:T(8,128)(2,1)S(1)}, bf16[1024,128]{1,0:T(8,128)(2,1)}, u32[]{:S(2)}, u32[]{:S(2)}) collective-permute-start(bf16[1024,128]{1,0:T(8,128)(2,1)S(1)} %collective-permute-done.7), channel_id=1, source_target_pairs={{64,0},{72,8},{80,16},{88,24},{96,32},{104,40},{112,48},{120,56},{... | collective-permute-start | bytes 786440 | tf_op jit(solution)/shard_map/ppermute | solution.py:12
  214.5 34.2 %collective-permute-start.12 = (f32[1024,128]{1,0:T(8,128)S(1)}, f32[1024,128]{1,0:T(8,128)S(1)}, u32[]{:S(2)}, u32[]{:S(2)}) collective-permute-start(f32[1024,128]{1,0:T(8,128)S(1)} %get-tuple-element.323), channel_id=1, source_target_pairs={{64,0},{72,8},{80,16},{88,24},{96,32},{104,40},{112,48},{120,56},{... | collective-permute-start | bytes 1572872 | tf_op jit(solution)/shard_map/ppermute | solution.py:12
  228.6 29.2 %collective-permute-start.13 = (f32[1024,128]{1,0:T(8,128)}, f32[1024,128]{1,0:T(8,128)}, u32[]{:S(2)}, u32[]{:S(2)}) collective-permute-start(f32[1024,128]{1,0:T(8,128)} %get-tuple-element.324), channel_id=1, source_target_pairs={{64,0},{72,8},{80,16},{88,24},{96,32},{104,40},{112,48},{120,56},{... | collective-permute-start | bytes 1572872 | tf_op jit(solution)/shard_map/ppermute | solution.py:12
  230.5 30.0 %collective-permute-start.14 = (bf16[1024,128]{1,0:T(8,128)(2,1)S(1)}, bf16[1024,128]{1,0:T(8,128)(2,1)S(1)}, u32[]{:S(2)}, u32[]{:S(2)}) collective-permute-start(bf16[1024,128]{1,0:T(8,128)(2,1)S(1)} %collective-permute-done.10), channel_id=1, source_target_pairs={{64,0},{72,8},{80,16},{88,24},{96,32},{104,40},{112,48},{120,56},{... | collective-permute-start | bytes 786440 | tf_op jit(solution)/shard_map/ppermute | solution.py:12
  232.5 30.9 %collective-permute-start.15 = (bf16[1024,128]{1,0:T(8,128)(2,1)}, bf16[1024,128]{1,0:T(8,128)(2,1)S(1)}, u32[]{:S(2)}, u32[]{:S(2)}) collective-permute-start(bf16[1024,128]{1,0:T(8,128)(2,1)} %collective-permute-done.11), channel_id=1, source_target_pairs={{64,0},{72,8},{80,16},{88,24},{96,32},{104,40},{112,48},{120,56},{... | collective-permute-start | bytes 786440 | tf_op jit(solution)/shard_map/ppermute | solution.py:12
  263.6 21.3 %collective-permute-start.16 = (f32[1024,128]{1,0:T(8,128)S(1)}, f32[1024,128]{1,0:T(8,128)S(1)}, u32[]{:S(2)}, u32[]{:S(2)}) collective-permute-start(f32[1024,128]{1,0:T(8,128)S(1)} %get-tuple-element.326), channel_id=1, source_target_pairs={{64,0},{72,8},{80,16},{88,24},{96,32},{104,40},{112,48},{120,56},{... | collective-permute-start | bytes 1572872 | tf_op jit(solution)/shard_map/ppermute | solution.py:12
  276.5 19.7 %collective-permute-start.17 = (f32[1024,128]{1,0:T(8,128)}, f32[1024,128]{1,0:T(8,128)}, u32[]{:S(2)}, u32[]{:S(2)}) collective-permute-start(f32[1024,128]{1,0:T(8,128)} %get-tuple-element.327), channel_id=1, source_target_pairs={{64,0},{72,8},{80,16},{88,24},{96,32},{104,40},{112,48},{120,56},{... | collective-permute-start | bytes 1572872 | tf_op jit(solution)/shard_map/ppermute | solution.py:12
  278.4 20.4 %collective-permute-start.18 = (bf16[1024,128]{1,0:T(8,128)(2,1)S(1)}, bf16[1024,128]{1,0:T(8,128)(2,1)S(1)}, u32[]{:S(2)}, u32[]{:S(2)}) collective-permute-start(bf16[1024,128]{1,0:T(8,128)(2,1)S(1)} %collective-permute-done.14), channel_id=1, source_target_pairs={{64,0},{72,8},{80,16},{88,24},{96,32},{104,40},{112,48},{120,56},{... | collective-permute-start | bytes 786440 | tf_op jit(solution)/shard_map/ppermute | solution.py:12
  280.4 21.3 %collective-permute-start.19 = (bf16[1024,128]{1,0:T(8,128)(2,1)S(1)}, bf16[1024,128]{1,0:T(8,128)(2,1)}, u32[]{:S(2)}, u32[]{:S(2)}) collective-permute-start(bf16[1024,128]{1,0:T(8,128)(2,1)S(1)} %collective-permute-done.15), channel_id=1, source_target_pairs={{64,0},{72,8},{80,16},{88,24},{96,32},{104,40},{112,48},{120,56},{... | collective-permute-start | bytes 786440 | tf_op jit(solution)/shard_map/ppermute | solution.py:12
  301.7 24.2 %collective-permute-start.20 = (f32[1024,128]{1,0:T(8,128)S(1)}, f32[1024,128]{1,0:T(8,128)}, u32[]{:S(2)}, u32[]{:S(2)}) collective-permute-start(f32[1024,128]{1,0:T(8,128)S(1)} %get-tuple-element.329), channel_id=1, source_target_pairs={{64,0},{72,8},{80,16},{88,24},{96,32},{104,40},{112,48},{120,56},{... | collective-permute-start | bytes 1572872 | tf_op jit(solution)/shard_map/ppermute | solution.py:12
  315.8 22.9 %collective-permute-start.21 = (f32[1024,128]{1,0:T(8,128)}, f32[1024,128]{1,0:T(8,128)S(1)}, u32[]{:S(2)}, u32[]{:S(2)}) collective-permute-start(f32[1024,128]{1,0:T(8,128)} %get-tuple-element.330), channel_id=1, source_target_pairs={{64,0},{72,8},{80,16},{88,24},{96,32},{104,40},{112,48},{120,56},{... | collective-permute-start | bytes 1572872 | tf_op jit(solution)/shard_map/ppermute | solution.py:12
  317.7 23.6 %collective-permute-start.22 = (bf16[1024,128]{1,0:T(8,128)(2,1)S(1)}, bf16[1024,128]{1,0:T(8,128)(2,1)S(1)}, u32[]{:S(2)}, u32[]{:S(2)}) collective-permute-start(bf16[1024,128]{1,0:T(8,128)(2,1)S(1)} %collective-permute-done.18), channel_id=1, source_target_pairs={{64,0},{72,8},{80,16},{88,24},{96,32},{104,40},{112,48},{120,56},{... | collective-permute-start | bytes 786440 | tf_op jit(solution)/shard_map/ppermute | solution.py:12
  319.6 24.6 %collective-permute-start.23 = (bf16[1024,128]{1,0:T(8,128)(2,1)}, bf16[1024,128]{1,0:T(8,128)(2,1)S(1)}, u32[]{:S(2)}, u32[]{:S(2)}) collective-permute-start(bf16[1024,128]{1,0:T(8,128)(2,1)} %collective-permute-done.19), channel_id=1, source_target_pairs={{64,0},{72,8},{80,16},{88,24},{96,32},{104,40},{112,48},{120,56},{... | collective-permute-start | bytes 786440 | tf_op jit(solution)/shard_map/ppermute | solution.py:12
  344.5 12.9 %copy-start.19 = (f32[1024,128]{1,0:T(8,128)}, f32[1024,128]{1,0:T(8,128)S(1)}, u32[]{:S(2)}) copy-start(f32[1024,128]{1,0:T(8,128)S(1)} %get-tuple-element.333) | copy-start | bytes 1572868
  344.5 25.0 %collective-permute-start.24 = (f32[1024,128]{1,0:T(8,128)}, f32[1024,128]{1,0:T(8,128)S(1)}, u32[]{:S(2)}, u32[]{:S(2)}) collective-permute-start(f32[1024,128]{1,0:T(8,128)} %get-tuple-element.332), channel_id=1, source_target_pairs={{64,0},{72,8},{80,16},{88,24},{96,32},{104,40},{112,48},{120,56},{... | collective-permute-start | bytes 1572872 | tf_op jit(solution)/shard_map/ppermute | solution.py:12
  357.4 26.3 %collective-permute-start.25 = (f32[1024,128]{1,0:T(8,128)}, f32[1024,128]{1,0:T(8,128)S(1)}, u32[]{:S(2)}, u32[]{:S(2)}) collective-permute-start(f32[1024,128]{1,0:T(8,128)} %copy-done.19), channel_id=1, source_target_pairs={{64,0},{72,8},{80,16},{88,24},{96,32},{104,40},{112,48},{120,56},{... | collective-permute-start | bytes 1572872 | tf_op jit(solution)/shard_map/ppermute | solution.py:12
  359.3 27.0 %collective-permute-start.26 = (bf16[1024,128]{1,0:T(8,128)(2,1)S(1)}, bf16[1024,128]{1,0:T(8,128)(2,1)S(1)}, u32[]{:S(2)}, u32[]{:S(2)}) collective-permute-start(bf16[1024,128]{1,0:T(8,128)(2,1)S(1)} %collective-permute-done.22), channel_id=1, source_target_pairs={{64,0},{72,8},{80,16},{88,24},{96,32},{104,40},{112,48},{120,56},{... | collective-permute-start | bytes 786440 | tf_op jit(solution)/shard_map/ppermute | solution.py:12
  361.3 27.9 %collective-permute-start.27 = (bf16[1024,128]{1,0:T(8,128)(2,1)S(1)}, bf16[1024,128]{1,0:T(8,128)(2,1)}, u32[]{:S(2)}, u32[]{:S(2)}) collective-permute-start(bf16[1024,128]{1,0:T(8,128)(2,1)S(1)} %collective-permute-done.23), channel_id=1, source_target_pairs={{64,0},{72,8},{80,16},{88,24},{96,32},{104,40},{112,48},{120,56},{... | collective-permute-start | bytes 786440 | tf_op jit(solution)/shard_map/ppermute | solution.py:12
  389.1 0.8 copy-start.9
  389.1 1.0 copy-start.10
  390.0 95.6 %reduce-scatter.5.cloned.1.call-start = ((), (), s32[]{:S(2)}) async-start(), calls=%async_computation.3 | async-start | bytes 589824 | tf_op jit(solution)/shard_map/reduce_scatter | solution.py:109
  390.7 181.4 %all-reduce.3.cloned.1.call-start = ((), (), s32[]{:S(2)}) async-start(), calls=%async_computation.4 | async-start | bytes 1048576 | tf_op jit(solution)/shard_map/psum | solution.py:123
  441.7 46.6 %collective-permute-start.28 = (bf16[128,128]{1,0:T(8,128)(2,1)S(1)}, bf16[128,128]{1,0:T(8,128)(2,1)S(1)}, u32[]{:S(2)}, u32[]{:S(2)}) collective-permute-start(bf16[128,128]{1,0:T(8,128)(2,1)S(1)} %convert_element_type.142), channel_id=1, source_target_pairs={{64,0},{72,8},{80,16},{88,24},{96,32},{104,40},{112,48},{120,56},{... | collective-permute-start | bytes 98312 | tf_op jit(solution)/shard_map/ppermute | solution.py:12
  486.4 3.5 collective-permute-start.29
Sparse Core Ops, SparseCore 0:
  390.1 50.7 reduce-scatter.2
  443.9 41.6 reduce-scatter.4
  491.0 81.0 all-reduce.2
where the time goes:
time: 592 us; the launch traced here: 582 us
  waiting for transfers between devices  335 us (57%)
  starting transfers between devices  130 us (22%)
  blocking collectives  62.6 us (11%)
  between operations  25 us (4%)
  matrix products  13.1 us (2%)
  other arithmetic  10.5 us (2%)
    ppermute x30, waiting for transfers between devices, from_behind(): return lax.ppermute(block, axis, route)  162 us
    ppermute x30, starting transfers between devices, from_behind(): return lax.ppermute(block, axis, route)  130 us
    psum x1, waiting for transfers between devices, body(): lax.psum(key_terms.astype(jnp.bfloat16), 'tensor').astype(jnp.float32)  80.5 us
    reduce_scatter x1, waiting for transfers between devices, body(): lax.psum_scatter(key_acc, 'inner', scatter_dimension=0, tiled=True)  50.1 us
    reduce_scatter x1, waiting for transfers between devices, body(): lax.psum_scatter(value_acc, 'inner', scatter_dimension=0, tiled=True)  41.9 us
    all_gather x1, blocking collectives, body(): lax.all_gather(key_own, 'inner', axis=0, tiled=True)  31.9 us
    all_gather x1, blocking collectives, body(): lax.all_gather(value_own, 'inner', axis=0, tiled=True)  30.7 us
  transfers between devices with their start and end apart: 33, of which 30 were waited for; matrix products, arithmetic and copies ran while one was open for 2% of the time, Pallas kernels for 0%

commit v1 on v0

v1 whole, which is shorter than its diff:
```python
import functools

import jax
import jax.numpy as jnp
from jax import lax
from jax.experimental import pallas as pl
from jax.experimental.pallas import tpu as pltpu
from jax.sharding import Mesh, PartitionSpec as P

BLK = 128
HD = 128
HEADS = 6
ROWS = HEADS * BLK
NBLK = 64
KVH = 8
Y = ("yh", "yl")
STAT_ROWS = 16
PACK_ROWS = 2 * ROWS + 6 * STAT_ROWS
SCALING = HD ** -0.5
LOG2E = 1.4426950408889634
CHUNK = 2 * BLK
F32 = jnp.float32
BF16 = jnp.bfloat16


def shift(block, axis, distance):
    size = lax.axis_size(axis)
    return lax.ppermute(block, axis, [(i, (i + distance) % size) for i in range(size)])


def vmem(count):
    return [pl.BlockSpec(memory_space=pltpu.VMEM)] * count


def smem(count):
    return [pl.BlockSpec(memory_space=pltpu.SMEM)] * count


def prepare_kernel(where, parents, q_ref, do_ref, o_ref, ln_ref, pack_ref, reach_ref, stat):
    def clear(i, carry):
        reach_ref[i] = 0
        return carry

    lax.fori_loop(0, 2 * NBLK, clear, 0)
    for side in range(2):

        def climb(state, side=side):
            block, _ = state
            reach_ref[side * NBLK + block] = 1
            above = parents[block]
            return above, above != block

        lax.while_loop(lambda state: state[1], climb, (where[side], True))

    q = jnp.swapaxes(q_ref[...].astype(F32), 0, 1)
    do = jnp.swapaxes(do_ref[...].astype(F32), 0, 1)
    o = jnp.swapaxes(o_ref[...].astype(F32), 0, 1)
    pack_ref[0:ROWS] = q.reshape(ROWS, HD).astype(BF16)
    pack_ref[ROWS : 2 * ROWS] = do.reshape(ROWS, HD).astype(BF16)
    stat[...] = jnp.zeros_like(stat)
    stat[0, 0:HEADS] = ln_ref[...]
    prod = do * o
    for h in range(HEADS):
        stat[1, h : h + 1] = jnp.sum(prod[h].T, axis=0, keepdims=True)
    for which in range(2):
        rest = stat[which]
        for part in range(3):
            high = rest.astype(BF16)
            start = 2 * ROWS + (which * 3 + part) * STAT_ROWS
            pack_ref[start : start + STAT_ROWS] = high
            rest = rest - high.astype(F32)


def prepare(where, parents, queries, out_grad, outputs, log_norm):
    return pl.pallas_call(
        prepare_kernel,
        out_shape=(
            jax.ShapeDtypeStruct((PACK_ROWS, HD), BF16),
            jax.ShapeDtypeStruct((2 * NBLK,), jnp.int32),
        ),
        in_specs=smem(2) + vmem(4),
        out_specs=(pl.BlockSpec(memory_space=pltpu.VMEM), pl.BlockSpec(memory_space=pltpu.SMEM)),
        scratch_shapes=[pltpu.VMEM((2, STAT_ROWS, BLK), F32)],
        name="prepare",
    )(where, parents, queries, out_grad, outputs, log_norm)


NT = (((1,), (1,)), ((), ()))
NN = (((1,), (0,)), ((), ()))


def mm(a, b, dims):
    return lax.dot_general(a, b, dims, preferred_element_type=F32)


def column_kernel(own, *refs):
    if own:
        where, reach, pack0, pack1, col, part, dq_out, dk, dv, stats = refs
        dq_out[...] = jnp.zeros_like(dq_out)
    else:
        where, reach, pack0, pack1, col, dq_in, part, dq_out, dk, dv, stats = refs
        dq_out[...] = dq_in[...]
    packs = (pack0, pack1)
    for side in range(2):
        for which in range(2):
            base = 2 * ROWS + which * 3 * STAT_ROWS
            total = packs[side][base : base + STAT_ROWS].astype(F32)
            for k in range(1, 3):
                lo = base + k * STAT_ROWS
                total = total + packs[side][lo : lo + STAT_ROWS].astype(F32)
            stats[side, which] = total * LOG2E if which == 0 else total
    first = where[2]

    def per_block(j, carry):
        block = first + 16 * (j // 2) + j % 2
        dk[...] = jnp.zeros_like(dk)
        dv[...] = jnp.zeros_like(dv)
        for side in range(2):

            @pl.when(reach[side * NBLK + block] == 1)
            def _(side=side):
                pack = packs[side]
                keys = col[j, 0:BLK]
                values = col[j, BLK : 2 * BLK]
                keys_t = keys.T
                dk_new = dk[...]
                dv_new = dv[...]
                for c in range(ROWS // CHUNK):
                    lo = c * CHUNK
                    q = pack[lo : lo + CHUNK]
                    do = pack[ROWS + lo : ROWS + lo + CHUNK]
                    norm = jnp.concatenate([stats[side, 0, 2 * c : 2 * c + 1], stats[side, 0, 2 * c + 1 : 2 * c + 2]], 1)
                    dots = jnp.concatenate([stats[side, 1, 2 * c : 2 * c + 1], stats[side, 1, 2 * c + 1 : 2 * c + 2]], 1)
                    probs = jnp.exp2(mm(keys, q, NT) * (SCALING * LOG2E) - norm)
                    if own and side == 0:
                        token = lax.broadcasted_iota(jnp.int32, (BLK, CHUNK), 1) % BLK
                        at = lax.broadcasted_iota(jnp.int32, (BLK, CHUNK), 0)
                        least = jnp.where(block == where[0], 0, -BLK)
                        probs = jnp.where(token - at >= least, probs, 0.0)
                    dprobs = mm(values, do, NT)
                    dscores = (probs * (dprobs - dots) * SCALING).astype(BF16)
                    dv_new = dv_new + mm(probs.astype(BF16), do, NN)
                    dk_new = dk_new + mm(dscores, q, NN)
                    dq_out[side, :, lo : lo + CHUNK] += mm(keys_t, dscores, NN)
                dk[...] = dk_new
                dv[...] = dv_new

        part[j, 0:BLK] = dk[...].astype(part.dtype)
        part[j, BLK : 2 * BLK] = dv[...].astype(part.dtype)
        return carry

    lax.fori_loop(0, 8, per_block, 0)


def column(own, where, reach, pack0, pack1, col, dq=None):
    args = (where, reach, pack0, pack1, col) + (() if own else (dq,))
    return pl.pallas_call(
        functools.partial(column_kernel, own),
        out_shape=(
            jax.ShapeDtypeStruct((8, 2 * BLK, HD), F32 if own else BF16),
            jax.ShapeDtypeStruct((2, HD, ROWS), F32),
        ),
        in_specs=smem(2) + vmem(len(args) - 2),
        out_specs=tuple(vmem(2)),
        scratch_shapes=[
            pltpu.VMEM((BLK, HD), F32),
            pltpu.VMEM((BLK, HD), F32),
            pltpu.VMEM((2, 2, STAT_ROWS, BLK), F32),
        ],
        input_output_aliases={} if own else {5: 1},
        cost_estimate=pl.CostEstimate(flops=600_000_000, bytes_accessed=4_000_000, transcendentals=500_000),
        name="own_column" if own else "column",
    )(*args)


def query_kernel(mine, other, out):
    total = mine[...] + other[...]
    heads = jnp.stack([total[:, h * BLK : (h + 1) * BLK].T for h in range(HEADS)])
    out[...] = jnp.swapaxes(heads, 0, 1).astype(BF16)


def finish_query(mine, other):
    return pl.pallas_call(
        query_kernel,
        out_shape=jax.ShapeDtypeStruct((BLK, HEADS, HD), BF16),
        in_specs=vmem(2),
        out_specs=vmem(1)[0],
        name="finish_query",
    )(mine, other)


def sum_columns_kernel(own, a, b, c, out):
    out[...] = (own[...] + a[...].astype(F32) + b[...].astype(F32) + c[...].astype(F32)).astype(BF16)


def sum_columns(own, a, b, c):
    return pl.pallas_call(
        sum_columns_kernel,
        out_shape=jax.ShapeDtypeStruct((8, 2 * BLK, HD), BF16),
        in_specs=vmem(4),
        out_specs=vmem(1)[0],
        name="sum_columns",
    )(own, a, b, c)


def sum_rows_kernel(parts, out):
    total = parts[0].astype(F32)
    for j in range(1, 8):
        total = total + parts[j].astype(F32)
    low = total.astype(BF16)
    for z in range(KVH):
        out[z] = low


def sum_rows(parts):
    return pl.pallas_call(
        sum_rows_kernel,
        out_shape=jax.ShapeDtypeStruct((KVH, 2 * BLK, HD), BF16),
        in_specs=vmem(1),
        out_specs=vmem(1)[0],
        name="sum_rows",
    )(parts)


def split_heads_kernel(parts, key_out, value_out):
    both = parts[...].astype(F32)
    key_out[...] = jnp.swapaxes(both[:, 0:BLK], 0, 1).astype(BF16)
    value_out[...] = jnp.swapaxes(both[:, BLK : 2 * BLK], 0, 1).astype(BF16)


def split_heads(parts):
    return pl.pallas_call(
        split_heads_kernel,
        out_shape=(jax.ShapeDtypeStruct((BLK, KVH, HD), BF16),) * 2,
        in_specs=vmem(1),
        out_specs=tuple(vmem(2)),
        name="split_heads",
    )(parts)


def body(queries, keys, values, outputs, out_grad, log_norm, parents):
    yh, core, x, yl, z = (lax.axis_index(a) for a in ("yh", "core", "x", "yl", "z"))
    kv = jnp.concatenate(
        [lax.dynamic_index_in_dim(keys, z, 1, False), lax.dynamic_index_in_dim(values, z, 1, False)], 0
    )
    base = 16 * yh + 2 * x + yl
    ours, theirs = base + 8 * core, base + 8 * (1 - core)

    def where(distance):
        return jnp.stack([ours, theirs, 8 * core + 2 * ((x + distance) % 4)]).astype(jnp.int32)

    pack0, reach = prepare(where(0), parents, queries, out_grad, outputs, log_norm)
    pack1 = shift(pack0, "core", 1)
    col = lax.all_to_all(jnp.broadcast_to(kv[None], (8, 2 * BLK, HD)), Y, 0, 0)
    col_back, col_next, col_far = shift(col, "x", 1), shift(col, "x", -1), shift(col, "x", 2)
    part_own, dq = column(True, where(0), reach, pack0, pack1, col)
    part_back, dq = column(False, where(-1), reach, pack0, pack1, col_back, dq)
    got_back = shift(part_back, "x", -1)
    part_next, dq = column(False, where(1), reach, pack0, pack1, col_next, dq)
    got_next = shift(part_next, "x", 1)
    part_far, dq = column(False, where(2), reach, pack0, pack1, col_far, dq)
    got_far = shift(part_far, "x", 2)
    dq_other = shift(dq[1], "core", 1)
    query_grad = finish_query(dq[0], dq_other)
    row = lax.all_to_all(sum_columns(part_own, got_back, got_next, got_far), Y, 0, 0)
    heads = lax.all_to_all(sum_rows(row), "z", 0, 0)
    key_grad, value_grad = split_heads(heads)
    return query_grad, key_grad, value_grad


def solution(mesh):
    fine = Mesh(mesh.devices.reshape(4, 2, 4, 2, 8), ("yh", "core", "x", "yl", "z"))
    tokens = ("yh", "core", "x", "yl")
    in_specs = (
        P(tokens, "z", None),
        P(tokens, None, None),
        P(tokens, None, None),
        P(tokens, "z", None),
        P(tokens, "z", None),
        P("z", tokens),
        P(),
    )
    out_specs = (P(tokens, "z", None), P(tokens, None, None), P(tokens, None, None))
    return jax.shard_map(body, mesh=fine, in_specs=in_specs, out_specs=out_specs, check_vma=False)
```

time: 592 us -> 153 us (0.26)
  the two profiles are of different devices: /device:TPU:6 before, /device:TPU:4 now
where the time goes in v1:
time: 153 us; the launch traced here: 152 us
  starting transfers between devices  51.4 us (34%)
  waiting for transfers between devices  36.6 us (24%)
  Pallas kernels  28.8 us (19%)
  blocking collectives  20.4 us (13%)
  local copies, waits for them, and re-layouts  12.7 us (8%)
    ppermute x8, starting transfers between devices, shift(): lax.ppermute(block, axis, [(i, (i + distance) % size) for i in range(size)])  33.7 us
    all_to_all x1, blocking collectives, body(): lax.all_to_all(sum_columns(part_own, got_back, got_next, got_far), Y, 0, 0)  20.4 us
    pallas_call x4, Pallas kernels, column(): pl.pallas_call(functools.partial(column_kernel, own), out_shape=(jax.Shap...  17 us
    all_to_all x1, waiting for transfers between devices, body(): col = lax.all_to_all(jnp.broadcast_to(kv[None], (8, 2 * BLK, HD)), Y, 0, 0)  16.8 us
    ppermute x8, waiting for transfers between devices, shift(): lax.ppermute(block, axis, [(i, (i + distance) % size) for i in range(size)])  14.3 us
    all_to_all x1, starting transfers between devices, body(): heads = lax.all_to_all(sum_rows(row), 'z', 0, 0)  10.4 us
    unnamed x38, local copies, waits for them, and re-layouts  9.81 us
    all_to_all x1, starting transfers between devices, body(): col = lax.all_to_all(jnp.broadcast_to(kv[None], (8, 2 * BLK, HD)), Y, 0, 0)  7.23 us
  transfers between devices with their start and end apart: 10, of which 7 were waited for; matrix products, arithmetic and copies ran while one was open for 4% of the time, Pallas kernels for 12%

profile of v1, /device:TPU:4, one launch (start us, length us, event | category | flops | bytes accessed | tf_op | source)
XLA Modules:
  0.0 152.0 jit_solution(7763392857756119894)
XLA Ops:
  0.6 1.2 constant_dynamic-slice_fusion
  1.9 0.9 broadcast_in_dim.2
  2.7 0.0 copy-start.7
  2.7 7.2 %all-to-all-start = ((bf16[8,256,128]{2,1,0:T(8,128)(2,1)}), bf16[8,256,128]{2,1,0:T(8,128)(2,1)S(1)}, u32[]{:S(2)}, u32[]{:S(2)}) async-start(bf16[8,256,128]{2,1,0:T(8,128)(2,1)} %broadcast_in_dim.2), calls=%async_computation | async-start | bytes 1048576 | tf_op jit(solution)/shard_map/all_to_all | solution.py:254
  10.0 0.7 pad_add_fusion.4
  10.6 16.8 %all-to-all-done.refs_4_ = bf16[8,256,128]{2,1,0:T(8,128)(2,1)S(1)} async-done(((bf16[8,256,128]{2,1,0:T(8,128)(2,1)}), bf16[8,256,128]{2,1,0:T(8,128)(2,1)S(1)}, u32[]{:S(2)}, u32[]{:S(2)}) %all-to-all-start) | async-done | bytes 524320 | tf_op jit(solution)/shard_map/all_to_all | solution.py:254
  27.4 0.0 copy-start.2
  27.4 3.1 %collective-permute-start.3 = (bf16[8,256,128]{2,1,0:T(8,128)(2,1)S(1)}, bf16[8,256,128]{2,1,0:T(8,128)(2,1)S(1)}, u32[]{:S(2)}, u32[]{:S(2)}) collective-permute-start(bf16[8,256,128]{2,1,0:T(8,128)(2,1)S(1)} %all-to-all-done.refs_4_), channel_id=1, source_target_pairs={{0,16},{16,32},{32,48},{48,0},{1,17},{17,33},{33,49},{49,1},{2,18}... | collective-permute-start | bytes 1572872 | tf_op jit(solution)/shard_map/ppermute | solution.py:28
  30.6 0.7 pad_add_fusion.3
  31.2 0.0 copy-done.7
  31.2 0.8 copy.17.q_ref
  32.1 0.1 copy-done.8
  32.1 0.0 copy-start.9
  32.1 0.8 copy.18.do_ref
  33.0 0.1 copy-done.9
  33.1 0.8 copy.19.o_ref
  33.9 3.2 %prepare.1 = (bf16[1632,128]{1,0:T(8,128)(2,1)}, s32[128]{0:T(128)}) custom-call(s32[3]{0:T(128)} %get-tuple-element.38.where.refs_0_, s32[64]{0:T(128)} %parents.1, bf16[128,6,128]{2,1,0:T(8,128)(2,1)} %copy.17.q_ref, bf16[128,6,128]{2,1,0:T(8,128)(2,1)} %copy.18.do_ref, bf16[128,6,128]{2,1,0:T(8,128)(2,1)} %copy.19.o_ref, f32[6,128]{1,0:T(8,128)} %ln_ref.1), custom_call_target="tpu_custom_call" | custom-call | tf_op jit(solution)/shard_map/prepare/pallas_call | solution.py:75
  37.1 1.9 %collective-permute-start = (bf16[1632,128]{1,0:T(8,128)(2,1)}, bf16[1632,128]{1,0:T(8,128)(2,1)S(1)}, u32[]{:S(2)}, u32[]{:S(2)}) collective-permute-start(bf16[1632,128]{1,0:T(8,128)(2,1)} %get-tuple-element.16.refs_2_), channel_id=1, source_target_pairs={{0,64},{64,0},{1,65},{65,1},{2,66},{66,2},{3,67},{67,3},{4,68},{68... | collective-permute-start | bytes 1253384 | tf_op jit(solution)/shard_map/ppermute | solution.py:28
  39.0 2.7 %collective-permute-start.2 = (bf16[8,256,128]{2,1,0:T(8,128)(2,1)S(1)}, bf16[8,256,128]{2,1,0:T(8,128)(2,1)S(1)}, u32[]{:S(2)}, u32[]{:S(2)}) collective-permute-start(bf16[8,256,128]{2,1,0:T(8,128)(2,1)S(1)} %all-to-all-done.refs_4_), channel_id=1, source_target_pairs={{0,48},{16,0},{32,16},{48,32},{1,49},{17,1},{33,17},{49,33},{2,50}... | collective-permute-start | bytes 1572872 | tf_op jit(solution)/shard_map/ppermute | solution.py:28
  41.8 0.0 copy-done.2
  41.8 3.6 %collective-permute-start.1 = (bf16[8,256,128]{2,1,0:T(8,128)(2,1)S(1)}, bf16[8,256,128]{2,1,0:T(8,128)(2,1)S(1)}, u32[]{:S(2)}, u32[]{:S(2)}) collective-permute-start(bf16[8,256,128]{2,1,0:T(8,128)(2,1)S(1)} %all-to-all-done.refs_4_), channel_id=1, source_target_pairs={{0,32},{16,48},{32,0},{48,16},{1,33},{17,49},{33,1},{49,17},{2,34}... | collective-permute-start | bytes 1572872 | tf_op jit(solution)/shard_map/ppermute | solution.py:28
  45.4 0.0 collective-permute-done.refs_3_
  45.4 0.0 copy-start.15
  45.4 0.7 copy-done.15
  46.2 5.2 %own_column.1 = (f32[8,256,128]{2,1,0:T(8,128)}, f32[2,128,768]{2,1,0:T(8,128)}) custom-call(s32[3]{0:T(128)} %get-tuple-element.38.where.refs_0_, s32[128]{0:T(128)} %get-tuple-element.15.refs_1_, bf16[1632,128]{1,0:T(8,128)(2,1)} %get-tuple-element.16.refs_2_, bf16[1632,128]{1,0:T(8,128)(2,1)} %copy-done.15, bf16[8,256,128]{2,1,0:T(8,128)(2,1)} %copy-done.2), custom_call_target="tpu_custom_call" | custom-call | flops 600000000 | bytes 4000000 | tf_op jit(solution)/shard_map/own_column/pallas_call | solution.py:157
  51.3 0.0 collective-permute-done.3.refs_4_
  51.3 0.0 copy-start.11
  51.3 0.8 copy-done.11
  52.1 2.9 %column.3 = (bf16[8,256,128]{2,1,0:T(8,128)(2,1)}, f32[2,128,768]{2,1,0:T(8,128)}) custom-call(s32[3]{0:T(128)} %get-tuple-element.33.refs_0_, s32[128]{0:T(128)} %get-tuple-element.15.refs_1_, bf16[1632,128]{1,0:T(8,128)(2,1)} %get-tuple-element.16.refs_2_, bf16[1632,128]{1,0:T(8,128)(2,1)} %copy-done.15, ...), custom_call_target="tpu_custom_call", output_to_operand_aliasing={{1}: (5, {})} | custom-call | flops 600000000 | bytes 4000000 | tf_op jit(solution)/shard_map/column/pallas_call | solution.py:157
  55.1 0.6 collective-permute-done.2.refs_4_
  55.7 0.0 copy-start.14
  55.7 0.8 copy-done.14
  56.4 4.4 %column.4 = (bf16[8,256,128]{2,1,0:T(8,128)(2,1)}, f32[2,128,768]{2,1,0:T(8,128)}) custom-call(s32[3]{0:T(128)} %get-tuple-element.37.refs_0_, s32[128]{0:T(128)} %get-tuple-element.15.refs_1_, bf16[1632,128]{1,0:T(8,128)(2,1)} %get-tuple-element.16.refs_2_, bf16[1632,128]{1,0:T(8,128)(2,1)} %copy-done.15, ...), custom_call_target="tpu_custom_call", output_to_operand_aliasing={{1}: (5, {})} | custom-call | flops 600000000 | bytes 4000000 | tf_op jit(solution)/shard_map/column/pallas_call | solution.py:157
  60.9 0.0 collective-permute-done.1.refs_4_
  60.9 0.0 copy-start.12
  60.9 0.8 copy-done.12
  61.7 0.0 copy-start.13
  61.7 0.0 copy-start.10
  61.7 4.5 %column.5 = (bf16[8,256,128]{2,1,0:T(8,128)(2,1)}, f32[2,128,768]{2,1,0:T(8,128)}) custom-call(s32[3]{0:T(128)} %get-tuple-element.39.refs_0_, s32[128]{0:T(128)} %get-tuple-element.15.refs_1_, bf16[1632,128]{1,0:T(8,128)(2,1)} %get-tuple-element.16.refs_2_, bf16[1632,128]{1,0:T(8,128)(2,1)} %copy-done.15, ...), custom_call_target="tpu_custom_call", output_to_operand_aliasing={{1}: (5, {})} | custom-call | flops 600000000 | bytes 4000000 | tf_op jit(solution)/shard_map/column/pallas_call | solution.py:157
  66.2 11.3 %collective-permute-start.7 = (bf16[8,256,128]{2,1,0:T(8,128)(2,1)}, bf16[8,256,128]{2,1,0:T(8,128)(2,1)S(1)}, u32[]{:S(2)}, u32[]{:S(2)}) collective-permute-start(bf16[8,256,128]{2,1,0:T(8,128)(2,1)} %get-tuple-element.24), channel_id=1, source_target_pairs={{0,32},{16,48},{32,0},{48,16},{1,33},{17,49},{33,1},{49,17},{2,34}... | collective-permute-start | bytes 1572872 | tf_op jit(solution)/shard_map/ppermute | solution.py:28
  77.5 0.0 copy-done.13
  77.5 5.8 %collective-permute-start.6 = (bf16[8,256,128]{2,1,0:T(8,128)(2,1)S(1)}, bf16[8,256,128]{2,1,0:T(8,128)(2,1)S(1)}, u32[]{:S(2)}, u32[]{:S(2)}) collective-permute-start(bf16[8,256,128]{2,1,0:T(8,128)(2,1)S(1)} %copy-done.13), channel_id=1, source_target_pairs={{0,16},{16,32},{32,48},{48,0},{1,17},{17,33},{33,49},{49,1},{2,18}... | collective-permute-start | bytes 1572872 | tf_op jit(solution)/shard_map/ppermute | solution.py:28
  83.3 0.0 copy-done.10
  83.3 3.4 %collective-permute-start.5 = (bf16[8,256,128]{2,1,0:T(8,128)(2,1)S(1)}, bf16[8,256,128]{2,1,0:T(8,128)(2,1)S(1)}, u32[]{:S(2)}, u32[]{:S(2)}) collective-permute-start(bf16[8,256,128]{2,1,0:T(8,128)(2,1)S(1)} %copy-done.10), channel_id=1, source_target_pairs={{0,48},{16,0},{32,16},{48,32},{1,49},{17,1},{33,17},{49,33},{2,50}... | collective-permute-start | bytes 1572872 | tf_op jit(solution)/shard_map/ppermute | solution.py:28
  86.7 3.0 %collective-permute-done.7.c = bf16[8,256,128]{2,1,0:T(8,128)(2,1)S(1)} collective-permute-done((bf16[8,256,128]{2,1,0:T(8,128)(2,1)}, bf16[8,256,128]{2,1,0:T(8,128)(2,1)S(1)}, u32[]{:S(2)}, u32[]{:S(2)}) %collective-permute-start.7) | collective-permute-done | bytes 524320 | tf_op jit(solution)/shard_map/ppermute | solution.py:28
  89.8 4.4 %collective-permute-done.6.b = bf16[8,256,128]{2,1,0:T(8,128)(2,1)S(1)} collective-permute-done((bf16[8,256,128]{2,1,0:T(8,128)(2,1)S(1)}, bf16[8,256,128]{2,1,0:T(8,128)(2,1)S(1)}, u32[]{:S(2)}, u32[]{:S(2)}) %collective-permute-start.6) | collective-permute-done | bytes 524320 | tf_op jit(solution)/shard_map/ppermute | solution.py:28
  94.1 4.6 %collective-permute-done.5.a = bf16[8,256,128]{2,1,0:T(8,128)(2,1)S(1)} collective-permute-done((bf16[8,256,128]{2,1,0:T(8,128)(2,1)S(1)}, bf16[8,256,128]{2,1,0:T(8,128)(2,1)S(1)}, u32[]{:S(2)}, u32[]{:S(2)}) %collective-permute-start.5) | collective-permute-done | bytes 524320 | tf_op jit(solution)/shard_map/ppermute | solution.py:28
  98.7 0.0 copy-done.3
  98.8 0.0 copy-done.4
  98.8 0.8 copy-done.5
  99.5 2.7 %sum_columns.1 = bf16[8,256,128]{2,1,0:T(8,128)(2,1)} custom-call(f32[8,256,128]{2,1,0:T(8,128)} %get-tuple-element.21.own, bf16[8,256,128]{2,1,0:T(8,128)(2,1)} %copy-done.5, bf16[8,256,128]{2,1,0:T(8,128)(2,1)} %copy-done.4, bf16[8,256,128]{2,1,0:T(8,128)(2,1)} %copy-done.3), custom_call_target="tpu_custom_call" | custom-call | tf_op jit(solution)/shard_map/sum_columns/pallas_call | solution.py:197
  102.2 20.4 %all_to_all.15.parts = bf16[8,256,128]{2,1,0:T(8,128)(2,1)} all-to-all(bf16[8,256,128]{2,1,0:T(8,128)(2,1)} %sum_columns.1), channel_id=1, replica_groups=mesh['yh'=4,'core'=2,'x'=4,'yl'=2,'z'=8] {'yh','yl'}, dimensions={0} | all-to-all | bytes 1048576 | tf_op jit(solution)/shard_map/all_to_all | solution.py:265
  122.7 1.9 %sum_rows.1 = bf16[8,256,128]{2,1,0:T(8,128)(2,1)} custom-call(bf16[8,256,128]{2,1,0:T(8,128)(2,1)} %all_to_all.15.parts), custom_call_target="tpu_custom_call" | custom-call | tf_op jit(solution)/shard_map/sum_rows/pallas_call | solution.py:216
  124.6 10.4 %all-to-all-start.2 = ((bf16[8,256,128]{2,1,0:T(8,128)(2,1)}), bf16[8,256,128]{2,1,0:T(8,128)(2,1)S(1)}, u32[]{:S(2)}, u32[]{:S(2)}) async-start(bf16[8,256,128]{2,1,0:T(8,128)(2,1)} %sum_rows.1), calls=%async_computation.2 | async-start | bytes 1048576 | tf_op jit(solution)/shard_map/all_to_all | solution.py:266
  135.0 0.0 copy-done.1
  135.0 0.8 slice_bitcast_fusion
  135.8 1.9 %collective-permute-start.4 = (f32[128,768]{1,0:T(8,128)S(1)}, f32[128,768]{1,0:T(8,128)S(1)}, u32[]{:S(2)}, u32[]{:S(2)}) collective-permute-start(f32[128,768]{1,0:T(8,128)S(1)} %get-tuple-element.35), channel_id=1, source_target_pairs={{0,64},{64,0},{1,65},{65,1},{2,66},{66,2},{3,67},{67,3},{4,68},{68... | collective-permute-start | bytes 1179656 | tf_op jit(solution)/shard_map/ppermute | solution.py:28
  137.7 1.7 %collective-permute-done.4.other = f32[128,768]{1,0:T(8,128)S(1)} collective-permute-done((f32[128,768]{1,0:T(8,128)S(1)}, f32[128,768]{1,0:T(8,128)S(1)}, u32[]{:S(2)}, u32[]{:S(2)}) %collective-permute-start.4) | collective-permute-done | bytes 393248 | tf_op jit(solution)/shard_map/ppermute | solution.py:28
  139.4 0.7 copy-done.6
  140.2 2.0 %finish_query.1 = bf16[128,6,128]{2,1,0:T(8,128)(2,1)} custom-call(f32[128,768]{1,0:T(8,128)} %get-tuple-element.36.mine, f32[128,768]{1,0:T(8,128)} %copy-done.6), custom_call_target="tpu_custom_call" | custom-call | tf_op jit(solution)/shard_map/finish_query/pallas_call | solution.py:183
  142.2 1.7 %copy.22 = bf16[128,6,128]{2,0,1:T(8,128)(2,1)} copy(bf16[128,6,128]{2,1,0:T(8,128)(2,1)} %finish_query.1) | data formatting | bytes 393216
  143.8 5.4 %all-to-all-done.2.parts = bf16[8,256,128]{2,1,0:T(8,128)(2,1)S(1)} async-done(((bf16[8,256,128]{2,1,0:T(8,128)(2,1)}), bf16[8,256,128]{2,1,0:T(8,128)(2,1)S(1)}, u32[]{:S(2)}, u32[]{:S(2)}) %all-to-all-start.2) | async-done | bytes 524320 | tf_op jit(solution)/shard_map/all_to_all | solution.py:266
  149.3 0.8 copy-done
  150.1 2.0 %split_heads.1 = (bf16[128,8,128]{2,1,0:T(8,128)(2,1)}, bf16[128,8,128]{2,1,0:T(8,128)(2,1)}) custom-call(bf16[8,256,128]{2,1,0:T(8,128)(2,1)} %copy-done), custom_call_target="tpu_custom_call" | custom-call | tf_op jit(solution)/shard_map/split_heads/pallas_call | solution.py:232
  (10 shorter events, 0.0 us)
Async XLA Ops:
  2.7 28.5 %copy-start.7 = (bf16[128,6,128]{2,0,1:T(8,128)(2,1)S(1)}, bf16[128,6,128]{2,0,1:T(8,128)(2,1)}, u32[]{:S(2)}) copy-start(bf16[128,6,128]{2,0,1:T(8,128)(2,1)} %param.7) | copy-start | bytes 589828
  2.7 24.7 %all-to-all-start = ((bf16[8,256,128]{2,1,0:T(8,128)(2,1)}), bf16[8,256,128]{2,1,0:T(8,128)(2,1)S(1)}, u32[]{:S(2)}, u32[]{:S(2)}) async-start(bf16[8,256,128]{2,1,0:T(8,128)(2,1)} %broadcast_in_dim.2), calls=%async_computation | async-start | bytes 1048576 | tf_op jit(solution)/shard_map/all_to_all | solution.py:254
  27.4 14.3 %copy-start.2 = (bf16[8,256,128]{2,1,0:T(8,128)(2,1)}, bf16[8,256,128]{2,1,0:T(8,128)(2,1)S(1)}, u32[]{:S(2)}) copy-start(bf16[8,256,128]{2,1,0:T(8,128)(2,1)S(1)} %all-to-all-done.refs_4_) | copy-start | bytes 1572868
  27.4 23.9 %collective-permute-start.3 = (bf16[8,256,128]{2,1,0:T(8,128)(2,1)S(1)}, bf16[8,256,128]{2,1,0:T(8,128)(2,1)S(1)}, u32[]{:S(2)}, u32[]{:S(2)}) collective-permute-start(bf16[8,256,128]{2,1,0:T(8,128)(2,1)S(1)} %all-to-all-done.refs_4_), channel_id=1, source_target_pairs={{0,16},{16,32},{32,48},{48,0},{1,17},{17,33},{33,49},{49,1},{2,18}... | collective-permute-start | bytes 1572872 | tf_op jit(solution)/shard_map/ppermute | solution.py:28
  31.2 0.9 copy-start.8
  32.1 0.9 copy-start.9
  37.1 8.3 %collective-permute-start = (bf16[1632,128]{1,0:T(8,128)(2,1)}, bf16[1632,128]{1,0:T(8,128)(2,1)S(1)}, u32[]{:S(2)}, u32[]{:S(2)}) collective-permute-start(bf16[1632,128]{1,0:T(8,128)(2,1)} %get-tuple-element.16.refs_2_), channel_id=1, source_target_pairs={{0,64},{64,0},{1,65},{65,1},{2,66},{66,2},{3,67},{67,3},{4,68},{68... | collective-permute-start | bytes 1253384 | tf_op jit(solution)/shard_map/ppermute | solution.py:28
  39.0 16.6 %collective-permute-start.2 = (bf16[8,256,128]{2,1,0:T(8,128)(2,1)S(1)}, bf16[8,256,128]{2,1,0:T(8,128)(2,1)S(1)}, u32[]{:S(2)}, u32[]{:S(2)}) collective-permute-start(bf16[8,256,128]{2,1,0:T(8,128)(2,1)S(1)} %all-to-all-done.refs_4_), channel_id=1, source_target_pairs={{0,48},{16,0},{32,16},{48,32},{1,49},{17,1},{33,17},{49,33},{2,50}... | collective-permute-start | bytes 1572872 | tf_op jit(solution)/shard_map/ppermute | solution.py:28
  41.8 19.1 %collective-permute-start.1 = (bf16[8,256,128]{2,1,0:T(8,128)(2,1)S(1)}, bf16[8,256,128]{2,1,0:T(8,128)(2,1)S(1)}, u32[]{:S(2)}, u32[]{:S(2)}) collective-permute-start(bf16[8,256,128]{2,1,0:T(8,128)(2,1)S(1)} %all-to-all-done.refs_4_), channel_id=1, source_target_pairs={{0,32},{16,48},{32,0},{48,16},{1,33},{17,49},{33,1},{49,17},{2,34}... | collective-permute-start | bytes 1572872 | tf_op jit(solution)/shard_map/ppermute | solution.py:28
  45.4 0.7 copy-start.15
  51.3 0.8 copy-start.11
  55.7 0.8 copy-start.14
  60.9 0.8 copy-start.12
  61.7 15.8 %copy-start.13 = (bf16[8,256,128]{2,1,0:T(8,128)(2,1)S(1)}, bf16[8,256,128]{2,1,0:T(8,128)(2,1)}, u32[]{:S(2)}) copy-start(bf16[8,256,128]{2,1,0:T(8,128)(2,1)} %get-tuple-element.23) | copy-start | bytes 1572868
  61.7 21.6 %copy-start.10 = (bf16[8,256,128]{2,1,0:T(8,128)(2,1)S(1)}, bf16[8,256,128]{2,1,0:T(8,128)(2,1)}, u32[]{:S(2)}) copy-start(bf16[8,256,128]{2,1,0:T(8,128)(2,1)} %get-tuple-element.22) | copy-start | bytes 1572868
  66.2 23.5 %collective-permute-start.7 = (bf16[8,256,128]{2,1,0:T(8,128)(2,1)}, bf16[8,256,128]{2,1,0:T(8,128)(2,1)S(1)}, u32[]{:S(2)}, u32[]{:S(2)}) collective-permute-start(bf16[8,256,128]{2,1,0:T(8,128)(2,1)} %get-tuple-element.24), channel_id=1, source_target_pairs={{0,32},{16,48},{32,0},{48,16},{1,33},{17,49},{33,1},{49,17},{2,34}... | collective-permute-start | bytes 1572872 | tf_op jit(solution)/shard_map/ppermute | solution.py:28
  77.5 16.6 %collective-permute-start.6 = (bf16[8,256,128]{2,1,0:T(8,128)(2,1)S(1)}, bf16[8,256,128]{2,1,0:T(8,128)(2,1)S(1)}, u32[]{:S(2)}, u32[]{:S(2)}) collective-permute-start(bf16[8,256,128]{2,1,0:T(8,128)(2,1)S(1)} %copy-done.13), channel_id=1, source_target_pairs={{0,16},{16,32},{32,48},{48,0},{1,17},{17,33},{33,49},{49,1},{2,18}... | collective-permute-start | bytes 1572872 | tf_op jit(solution)/shard_map/ppermute | solution.py:28
  83.3 15.4 %collective-permute-start.5 = (bf16[8,256,128]{2,1,0:T(8,128)(2,1)S(1)}, bf16[8,256,128]{2,1,0:T(8,128)(2,1)S(1)}, u32[]{:S(2)}, u32[]{:S(2)}) collective-permute-start(bf16[8,256,128]{2,1,0:T(8,128)(2,1)S(1)} %copy-done.10), channel_id=1, source_target_pairs={{0,48},{16,0},{32,16},{48,32},{1,49},{17,1},{33,17},{49,33},{2,50}... | collective-permute-start | bytes 1572872 | tf_op jit(solution)/shard_map/ppermute | solution.py:28
  89.7 9.0 %copy-start.3 = (bf16[8,256,128]{2,1,0:T(8,128)(2,1)}, bf16[8,256,128]{2,1,0:T(8,128)(2,1)S(1)}, u32[]{:S(2)}) copy-start(bf16[8,256,128]{2,1,0:T(8,128)(2,1)S(1)} %collective-permute-done.7.c) | copy-start | bytes 1572868
  94.1 4.6 %copy-start.4 = (bf16[8,256,128]{2,1,0:T(8,128)(2,1)}, bf16[8,256,128]{2,1,0:T(8,128)(2,1)S(1)}, u32[]{:S(2)}) copy-start(bf16[8,256,128]{2,1,0:T(8,128)(2,1)S(1)} %collective-permute-done.6.b) | copy-start | bytes 1572868
  98.7 0.8 copy-start.5
  124.6 10.4 %copy-start.1 = (f32[2,128,768]{2,1,0:T(8,128)S(1)}, f32[2,128,768]{2,1,0:T(8,128)}, u32[]{:S(2)}) copy-start(f32[2,128,768]{2,1,0:T(8,128)} %get-tuple-element.20) | copy-start | bytes 2359300
  124.6 24.7 %all-to-all-start.2 = ((bf16[8,256,128]{2,1,0:T(8,128)(2,1)}), bf16[8,256,128]{2,1,0:T(8,128)(2,1)S(1)}, u32[]{:S(2)}, u32[]{:S(2)}) async-start(bf16[8,256,128]{2,1,0:T(8,128)(2,1)} %sum_rows.1), calls=%async_computation.2 | async-start | bytes 1048576 | tf_op jit(solution)/shard_map/all_to_all | solution.py:266
  135.8 3.6 %collective-permute-start.4 = (f32[128,768]{1,0:T(8,128)S(1)}, f32[128,768]{1,0:T(8,128)S(1)}, u32[]{:S(2)}, u32[]{:S(2)}) collective-permute-start(f32[128,768]{1,0:T(8,128)S(1)} %get-tuple-element.35), channel_id=1, source_target_pairs={{0,64},{64,0},{1,65},{65,1},{2,66},{66,2},{3,67},{67,3},{4,68},{68... | collective-permute-start | bytes 1179656 | tf_op jit(solution)/shard_map/ppermute | solution.py:28
  139.4 0.7 copy-start.6
  149.3 0.8 copy-start

commit v2 on v1

v2 whole, which is shorter than its diff:
```python
import functools

import jax
import jax.numpy as jnp
from jax import lax
from jax.experimental import pallas as pl
from jax.experimental.pallas import tpu as pltpu
from jax.sharding import Mesh, PartitionSpec as P

BLK = 128
HD = 128
HEADS = 6
ROWS = HEADS * BLK
NBLK = 64
KVH = 8
SIDES = 8
DISTANCES = (0, 1, -1, 2)
Y = ("yh", "yl")
STAT_ROWS = 16
PACK_ROWS = 2 * ROWS + 6 * STAT_ROWS
SCALING = HD ** -0.5
LOG2E = 1.4426950408889634
CHUNK = 2 * BLK
F32 = jnp.float32
BF16 = jnp.bfloat16


def shift(block, axis, distance):
    size = lax.axis_size(axis)
    return lax.ppermute(block, axis, [(i, (i + distance) % size) for i in range(size)])


def vmem(count):
    return [pl.BlockSpec(memory_space=pltpu.VMEM)] * count


def smem(count):
    return [pl.BlockSpec(memory_space=pltpu.SMEM)] * count


def prepare_kernel(ids, parents, q_ref, do_ref, o_ref, ln_ref, pack_ref, reach_ref, stat):
    def clear(i, carry):
        reach_ref[i] = 0
        return carry

    lax.fori_loop(0, SIDES * NBLK, clear, 0)

    def walk(side, carry):
        def climb(state):
            block, _ = state
            reach_ref[side * NBLK + block] = 1
            above = parents[block]
            return above, above != block

        lax.while_loop(lambda state: state[1], climb, (ids[side], True))
        return carry

    lax.fori_loop(0, SIDES, walk, 0)

    pack_ref[0:ROWS] = q_ref[...].reshape(ROWS, HD)
    pack_ref[ROWS : 2 * ROWS] = do_ref[...].reshape(ROWS, HD)
    stat[...] = jnp.zeros_like(stat)
    stat[0, 0:HEADS] = ln_ref[...]
    for h in range(HEADS):
        prod = do_ref[h].astype(F32) * o_ref[h].astype(F32)
        stat[1, h : h + 1] = jnp.sum(prod.T, axis=0, keepdims=True)
    for which in range(2):
        rest = stat[which]
        for part in range(3):
            high = rest.astype(BF16)
            start = 2 * ROWS + (which * 3 + part) * STAT_ROWS
            pack_ref[start : start + STAT_ROWS] = high
            rest = rest - high.astype(F32)


def prepare(ids, parents, queries, out_grad, outputs, log_norm):
    return pl.pallas_call(
        prepare_kernel,
        out_shape=(
            jax.ShapeDtypeStruct((PACK_ROWS, HD), BF16),
            jax.ShapeDtypeStruct((SIDES * NBLK,), jnp.int32),
        ),
        in_specs=smem(2) + vmem(4),
        out_specs=(pl.BlockSpec(memory_space=pltpu.VMEM), pl.BlockSpec(memory_space=pltpu.SMEM)),
        scratch_shapes=[pltpu.VMEM((2, STAT_ROWS, BLK), F32)],
        cost_estimate=pl.CostEstimate(flops=4_000_000, bytes_accessed=1_000_000, transcendentals=0),
        name="prepare",
    )(ids, parents, queries, out_grad, outputs, log_norm)


NT = (((1,), (1,)), ((), ()))
NN = (((1,), (0,)), ((), ()))


def mm(a, b, dims):
    return lax.dot_general(a, b, dims, preferred_element_type=F32)


def attend_kernel(ids, reach, *refs):
    packs, (col, part), grads, (dk, dv, stats) = refs[:8], refs[8:10], refs[10:18], refs[18:]
    for side in range(SIDES):
        grads[side][...] = jnp.zeros((HD, ROWS), F32)
        for which in range(2):
            base = 2 * ROWS + which * 3 * STAT_ROWS
            total = packs[side][base : base + STAT_ROWS].astype(F32)
            for k in range(1, 3):
                lo = base + k * STAT_ROWS
                total = total + packs[side][lo : lo + STAT_ROWS].astype(F32)
            stats[side, which] = total * LOG2E if which == 0 else total
    first = ids[SIDES]

    def per_block(j, carry):
        block = first + 16 * (j // 2) + j % 2
        dk[...] = jnp.zeros_like(dk)
        dv[...] = jnp.zeros_like(dv)
        for side in range(SIDES):

            @pl.when(reach[side * NBLK + block] == 1)
            def _(side=side):
                pack = packs[side]
                keys = col[j, 0:BLK]
                values = col[j, BLK : 2 * BLK]
                keys_t = keys.T
                dk_new = dk[...]
                dv_new = dv[...]
                for c in range(ROWS // CHUNK):
                    lo = c * CHUNK
                    q = pack[lo : lo + CHUNK]
                    do = pack[ROWS + lo : ROWS + lo + CHUNK]
                    norm, dots = (
                        jnp.concatenate(
                            [stats[side, which, 2 * c : 2 * c + 1], stats[side, which, 2 * c + 1 : 2 * c + 2]], 1
                        )
                        for which in range(2)
                    )
                    probs = jnp.exp2(mm(keys, q, NT) * (SCALING * LOG2E) - norm)
                    if side == 0:
                        token = lax.broadcasted_iota(jnp.int32, (BLK, CHUNK), 1) % BLK
                        at = lax.broadcasted_iota(jnp.int32, (BLK, CHUNK), 0)
                        least = jnp.where(block == ids[0], 0, -BLK)
                        probs = jnp.where(token - at >= least, probs, 0.0)
                    dprobs = mm(values, do, NT)
                    dscores = (probs * (dprobs - dots) * SCALING).astype(BF16)
                    dv_new = dv_new + mm(probs.astype(BF16), do, NN)
                    dk_new = dk_new + mm(dscores, q, NN)
                    grads[side][:, lo : lo + CHUNK] += mm(keys_t, dscores, NN)
                dk[...] = dk_new
                dv[...] = dv_new

        part[j, 0:BLK] = dk[...].astype(BF16)
        part[j, BLK : 2 * BLK] = dv[...].astype(BF16)
        return carry

    lax.fori_loop(0, 8, per_block, 0)


def attend(ids, reach, packs, col):
    return pl.pallas_call(
        attend_kernel,
        out_shape=(jax.ShapeDtypeStruct((8, 2 * BLK, HD), BF16),)
        + (jax.ShapeDtypeStruct((HD, ROWS), F32),) * SIDES,
        in_specs=smem(2) + vmem(SIDES + 1),
        out_specs=tuple(vmem(SIDES + 1)),
        scratch_shapes=[
            pltpu.VMEM((BLK, HD), F32),
            pltpu.VMEM((BLK, HD), F32),
            pltpu.VMEM((SIDES, 2, STAT_ROWS, BLK), F32),
        ],
        compiler_params=pltpu.CompilerParams(vmem_limit_bytes=32 * 1024 * 1024),
        cost_estimate=pl.CostEstimate(flops=2_000_000_000, bytes_accessed=8_000_000, transcendentals=2_000_000),
        name="attend",
    )(ids, reach, *packs, col)


def add_cores_kernel(*refs):
    for a, b, out in zip(refs[0:4], refs[4:8], refs[8:12], strict=True):
        out[...] = a[...] + b[...]


def add_cores(mine, other):
    return pl.pallas_call(
        add_cores_kernel,
        out_shape=(jax.ShapeDtypeStruct((HD, ROWS), F32),) * 4,
        in_specs=vmem(8),
        out_specs=tuple(vmem(4)),
        cost_estimate=pl.CostEstimate(flops=400_000, bytes_accessed=5_000_000, transcendentals=0),
        name="add_cores",
    )(*mine, *other)


def query_kernel(a, b, c, d, out):
    total = (a[...] + b[...]) + (c[...] + d[...])
    for h in range(HEADS):
        out[h] = total[:, h * BLK : (h + 1) * BLK].T.astype(BF16)


def finish_query(parts):
    return pl.pallas_call(
        query_kernel,
        out_shape=jax.ShapeDtypeStruct((HEADS, BLK, HD), BF16),
        in_specs=vmem(4),
        out_specs=vmem(1)[0],
        cost_estimate=pl.CostEstimate(flops=400_000, bytes_accessed=2_000_000, transcendentals=0),
        name="finish_query",
    )(*parts)


def sum_rows_kernel(parts, out):
    total = parts[0].astype(F32)
    for j in range(1, 8):
        total = total + parts[j].astype(F32)
    low = total.astype(BF16)
    for z in range(KVH):
        out[z] = low


def sum_rows(parts):
    return pl.pallas_call(
        sum_rows_kernel,
        out_shape=jax.ShapeDtypeStruct((KVH, 2 * BLK, HD), BF16),
        in_specs=vmem(1),
        out_specs=vmem(1)[0],
        name="sum_rows",
    )(parts)


def split_heads_kernel(parts, key_out, value_out):
    both = parts[...].astype(F32)
    key_out[...] = jnp.swapaxes(both[:, 0:BLK], 0, 1).astype(BF16)
    value_out[...] = jnp.swapaxes(both[:, BLK : 2 * BLK], 0, 1).astype(BF16)


def split_heads(parts):
    return pl.pallas_call(
        split_heads_kernel,
        out_shape=(jax.ShapeDtypeStruct((BLK, KVH, HD), BF16),) * 2,
        in_specs=vmem(1),
        out_specs=tuple(vmem(2)),
        name="split_heads",
    )(parts)


def body(queries, keys, values, outputs, out_grad, log_norm, parents):
    yh, core, x, yl, z = (lax.axis_index(a) for a in ("yh", "core", "x", "yl", "z"))
    kv = jnp.concatenate(
        [lax.dynamic_index_in_dim(keys, z, 1, False), lax.dynamic_index_in_dim(values, z, 1, False)], 0
    )
    ids = [
        16 * yh + 8 * (core if side < 4 else 1 - core) + 2 * ((x + DISTANCES[side % 4]) % 4) + yl
        for side in range(SIDES)
    ]
    ids = jnp.stack([*ids, 8 * core + 2 * x]).astype(jnp.int32)

    col = lax.all_to_all(jnp.broadcast_to(kv[None], (8, 2 * BLK, HD)), Y, 0, 0)
    queries, out_grad, outputs = (jnp.swapaxes(a, 0, 1) for a in (queries, out_grad, outputs))
    pack, reach = prepare(ids, parents, queries, out_grad, outputs, log_norm)
    packs = [pack] + [shift(pack, "x", -d) for d in DISTANCES[1:]]
    packs = packs + [shift(p, "core", 1) for p in packs]
    part, *grads = attend(ids, reach, packs, col)
    row = lax.all_to_all(part, Y, 0, 0)
    sums = add_cores(grads[:4], [shift(g, "core", 1) for g in grads[4:]])
    query_grad = finish_query([sums[0]] + [shift(g, "x", d) for g, d in zip(sums[1:], DISTANCES[1:], strict=True)])
    heads = lax.all_to_all(sum_rows(row), "z", 0, 0)
    key_grad, value_grad = split_heads(heads)
    return jnp.swapaxes(query_grad, 0, 1), key_grad, value_grad


def solution(mesh):
    fine = Mesh(mesh.devices.reshape(4, 2, 4, 2, 8), ("yh", "core", "x", "yl", "z"))
    tokens = ("yh", "core", "x", "yl")
    in_specs = (
        P(tokens, "z", None),
        P(tokens, None, None),
        P(tokens, None, None),
        P(tokens, "z", None),
        P(tokens, "z", None),
        P("z", tokens),
        P(),
    )
    out_specs = (P(tokens, "z", None), P(tokens, None, None), P(tokens, None, None))
    return jax.shard_map(body, mesh=fine, in_specs=in_specs, out_specs=out_specs, check_vma=False)
```

time: 153 us -> 144 us (0.941)
  the two profiles are of different devices: /device:TPU:4 before, /device:TPU:6 now
where the time goes in v2:
time: 144 us; the launch traced here: 143 us
  starting transfers between devices  55.5 us (39%)
  waiting for transfers between devices  27.9 us (19%)
  blocking collectives  26.5 us (18%)
  Pallas kernels  19.9 us (14%)
  local copies, waits for them, and re-layouts  12.1 us (8%)
    ppermute x14, starting transfers between devices, shift(): lax.ppermute(block, axis, [(i, (i + distance) % size) for i in range(size)])  38 us
    ppermute x14, waiting for transfers between devices, shift(): lax.ppermute(block, axis, [(i, (i + distance) % size) for i in range(size)])  27.9 us
    all_to_all x1, blocking collectives, body(): row = lax.all_to_all(part, Y, 0, 0)  26.5 us
    all_to_all x1, starting transfers between devices, body(): heads = lax.all_to_all(sum_rows(row), 'z', 0, 0)  10.5 us
    unnamed x48, local copies, waits for them, and re-layouts  9.47 us
    all_to_all x1, starting transfers between devices, body(): col = lax.all_to_all(jnp.broadcast_to(kv[None], (8, 2 * BLK, HD)), Y, 0, 0)  7.1 us
    pallas_call x1, Pallas kernels, prepare(): pl.pallas_call(prepare_kernel, out_shape=(jax.ShapeDtypeStruct((PACK_ROWS...  5.58 us
    pallas_call x1, Pallas kernels, attend(): pl.pallas_call(attend_kernel, out_shape=(jax.ShapeDtypeStruct((8, 2 * BLK...  5.22 us
  transfers between devices with their start and end apart: 16, of which 7 were waited for; matrix products, arithmetic and copies ran while one was open for 0% of the time, Pallas kernels for 8%

profile of v2, /device:TPU:6, one launch (start us, length us, event | category | flops | bytes accessed | tf_op | source)
XLA Modules:
  0.0 142.9 jit_solution(1286423172394672826)
XLA Ops:
  0.6 1.2 constant_dynamic-slice_fusion
  1.9 0.9 broadcast_in_dim.2
  2.7 7.1 %all-to-all-start = ((bf16[8,256,128]{2,1,0:T(8,128)(2,1)}), bf16[8,256,128]{2,1,0:T(8,128)(2,1)S(1)}, u32[]{:S(2)}, u32[]{:S(2)}) async-start(bf16[8,256,128]{2,1,0:T(8,128)(2,1)} %broadcast_in_dim.2), calls=%async_computation | async-start | bytes 1048576 | tf_op jit(solution)/shard_map/all_to_all | solution.py:254
  9.8 0.6 stack.39.ids
  10.4 5.6 %prepare.1 = (bf16[1632,128]{1,0:T(8,128)(2,1)}, s32[512]{0:T(512)}) custom-call(s32[9]{0:T(128)} %stack.39.ids, s32[64]{0:T(128)} %parents.1, bf16[6,128,128]{2,1,0:T(8,128)(2,1)} %bitcast.20, bf16[6,128,128]{2,1,0:T(8,128)(2,1)} %bitcast.21, bf16[6,128,128]{2,1,0:T(8,128)(2,1)} %bitcast.22, f32[6,128]{1,0:T(8,128)} %ln_ref.1), custom_call_target="tpu_custom_call" | custom-call | flops 4000000 | bytes 1000000 | tf_op jit(solution)/shard_map/prepare/pallas_call | solution.py:77
  16.0 0.0 copy-start.14
  16.0 0.0 copy-start.4
  16.0 3.3 %collective-permute-start.2 = (bf16[1632,128]{1,0:T(8,128)(2,1)}, bf16[1632,128]{1,0:T(8,128)(2,1)S(1)}, u32[]{:S(2)}, u32[]{:S(2)}) collective-permute-start(bf16[1632,128]{1,0:T(8,128)(2,1)} %get-tuple-element.21.refs_0_), channel_id=1, source_target_pairs={{0,32},{16,48},{32,0},{48,16},{1,33},{17,49},{33,1},{49,17},{2,34}... | collective-permute-start | bytes 1253384 | tf_op jit(solution)/shard_map/ppermute | solution.py:30
  19.3 4.0 %collective-permute-start.1 = (bf16[1632,128]{1,0:T(8,128)(2,1)}, bf16[1632,128]{1,0:T(8,128)(2,1)S(1)}, u32[]{:S(2)}, u32[]{:S(2)}) collective-permute-start(bf16[1632,128]{1,0:T(8,128)(2,1)} %get-tuple-element.21.refs_0_), channel_id=1, source_target_pairs={{0,16},{16,32},{32,48},{48,0},{1,17},{17,33},{33,49},{49,1},{2,18}... | collective-permute-start | bytes 1253384 | tf_op jit(solution)/shard_map/ppermute | solution.py:30
  23.4 1.9 %collective-permute-start = (bf16[1632,128]{1,0:T(8,128)(2,1)}, bf16[1632,128]{1,0:T(8,128)(2,1)S(1)}, u32[]{:S(2)}, u32[]{:S(2)}) collective-permute-start(bf16[1632,128]{1,0:T(8,128)(2,1)} %get-tuple-element.21.refs_0_), channel_id=1, source_target_pairs={{0,48},{16,0},{32,16},{48,32},{1,49},{17,1},{33,17},{49,33},{2,50}... | collective-permute-start | bytes 1253384 | tf_op jit(solution)/shard_map/ppermute | solution.py:30
  25.3 1.9 %collective-permute-start.3 = (bf16[1632,128]{1,0:T(8,128)(2,1)}, bf16[1632,128]{1,0:T(8,128)(2,1)S(1)}, u32[]{:S(2)}, u32[]{:S(2)}) collective-permute-start(bf16[1632,128]{1,0:T(8,128)(2,1)} %get-tuple-element.21.refs_0_), channel_id=1, source_target_pairs={{0,64},{64,0},{1,65},{65,1},{2,66},{66,2},{3,67},{67,3},{4,68},{68... | collective-permute-start | bytes 1253384 | tf_op jit(solution)/shard_map/ppermute | solution.py:30
  27.2 5.0 %collective-permute-done.2.refs_3_ = bf16[1632,128]{1,0:T(8,128)(2,1)S(1)} collective-permute-done((bf16[1632,128]{1,0:T(8,128)(2,1)}, bf16[1632,128]{1,0:T(8,128)(2,1)S(1)}, u32[]{:S(2)}, u32[]{:S(2)}) %collective-permute-start.2) | collective-permute-done | bytes 417824 | tf_op jit(solution)/shard_map/ppermute | solution.py:30
  32.2 1.9 %collective-permute-start.6 = (bf16[1632,128]{1,0:T(8,128)(2,1)S(1)}, bf16[1632,128]{1,0:T(8,128)(2,1)S(1)}, u32[]{:S(2)}, u32[]{:S(2)}) collective-permute-start(bf16[1632,128]{1,0:T(8,128)(2,1)S(1)} %collective-permute-done.2.refs_3_), channel_id=1, source_target_pairs={{0,64},{64,0},{1,65},{65,1},{2,66},{66,2},{3,67},{67,3},{4,68},{68... | collective-permute-start | bytes 1253384 | tf_op jit(solution)/shard_map/ppermute | solution.py:30
  34.1 3.4 %collective-permute-done.1.refs_2_ = bf16[1632,128]{1,0:T(8,128)(2,1)S(1)} collective-permute-done((bf16[1632,128]{1,0:T(8,128)(2,1)}, bf16[1632,128]{1,0:T(8,128)(2,1)S(1)}, u32[]{:S(2)}, u32[]{:S(2)}) %collective-permute-start.1) | collective-permute-done | bytes 417824 | tf_op jit(solution)/shard_map/ppermute | solution.py:30
  37.5 1.9 %collective-permute-start.5 = (bf16[1632,128]{1,0:T(8,128)(2,1)S(1)}, bf16[1632,128]{1,0:T(8,128)(2,1)S(1)}, u32[]{:S(2)}, u32[]{:S(2)}) collective-permute-start(bf16[1632,128]{1,0:T(8,128)(2,1)S(1)} %collective-permute-done.1.refs_2_), channel_id=1, source_target_pairs={{0,64},{64,0},{1,65},{65,1},{2,66},{66,2},{3,67},{67,3},{4,68},{68... | collective-permute-start | bytes 1253384 | tf_op jit(solution)/shard_map/ppermute | solution.py:30
  39.4 0.3 collective-permute-done.refs_1_
  39.7 2.1 %collective-permute-start.4 = (bf16[1632,128]{1,0:T(8,128)(2,1)S(1)}, bf16[1632,128]{1,0:T(8,128)(2,1)S(1)}, u32[]{:S(2)}, u32[]{:S(2)}) collective-permute-start(bf16[1632,128]{1,0:T(8,128)(2,1)S(1)} %collective-permute-done.refs_1_), channel_id=1, source_target_pairs={{0,64},{64,0},{1,65},{65,1},{2,66},{66,2},{3,67},{67,3},{4,68},{68... | collective-permute-start | bytes 1253384 | tf_op jit(solution)/shard_map/ppermute | solution.py:30
  41.8 0.0 collective-permute-done.3.refs_4_
  41.8 0.0 collective-permute-done.6.refs_7_
  41.9 0.0 collective-permute-done.5.refs_6_
  41.9 1.5 %collective-permute-done.4.refs_5_ = bf16[1632,128]{1,0:T(8,128)(2,1)S(1)} collective-permute-done((bf16[1632,128]{1,0:T(8,128)(2,1)S(1)}, bf16[1632,128]{1,0:T(8,128)(2,1)S(1)}, u32[]{:S(2)}, u32[]{:S(2)}) %collective-permute-start.4) | collective-permute-done | bytes 417824 | tf_op jit(solution)/shard_map/ppermute | solution.py:30
  43.3 0.0 all-to-all-done.refs_8_
  43.3 0.0 copy-done.14
  43.3 0.0 copy-done.4
  43.3 0.0 copy-start.5
  43.3 1.0 copy-done.5
  44.3 5.2 %attend.1 = (bf16[8,256,128]{2,1,0:T(8,128)(2,1)S(1)}, f32[128,768]{1,0:T(8,128)S(1)}, f32[128,768]{1,0:T(8,128)S(1)}, f32[128,768]{1,0:T(8,128)S(1)}, f32[128,7...) custom-call(s32[9]{0:T(128)S(1)} %copy-done.4, ...), custom_call_target="tpu_custom_call" | custom-call | flops 2000000000 | bytes 8000000 | tf_op jit(solution)/shard_map/attend/pallas_call | solution.py:158
  49.6 0.0 copy-start
  49.6 0.8 copy-done
  50.3 0.7 copy-done.1
  51.1 0.8 copy-done.2
  51.9 0.7 copy-done.3
  52.6 0.8 copy-done.6
  53.4 0.7 copy-done.8
  54.1 0.7 copy-done.10
  54.8 0.7 copy-done.12
  55.6 26.5 %all_to_all.15.parts = bf16[8,256,128]{2,1,0:T(8,128)(2,1)} all-to-all(bf16[8,256,128]{2,1,0:T(8,128)(2,1)S(1)} %get-tuple-element.34), channel_id=1, replica_groups=mesh['yh'=4,'core'=2,'x'=4,'yl'=2,'z'=8] {'yh','yl'}, dimensions={0} | all-to-all | bytes 1048576 | tf_op jit(solution)/shard_map/all_to_all | solution.py:260
  82.1 2.0 %sum_rows.1 = bf16[8,256,128]{2,1,0:T(8,128)(2,1)} custom-call(bf16[8,256,128]{2,1,0:T(8,128)(2,1)} %all_to_all.15.parts), custom_call_target="tpu_custom_call" | custom-call | tf_op jit(solution)/shard_map/sum_rows/pallas_call | solution.py:218
  84.1 10.5 %all-to-all-start.2 = ((bf16[8,256,128]{2,1,0:T(8,128)(2,1)}), bf16[8,256,128]{2,1,0:T(8,128)(2,1)S(1)}, u32[]{:S(2)}, u32[]{:S(2)}) async-start(bf16[8,256,128]{2,1,0:T(8,128)(2,1)} %sum_rows.1), calls=%async_computation.2 | async-start | bytes 1048576 | tf_op jit(solution)/shard_map/all_to_all | solution.py:263
  94.5 0.0 copy-done.13
  94.5 1.9 %collective-permute-start.7 = (f32[128,768]{1,0:T(8,128)S(1)}, f32[128,768]{1,0:T(8,128)S(1)}, u32[]{:S(2)}, u32[]{:S(2)}) collective-permute-start(f32[128,768]{1,0:T(8,128)S(1)} %copy-done.13), channel_id=1, source_target_pairs={{0,64},{64,0},{1,65},{65,1},{2,66},{66,2},{3,67},{67,3},{4,68},{68... | collective-permute-start | bytes 1179656 | tf_op jit(solution)/shard_map/ppermute | solution.py:30
  96.5 2.4 %collective-permute-start.8 = (f32[128,768]{1,0:T(8,128)S(1)}, f32[128,768]{1,0:T(8,128)S(1)}, u32[]{:S(2)}, u32[]{:S(2)}) collective-permute-start(f32[128,768]{1,0:T(8,128)S(1)} %copy-done.11), channel_id=1, source_target_pairs={{0,64},{64,0},{1,65},{65,1},{2,66},{66,2},{3,67},{67,3},{4,68},{68... | collective-permute-start | bytes 1179656 | tf_op jit(solution)/shard_map/ppermute | solution.py:30
  98.9 1.9 %collective-permute-start.9 = (f32[128,768]{1,0:T(8,128)S(1)}, f32[128,768]{1,0:T(8,128)S(1)}, u32[]{:S(2)}, u32[]{:S(2)}) collective-permute-start(f32[128,768]{1,0:T(8,128)S(1)} %copy-done.9), channel_id=1, source_target_pairs={{0,64},{64,0},{1,65},{65,1},{2,66},{66,2},{3,67},{67,3},{4,68},{68... | collective-permute-start | bytes 1179656 | tf_op jit(solution)/shard_map/ppermute | solution.py:30
  100.8 2.4 %collective-permute-start.10 = (f32[128,768]{1,0:T(8,128)S(1)}, f32[128,768]{1,0:T(8,128)S(1)}, u32[]{:S(2)}, u32[]{:S(2)}) collective-permute-start(f32[128,768]{1,0:T(8,128)S(1)} %copy-done.7), channel_id=1, source_target_pairs={{0,64},{64,0},{1,65},{65,1},{2,66},{66,2},{3,67},{67,3},{4,68},{68... | collective-permute-start | bytes 1179656 | tf_op jit(solution)/shard_map/ppermute | solution.py:30
  103.2 0.0 collective-permute-done.7.refs_4_
  103.3 0.0 copy-start.16
  103.3 0.0 collective-permute-done.8.refs_5_
  103.3 0.0 collective-permute-done.9.refs_6_
  103.3 1.3 collective-permute-done.10.refs_7_
  104.6 0.7 copy-done.19
  105.3 3.0 %add_cores.1 = (f32[128,768]{1,0:T(8,128)}, f32[128,768]{1,0:T(8,128)}, f32[128,768]{1,0:T(8,128)}, f32[128,768]{1,0:T(8,128)}) custom-call(f32[128,768]{1,0:T(8,128)} %copy-done, f32[128,768]{1,0:T(8,128)} %copy-done.1, f32[128,768]{1,0:T(8,128)} %copy-done.2, f32[128,768]{1,0:T(8,128)} %copy-done.3, f32[128,768]{1,0:T(8,128)} %copy-done.16, ...), custom_call_target="tpu_custom_call" | custom-call | flops 400000 | bytes 5000000 | tf_op jit(solution)/shard_map/add_cores/pallas_call | solution.py:181
  108.4 5.9 %collective-permute-start.11 = (f32[128,768]{1,0:T(8,128)}, f32[128,768]{1,0:T(8,128)S(1)}, u32[]{:S(2)}, u32[]{:S(2)}) collective-permute-start(f32[128,768]{1,0:T(8,128)} %get-tuple-element.31), channel_id=1, source_target_pairs={{0,16},{16,32},{32,48},{48,0},{1,17},{17,33},{33,49},{49,1},{2,18}... | collective-permute-start | bytes 1179656 | tf_op jit(solution)/shard_map/ppermute | solution.py:30
  114.2 1.9 %collective-permute-start.12 = (f32[128,768]{1,0:T(8,128)}, f32[128,768]{1,0:T(8,128)S(1)}, u32[]{:S(2)}, u32[]{:S(2)}) collective-permute-start(f32[128,768]{1,0:T(8,128)} %get-tuple-element.32), channel_id=1, source_target_pairs={{0,48},{16,0},{32,16},{48,32},{1,49},{17,1},{33,17},{49,33},{2,50}... | collective-permute-start | bytes 1179656 | tf_op jit(solution)/shard_map/ppermute | solution.py:30
  116.2 4.4 %collective-permute-start.13 = (f32[128,768]{1,0:T(8,128)}, f32[128,768]{1,0:T(8,128)S(1)}, u32[]{:S(2)}, u32[]{:S(2)}) collective-permute-start(f32[128,768]{1,0:T(8,128)} %get-tuple-element.33), channel_id=1, source_target_pairs={{0,32},{16,48},{32,0},{48,16},{1,33},{17,49},{33,1},{49,17},{2,34}... | collective-permute-start | bytes 1179656 | tf_op jit(solution)/shard_map/ppermute | solution.py:30
  120.6 11.3 %collective-permute-done.11.b = f32[128,768]{1,0:T(8,128)S(1)} collective-permute-done((f32[128,768]{1,0:T(8,128)}, f32[128,768]{1,0:T(8,128)S(1)}, u32[]{:S(2)}, u32[]{:S(2)}) %collective-permute-start.11) | collective-permute-done | bytes 393248 | tf_op jit(solution)/shard_map/ppermute | solution.py:30
  131.9 5.2 %collective-permute-done.12.c = f32[128,768]{1,0:T(8,128)S(1)} collective-permute-done((f32[128,768]{1,0:T(8,128)}, f32[128,768]{1,0:T(8,128)S(1)}, u32[]{:S(2)}, u32[]{:S(2)}) %collective-permute-start.12) | collective-permute-done | bytes 393248 | tf_op jit(solution)/shard_map/ppermute | solution.py:30
  137.1 0.0 collective-permute-done.13.d
  137.1 0.0 copy-done.20
  137.1 0.7 copy-done.21
  137.8 0.1 copy-done.22
  138.0 2.2 %finish_query.1 = bf16[6,128,128]{2,1,0:T(8,128)(2,1)} custom-call(f32[128,768]{1,0:T(8,128)} %get-tuple-element.30.a, f32[128,768]{1,0:T(8,128)} %copy-done.20, f32[128,768]{1,0:T(8,128)} %copy-done.21, f32[128,768]{1,0:T(8,128)} %copy-done.22), custom_call_target="tpu_custom_call" | custom-call | flops 400000 | bytes 2000000 | tf_op jit(solution)/shard_map/finish_query/pallas_call | solution.py:198
  140.2 0.0 all-to-all-done.2.parts
  140.2 0.8 copy-done.15
  140.9 2.0 %split_heads.1 = (bf16[128,8,128]{2,1,0:T(8,128)(2,1)}, bf16[128,8,128]{2,1,0:T(8,128)(2,1)}) custom-call(bf16[8,256,128]{2,1,0:T(8,128)(2,1)} %copy-done.15), custom_call_target="tpu_custom_call" | custom-call | tf_op jit(solution)/shard_map/split_heads/pallas_call | solution.py:234
  (27 shorter events, 0.1 us)
Async XLA Ops:
  2.7 40.6 %all-to-all-start = ((bf16[8,256,128]{2,1,0:T(8,128)(2,1)}), bf16[8,256,128]{2,1,0:T(8,128)(2,1)S(1)}, u32[]{:S(2)}, u32[]{:S(2)}) async-start(bf16[8,256,128]{2,1,0:T(8,128)(2,1)} %broadcast_in_dim.2), calls=%async_computation | async-start | bytes 1048576 | tf_op jit(solution)/shard_map/all_to_all | solution.py:254
  16.0 27.3 %copy-start.14 = (s32[512]{0:T(512)S(1)}, s32[512]{0:T(512)}, u32[]{:S(2)}) copy-start(s32[512]{0:T(512)} %get-tuple-element.20.reach) | copy-start | bytes 6148
  16.0 27.3 %copy-start.4 = (s32[9]{0:T(128)S(1)}, s32[9]{0:T(128)}, u32[]{:S(2)}) copy-start(s32[9]{0:T(128)} %stack.39.ids) | copy-start | bytes 112
  16.0 16.2 %collective-permute-start.2 = (bf16[1632,128]{1,0:T(8,128)(2,1)}, bf16[1632,128]{1,0:T(8,128)(2,1)S(1)}, u32[]{:S(2)}, u32[]{:S(2)}) collective-permute-start(bf16[1632,128]{1,0:T(8,128)(2,1)} %get-tuple-element.21.refs_0_), channel_id=1, source_target_pairs={{0,32},{16,48},{32,0},{48,16},{1,33},{17,49},{33,1},{49,17},{2,34}... | collective-permute-start | bytes 1253384 | tf_op jit(solution)/shard_map/ppermute | solution.py:30
  19.3 18.1 %collective-permute-start.1 = (bf16[1632,128]{1,0:T(8,128)(2,1)}, bf16[1632,128]{1,0:T(8,128)(2,1)S(1)}, u32[]{:S(2)}, u32[]{:S(2)}) collective-permute-start(bf16[1632,128]{1,0:T(8,128)(2,1)} %get-tuple-element.21.refs_0_), channel_id=1, source_target_pairs={{0,16},{16,32},{32,48},{48,0},{1,17},{17,33},{33,49},{49,1},{2,18}... | collective-permute-start | bytes 1253384 | tf_op jit(solution)/shard_map/ppermute | solution.py:30
  23.4 16.3 %collective-permute-start = (bf16[1632,128]{1,0:T(8,128)(2,1)}, bf16[1632,128]{1,0:T(8,128)(2,1)S(1)}, u32[]{:S(2)}, u32[]{:S(2)}) collective-permute-start(bf16[1632,128]{1,0:T(8,128)(2,1)} %get-tuple-element.21.refs_0_), channel_id=1, source_target_pairs={{0,48},{16,0},{32,16},{48,32},{1,49},{17,1},{33,17},{49,33},{2,50}... | collective-permute-start | bytes 1253384 | tf_op jit(solution)/shard_map/ppermute | solution.py:30
  25.3 16.6 %collective-permute-start.3 = (bf16[1632,128]{1,0:T(8,128)(2,1)}, bf16[1632,128]{1,0:T(8,128)(2,1)S(1)}, u32[]{:S(2)}, u32[]{:S(2)}) collective-permute-start(bf16[1632,128]{1,0:T(8,128)(2,1)} %get-tuple-element.21.refs_0_), channel_id=1, source_target_pairs={{0,64},{64,0},{1,65},{65,1},{2,66},{66,2},{3,67},{67,3},{4,68},{68... | collective-permute-start | bytes 1253384 | tf_op jit(solution)/shard_map/ppermute | solution.py:30
  32.2 9.6 %collective-permute-start.6 = (bf16[1632,128]{1,0:T(8,128)(2,1)S(1)}, bf16[1632,128]{1,0:T(8,128)(2,1)S(1)}, u32[]{:S(2)}, u32[]{:S(2)}) collective-permute-start(bf16[1632,128]{1,0:T(8,128)(2,1)S(1)} %collective-permute-done.2.refs_3_), channel_id=1, source_target_pairs={{0,64},{64,0},{1,65},{65,1},{2,66},{66,2},{3,67},{67,3},{4,68},{68... | collective-permute-start | bytes 1253384 | tf_op jit(solution)/shard_map/ppermute | solution.py:30
  37.5 4.4 %collective-permute-start.5 = (bf16[1632,128]{1,0:T(8,128)(2,1)S(1)}, bf16[1632,128]{1,0:T(8,128)(2,1)S(1)}, u32[]{:S(2)}, u32[]{:S(2)}) collective-permute-start(bf16[1632,128]{1,0:T(8,128)(2,1)S(1)} %collective-permute-done.1.refs_2_), channel_id=1, source_target_pairs={{0,64},{64,0},{1,65},{65,1},{2,66},{66,2},{3,67},{67,3},{4,68},{68... | collective-permute-start | bytes 1253384 | tf_op jit(solution)/shard_map/ppermute | solution.py:30
  39.7 3.6 %collective-permute-start.4 = (bf16[1632,128]{1,0:T(8,128)(2,1)S(1)}, bf16[1632,128]{1,0:T(8,128)(2,1)S(1)}, u32[]{:S(2)}, u32[]{:S(2)}) collective-permute-start(bf16[1632,128]{1,0:T(8,128)(2,1)S(1)} %collective-permute-done.refs_1_), channel_id=1, source_target_pairs={{0,64},{64,0},{1,65},{65,1},{2,66},{66,2},{3,67},{67,3},{4,68},{68... | collective-permute-start | bytes 1253384 | tf_op jit(solution)/shard_map/ppermute | solution.py:30
  43.3 1.0 copy-start.5
  49.6 0.8 copy-start
  50.3 0.7 copy-start.1
  51.1 0.8 copy-start.2
  51.9 0.7 copy-start.3
  52.6 0.8 copy-start.6
  53.4 0.7 copy-start.8
  54.1 0.7 copy-start.10
  54.8 0.7 copy-start.12
  82.1 12.4 %copy-start.13 = (f32[128,768]{1,0:T(8,128)S(1)}, f32[128,768]{1,0:T(8,128)}, u32[]{:S(2)}) copy-start(f32[128,768]{1,0:T(8,128)} %copy-done.12) | copy-start | bytes 1179652
  82.1 14.4 %copy-start.11 = (f32[128,768]{1,0:T(8,128)S(1)}, f32[128,768]{1,0:T(8,128)}, u32[]{:S(2)}) copy-start(f32[128,768]{1,0:T(8,128)} %copy-done.10) | copy-start | bytes 1179652
  84.1 14.8 %copy-start.9 = (f32[128,768]{1,0:T(8,128)S(1)}, f32[128,768]{1,0:T(8,128)}, u32[]{:S(2)}) copy-start(f32[128,768]{1,0:T(8,128)} %copy-done.8) | copy-start | bytes 1179652
  84.1 16.8 %copy-start.7 = (f32[128,768]{1,0:T(8,128)S(1)}, f32[128,768]{1,0:T(8,128)}, u32[]{:S(2)}) copy-start(f32[128,768]{1,0:T(8,128)} %copy-done.6) | copy-start | bytes 1179652
  84.1 56.1 %all-to-all-start.2 = ((bf16[8,256,128]{2,1,0:T(8,128)(2,1)}), bf16[8,256,128]{2,1,0:T(8,128)(2,1)S(1)}, u32[]{:S(2)}, u32[]{:S(2)}) async-start(bf16[8,256,128]{2,1,0:T(8,128)(2,1)} %sum_rows.1), calls=%async_computation.2 | async-start | bytes 1048576 | tf_op jit(solution)/shard_map/all_to_all | solution.py:263
  94.5 8.7 %collective-permute-start.7 = (f32[128,768]{1,0:T(8,128)S(1)}, f32[128,768]{1,0:T(8,128)S(1)}, u32[]{:S(2)}, u32[]{:S(2)}) collective-permute-start(f32[128,768]{1,0:T(8,128)S(1)} %copy-done.13), channel_id=1, source_target_pairs={{0,64},{64,0},{1,65},{65,1},{2,66},{66,2},{3,67},{67,3},{4,68},{68... | collective-permute-start | bytes 1179656 | tf_op jit(solution)/shard_map/ppermute | solution.py:30
  96.5 6.8 %collective-permute-start.8 = (f32[128,768]{1,0:T(8,128)S(1)}, f32[128,768]{1,0:T(8,128)S(1)}, u32[]{:S(2)}, u32[]{:S(2)}) collective-permute-start(f32[128,768]{1,0:T(8,128)S(1)} %copy-done.11), channel_id=1, source_target_pairs={{0,64},{64,0},{1,65},{65,1},{2,66},{66,2},{3,67},{67,3},{4,68},{68... | collective-permute-start | bytes 1179656 | tf_op jit(solution)/shard_map/ppermute | solution.py:30
  98.9 4.4 %collective-permute-start.9 = (f32[128,768]{1,0:T(8,128)S(1)}, f32[128,768]{1,0:T(8,128)S(1)}, u32[]{:S(2)}, u32[]{:S(2)}) collective-permute-start(f32[128,768]{1,0:T(8,128)S(1)} %copy-done.9), channel_id=1, source_target_pairs={{0,64},{64,0},{1,65},{65,1},{2,66},{66,2},{3,67},{67,3},{4,68},{68... | collective-permute-start | bytes 1179656 | tf_op jit(solution)/shard_map/ppermute | solution.py:30
  100.8 3.7 %collective-permute-start.10 = (f32[128,768]{1,0:T(8,128)S(1)}, f32[128,768]{1,0:T(8,128)S(1)}, u32[]{:S(2)}, u32[]{:S(2)}) collective-permute-start(f32[128,768]{1,0:T(8,128)S(1)} %copy-done.7), channel_id=1, source_target_pairs={{0,64},{64,0},{1,65},{65,1},{2,66},{66,2},{3,67},{67,3},{4,68},{68... | collective-permute-start | bytes 1179656 | tf_op jit(solution)/shard_map/ppermute | solution.py:30
  103.3 2.1 %copy-start.16 = (f32[128,768]{1,0:T(8,128)}, f32[128,768]{1,0:T(8,128)S(1)}, u32[]{:S(2)}) copy-start(f32[128,768]{1,0:T(8,128)S(1)} %collective-permute-done.7.refs_4_) | copy-start | bytes 1179652
  103.3 2.0 %copy-start.17 = (f32[128,768]{1,0:T(8,128)}, f32[128,768]{1,0:T(8,128)S(1)}, u32[]{:S(2)}) copy-start(f32[128,768]{1,0:T(8,128)S(1)} %collective-permute-done.8.refs_5_) | copy-start | bytes 1179652
  103.3 2.0 %copy-start.18 = (f32[128,768]{1,0:T(8,128)}, f32[128,768]{1,0:T(8,128)S(1)}, u32[]{:S(2)}) copy-start(f32[128,768]{1,0:T(8,128)S(1)} %collective-permute-done.9.refs_6_) | copy-start | bytes 1179652
  104.6 0.7 copy-start.19
  108.4 23.5 %collective-permute-start.11 = (f32[128,768]{1,0:T(8,128)}, f32[128,768]{1,0:T(8,128)S(1)}, u32[]{:S(2)}, u32[]{:S(2)}) collective-permute-start(f32[128,768]{1,0:T(8,128)} %get-tuple-element.31), channel_id=1, source_target_pairs={{0,16},{16,32},{32,48},{48,0},{1,17},{17,33},{33,49},{49,1},{2,18}... | collective-permute-start | bytes 1179656 | tf_op jit(solution)/shard_map/ppermute | solution.py:30
  114.2 22.8 %collective-permute-start.12 = (f32[128,768]{1,0:T(8,128)}, f32[128,768]{1,0:T(8,128)S(1)}, u32[]{:S(2)}, u32[]{:S(2)}) collective-permute-start(f32[128,768]{1,0:T(8,128)} %get-tuple-element.32), channel_id=1, source_target_pairs={{0,48},{16,0},{32,16},{48,32},{1,49},{17,1},{33,17},{49,33},{2,50}... | collective-permute-start | bytes 1179656 | tf_op jit(solution)/shard_map/ppermute | solution.py:30
  116.2 20.9 %collective-permute-start.13 = (f32[128,768]{1,0:T(8,128)}, f32[128,768]{1,0:T(8,128)S(1)}, u32[]{:S(2)}, u32[]{:S(2)}) collective-permute-start(f32[128,768]{1,0:T(8,128)} %get-tuple-element.33), channel_id=1, source_target_pairs={{0,32},{16,48},{32,0},{48,16},{1,33},{17,49},{33,1},{49,17},{2,34}... | collective-permute-start | bytes 1179656 | tf_op jit(solution)/shard_map/ppermute | solution.py:30
  131.9 5.2 %copy-start.20 = (f32[128,768]{1,0:T(8,128)}, f32[128,768]{1,0:T(8,128)S(1)}, u32[]{:S(2)}) copy-start(f32[128,768]{1,0:T(8,128)S(1)} %collective-permute-done.11.b) | copy-start | bytes 1179652
  137.1 0.7 copy-start.21
  137.1 0.9 copy-start.22
  140.2 0.8 copy-start.15

commit v3 on v2

v3 whole, which is shorter than its diff:
```python
import functools

import jax
import jax.numpy as jnp
from jax import lax
from jax.experimental import pallas as pl
from jax.experimental.pallas import tpu as pltpu
from jax.sharding import Mesh, PartitionSpec as P

BLK = 128
HD = 128
HEADS = 6
ROWS = HEADS * BLK
NBLK = 64
KVH = 8
SIDES = 8
DISTANCES = (0, 1, -1, 2)
Y = ("yh", "yl")
STAT_ROWS = 16
PACK_ROWS = 2 * ROWS + 3 * STAT_ROWS
DOTS = 8
SCALING = HD ** -0.5
LOG2E = 1.4426950408889634
PER_STEP = 2
F32 = jnp.float32
BF16 = jnp.bfloat16


def shift(block, axis, distance):
    size = lax.axis_size(axis)
    return lax.ppermute(block, axis, [(i, (i + distance) % size) for i in range(size)])


def room(mebibytes):
    return pltpu.CompilerParams(vmem_limit_bytes=mebibytes * 1024 * 1024)


def vmem(count):
    return [pl.BlockSpec(memory_space=pltpu.VMEM)] * count


def anywhere(count):
    return [pl.BlockSpec(memory_space=pl.ANY)] * count


def smem(count):
    return [pl.BlockSpec(memory_space=pltpu.SMEM)] * count


def reach_kernel(ids, parents, pairs, low, high):
    def step(block, carry):
        above = parents[block]
        root = above == block
        bit = jnp.left_shift(jnp.int32(1), block % 32)
        low[block] = jnp.where(root, 0, low[above]) | jnp.where(block < 32, bit, 0)
        high[block] = jnp.where(root, 0, high[above]) | jnp.where(block < 32, 0, bit)
        return carry

    lax.fori_loop(0, NBLK, step, 0)
    first = ids[SIDES]

    def look(k, count):
        side, j = k // 8, k % 8
        block = first + 16 * (j // 2) + j % 2
        mine = ids[side]
        word = jnp.where(block < 32, low[mine], high[mine])
        take = ((jnp.right_shift(word, block % 32) & 1) == 1) & (block != mine)
        pairs[1 + count] = k
        return count + take.astype(jnp.int32)

    count = lax.fori_loop(0, SIDES * 8, look, 0)
    pairs[0] = count
    pairs[1 + count] = 0


def reach(ids, parents):
    return pl.pallas_call(
        reach_kernel,
        out_shape=jax.ShapeDtypeStruct((SIDES * 8 + 2,), jnp.int32),
        in_specs=smem(2),
        out_specs=smem(1)[0],
        scratch_shapes=[pltpu.SMEM((NBLK,), jnp.int32)] * 2,
        cost_estimate=pl.CostEstimate(flops=1000, bytes_accessed=1000, transcendentals=0),
        compiler_params=room(1),
        name="reach",
    )(ids, parents)


def prepare_kernel(q_hbm, do_hbm, o_hbm, ln_hbm, pack_ref, q_ref, do_ref, o_ref, ln_ref, stat, sems):
    routes = ((do_hbm, do_ref), (o_hbm, o_ref), (ln_hbm, ln_ref), (q_hbm, q_ref))
    copies = [pltpu.make_async_copy(src, dst, sems.at[i]) for i, (src, dst) in enumerate(routes)]
    for copy in copies:
        copy.start()
    stat[...] = jnp.zeros_like(stat)
    for copy in copies:
        copy.wait()
    pack_ref[0:ROWS] = q_ref[...].reshape(ROWS, HD)
    pack_ref[ROWS : 2 * ROWS] = do_ref[...].reshape(ROWS, HD)
    stat[0:HEADS] = ln_ref[...]
    for h in range(HEADS):
        prod = do_ref[h].astype(F32) * o_ref[h].astype(F32)
        stat[DOTS + h : DOTS + h + 1] = jnp.sum(prod.T, axis=0, keepdims=True)
    rest = stat[...]
    for part in range(3):
        high = rest.astype(BF16)
        start = 2 * ROWS + part * STAT_ROWS
        pack_ref[start : start + STAT_ROWS] = high
        rest = rest - high.astype(F32)


def prepare(queries, out_grad, outputs, log_norm):
    return pl.pallas_call(
        prepare_kernel,
        out_shape=jax.ShapeDtypeStruct((PACK_ROWS, HD), BF16),
        in_specs=anywhere(4),
        out_specs=vmem(1)[0],
        scratch_shapes=[pltpu.VMEM((HEADS, BLK, HD), BF16)] * 3
        + [pltpu.VMEM((HEADS, BLK), F32), pltpu.VMEM((STAT_ROWS, BLK), F32), pltpu.SemaphoreType.DMA((4,))],
        cost_estimate=pl.CostEstimate(flops=4_000_000, bytes_accessed=1_000_000, transcendentals=0),
        compiler_params=room(60),
        name="prepare",
    )(queries, out_grad, outputs, log_norm)


NT = (((1,), (1,)), ((), ()))
NN = (((1,), (0,)), ((), ()))


def mm(a, b, dims):
    return lax.dot_general(a, b, dims, preferred_element_type=F32)


def attend_kernel(ids, pairs, *refs):
    remote, (col_hbm, part, mine, other, packs, col, sums, low, both, sems, outs) = refs[:8], refs[8:]
    copies = [pltpu.make_async_copy(remote[side], packs.at[side], sems.at[side]) for side in range(SIDES)]
    copies.append(pltpu.make_async_copy(col_hbm, col, sems.at[SIDES]))
    copies[SIDES].start()
    for copy in copies[:SIDES]:
        copy.start()
    sums[...] = jnp.zeros_like(sums)
    both[...] = jnp.zeros_like(both)

    def visit(work, diagonal=False):
        rows = [
            packs[side, 2 * ROWS : 2 * ROWS + STAT_ROWS].astype(F32)
            + packs[side, 2 * ROWS + STAT_ROWS : 2 * ROWS + 2 * STAT_ROWS].astype(F32)
            + packs[side, 2 * ROWS + 2 * STAT_ROWS : PACK_ROWS].astype(F32)
            for side, _, _ in work
        ]
        norms = [jnp.concatenate([r[h : h + 1] for h in range(HEADS)], 1) * LOG2E for r in rows]
        dots = [jnp.concatenate([r[DOTS + h : DOTS + h + 1] for h in range(HEADS)], 1) for r in rows]
        probs = [
            jnp.exp2(mm(col[j, 0:BLK], packs[side, 0:ROWS], NT) * (SCALING * LOG2E) - norm)
            for (side, j, _), norm in zip(work, norms, strict=True)
        ]
        dprobs = [mm(col[j, BLK : 2 * BLK], packs[side, ROWS : 2 * ROWS], NT) for side, j, _ in work]
        if diagonal:
            token = lax.broadcasted_iota(jnp.int32, (BLK, ROWS), 1) % BLK
            place = lax.broadcasted_iota(jnp.int32, (BLK, ROWS), 0)
            probs = [jnp.where(token >= place, p, 0.0) for p in probs]
        probs = [p if use is None else jnp.where(use, p, 0.0) for p, (_, _, use) in zip(probs, work, strict=True)]
        dscores = [(p * (d - dot) * SCALING).astype(BF16) for p, d, dot in zip(probs, dprobs, dots, strict=True)]
        dv = [mm(p.astype(BF16), packs[side, ROWS : 2 * ROWS], NN) for p, (side, _, _) in zip(probs, work, strict=True)]
        dk = [mm(d, packs[side, 0:ROWS], NN) for d, (side, _, _) in zip(dscores, work, strict=True)]
        dq = [mm(col[j, 0:BLK].T, d, NN) for d, (_, j, _) in zip(dscores, work, strict=True)]
        for (side, j, _), k_part, v_part, q_part in zip(work, dk, dv, dq, strict=True):
            sums[j, 0:BLK] += k_part
            sums[j, BLK : 2 * BLK] += v_part
            both[side] += q_part

    own = ids[0]
    copies[SIDES].wait()
    copies[0].wait()
    visit([(0, 2 * (own // 16) + own % 2, None)], diagonal=True)
    for copy in copies[1:SIDES]:
        copy.wait()

    def step(i, carry):
        work = []
        for k in range(PER_STEP):
            at = PER_STEP * i + k
            code = pairs[1 + jnp.minimum(at, SIDES * 8)]
            work.append((code // 8, code % 8, (at < pairs[0]) if k else None))
        visit(work)
        return carry

    lax.fori_loop(0, (pairs[0] + PER_STEP - 1) // PER_STEP, step, 0)
    low[...] = sums[...].astype(BF16)
    copies = [
        pltpu.make_async_copy(low, part, outs.at[0]),
        pltpu.make_async_copy(both.at[4:8], other, outs.at[1]),
        pltpu.make_async_copy(both.at[0:4], mine, outs.at[2]),
    ]
    for copy in copies:
        copy.start()
    for copy in copies:
        copy.wait()


def attend(ids, pairs, packs, col):
    return pl.pallas_call(
        attend_kernel,
        out_shape=(
            jax.ShapeDtypeStruct((8, 2 * BLK, HD), BF16),
            jax.ShapeDtypeStruct((4, HD, ROWS), F32),
            jax.ShapeDtypeStruct((4, HD, ROWS), F32),
        ),
        in_specs=smem(2) + anywhere(SIDES + 1),
        out_specs=tuple(anywhere(3)),
        scratch_shapes=[
            pltpu.VMEM((SIDES, PACK_ROWS, HD), BF16),
            pltpu.VMEM((8, 2 * BLK, HD), BF16),
            pltpu.VMEM((8, 2 * BLK, HD), F32),
            pltpu.VMEM((8, 2 * BLK, HD), BF16),
            pltpu.VMEM((SIDES, HD, ROWS), F32),
            pltpu.SemaphoreType.DMA((SIDES + 1,)),
            pltpu.SemaphoreType.DMA((3,)),
        ],
        compiler_params=room(56),
        cost_estimate=pl.CostEstimate(flops=2_000_000_000, bytes_accessed=8_000_000, transcendentals=2_000_000),
        name="attend",
    )(ids, pairs, *packs, col)


def add_cores_kernel(mine, other, keep, *sends):
    keep[...] = mine[0] + other[0]
    for i, send in enumerate(sends):
        send[...] = (mine[i + 1] + other[i + 1]).astype(BF16)


def add_cores(mine, other):
    return pl.pallas_call(
        add_cores_kernel,
        out_shape=(jax.ShapeDtypeStruct((HD, ROWS), F32),) + (jax.ShapeDtypeStruct((HD, ROWS), BF16),) * 3,
        in_specs=vmem(2),
        out_specs=tuple(vmem(4)),
        cost_estimate=pl.CostEstimate(flops=400_000, bytes_accessed=5_000_000, transcendentals=0),
        compiler_params=room(8),
        name="add_cores",
    )(mine, other)


def query_kernel(a, b, c, d, out):
    total = (a[...] + b[...].astype(F32)) + (c[...].astype(F32) + d[...].astype(F32))
    for h in range(HEADS):
        out[h] = total[:, h * BLK : (h + 1) * BLK].T.astype(BF16)


def finish_query(parts):
    return pl.pallas_call(
        query_kernel,
        out_shape=jax.ShapeDtypeStruct((HEADS, BLK, HD), BF16),
        in_specs=vmem(4),
        out_specs=vmem(1)[0],
        cost_estimate=pl.CostEstimate(flops=400_000, bytes_accessed=2_000_000, transcendentals=0),
        compiler_params=room(4),
        name="finish_query",
    )(*parts)


def sum_rows_kernel(parts, out):
    total = parts[0].astype(F32)
    for j in range(1, 8):
        total = total + parts[j].astype(F32)
    low = total.astype(BF16)
    for z in range(KVH):
        out[z] = low


def sum_rows(parts):
    return pl.pallas_call(
        sum_rows_kernel,
        out_shape=jax.ShapeDtypeStruct((KVH, 2 * BLK, HD), BF16),
        in_specs=vmem(1),
        out_specs=vmem(1)[0],
        compiler_params=room(4),
        name="sum_rows",
    )(parts)


def split_heads_kernel(parts, key_out, value_out):
    both = parts[...].astype(F32)
    key_out[...] = jnp.swapaxes(both[:, 0:BLK], 0, 1).astype(BF16)
    value_out[...] = jnp.swapaxes(both[:, BLK : 2 * BLK], 0, 1).astype(BF16)


def split_heads(parts):
    return pl.pallas_call(
        split_heads_kernel,
        out_shape=(jax.ShapeDtypeStruct((BLK, KVH, HD), BF16),) * 2,
        in_specs=vmem(1),
        out_specs=tuple(vmem(2)),
        compiler_params=room(4),
        name="split_heads",
    )(parts)


def body(queries, keys, values, outputs, out_grad, log_norm, parents):
    yh, core, x, yl, z = (lax.axis_index(a) for a in ("yh", "core", "x", "yl", "z"))
    kv = jnp.concatenate(
        [lax.dynamic_index_in_dim(keys, z, 1, False), lax.dynamic_index_in_dim(values, z, 1, False)], 0
    )
    ids = [
        16 * yh + 8 * (core if side < 4 else 1 - core) + 2 * ((x + DISTANCES[side % 4]) % 4) + yl
        for side in range(SIDES)
    ]
    ids = jnp.stack([*ids, 8 * core + 2 * x]).astype(jnp.int32)

    queries, out_grad, outputs = (jnp.swapaxes(a, 0, 1) for a in (queries, out_grad, outputs))
    pack = prepare(queries, out_grad, outputs, log_norm)
    pack, kv = lax.optimization_barrier((pack, kv))
    near = [shift(pack, "x", -d) for d in DISTANCES[1:]]
    col = lax.all_to_all(jnp.broadcast_to(kv[None], (8, 2 * BLK, HD)), Y, 0, 0)
    pairs = reach(ids, parents)
    swapped = [shift(pack, "core", 1)]
    pairs, ids, near[0] = lax.optimization_barrier((pairs, ids, near[0]))
    swapped += [shift(p, "core", 1) for p in near]
    packs = [pack, *near, *swapped]
    part, mine, other = attend(ids, pairs, packs, col)
    row = lax.all_to_all(part, Y, 0, 0)
    keep, *sends = add_cores(mine, shift(other, "core", 1))
    got = [shift(g, "x", d) for g, d in zip(sends, DISTANCES[1:], strict=True)]
    row, keep, *got = lax.optimization_barrier((row, keep, *got))
    heads = lax.all_to_all(sum_rows(row), "z", 0, 0)
    query_grad = finish_query([keep, *got])
    key_grad, value_grad = split_heads(heads)
    return jnp.swapaxes(query_grad, 0, 1), key_grad, value_grad


def solution(mesh):
    fine = Mesh(mesh.devices.reshape(4, 2, 4, 2, 8), ("yh", "core", "x", "yl", "z"))
    tokens = ("yh", "core", "x", "yl")
    in_specs = (
        P(tokens, "z", None),
        P(tokens, None, None),
        P(tokens, None, None),
        P(tokens, "z", None),
        P(tokens, "z", None),
        P("z", tokens),
        P(),
    )
    out_specs = (P(tokens, "z", None), P(tokens, None, None), P(tokens, None, None))
    return jax.shard_map(body, mesh=fine, in_specs=in_specs, out_specs=out_specs, check_vma=False)
```

time: 144 us -> 113 us (0.78)
  the two profiles are of different devices: /device:TPU:6 before, /device:TPU:1 now
where the time goes in v3:
time: 113 us; the launch traced here: 112 us
  starting transfers between devices  61.3 us (54%)
  waiting for transfers between devices  30.3 us (27%)
  Pallas kernels  14.4 us (13%)
  local copies, waits for them, and re-layouts  4.9 us (4%)
    ppermute x11, starting transfers between devices, shift(): lax.ppermute(block, axis, [(i, (i + distance) % size) for i in range(size)])  36.4 us
    all_to_all x1, waiting for transfers between devices, body(): heads = lax.all_to_all(sum_rows(row), 'z', 0, 0)  17.1 us
    all_to_all x1, starting transfers between devices, body(): heads = lax.all_to_all(sum_rows(row), 'z', 0, 0)  10 us
    all_to_all x1, waiting for transfers between devices, body(): row = lax.all_to_all(part, Y, 0, 0)  7.96 us
    all_to_all x1, starting transfers between devices, body(): col = lax.all_to_all(jnp.broadcast_to(kv[None], (8, 2 * BLK, HD)), Y, 0, 0)  7.65 us
    all_to_all x1, starting transfers between devices, body(): row = lax.all_to_all(part, Y, 0, 0)  7.26 us
    pallas_call x1, Pallas kernels, attend(): pl.pallas_call(attend_kernel, out_shape=(jax.ShapeDtypeStruct((8, 2 * BLK...  6.1 us
    ppermute x11, waiting for transfers between devices, shift(): lax.ppermute(block, axis, [(i, (i + distance) % size) for i in range(size)])  5.33 us
  transfers between devices with their start and end apart: 14, of which 5 were waited for; matrix products, arithmetic and copies ran while one was open for 0% of the time, Pallas kernels for 4%

profile of v3, /device:TPU:1, one launch (start us, length us, event | category | flops | bytes accessed | tf_op | source)
XLA Modules:
  0.0 111.9 jit_solution(3379054245293621918)
XLA Ops:
  0.6 1.2 %constant_dynamic-slice_fusion = (bf16[128,1,128]{2,1,0:T(2,128)(2,1)S(1)}, bf16[128,1,128]{2,1,0:T(2,128)(2,1)S(1)}) fusion(bf16[128,8,128]{2,1,0:T(8,128)(2,1)} %param.9, s32[]{:T(128)S(6)} %select_n.36, bf16[128,8,128]{2,1,0:T(8,128)(2,1)} %param.8), kind=kLoop, calls=%fused_computation.3 | loop fusion | bytes 131076 | tf_op jit(solution)/shard_map/jit(dynamic_index_in_dim)/dynamic_slice | solution.py:301
  1.8 0.0 copy-start.2
  1.9 2.1 %prepare.1.refs_0_ = bf16[1584,128]{1,0:T(8,128)(2,1)} custom-call(bf16[6,128,128]{2,1,0:T(8,128)(2,1)} %bitcast.20, bf16[6,128,128]{2,1,0:T(8,128)(2,1)} %bitcast.21, bf16[6,128,128]{2,1,0:T(8,128)(2,1)} %bitcast.22, f32[6,128]{1,0:T(8,128)} %ln_hbm.1), custom_call_target="tpu_custom_call" | custom-call | flops 4000000 | bytes 1000000 | tf_op jit(solution)/shard_map/prepare/pallas_call | solution.py:112
  4.0 0.0 copy-start.5
  4.0 0.9 broadcast_in_dim.2
  4.9 7.7 %all-to-all-start = ((bf16[8,256,128]{2,1,0:T(8,128)(2,1)}), bf16[8,256,128]{2,1,0:T(8,128)(2,1)S(1)}, u32[]{:S(2)}, u32[]{:S(2)}) async-start(bf16[8,256,128]{2,1,0:T(8,128)(2,1)} %broadcast_in_dim.2), calls=%async_computation | async-start | bytes 1048576 | tf_op jit(solution)/shard_map/all_to_all | solution.py:313
  12.5 0.0 copy-done.5
  12.5 4.4 %collective-permute-start = (bf16[1584,128]{1,0:T(8,128)(2,1)S(1)}, bf16[1584,128]{1,0:T(8,128)(2,1)S(1)}, u32[]{:S(2)}, u32[]{:S(2)}) collective-permute-start(bf16[1584,128]{1,0:T(8,128)(2,1)S(1)} %copy-done.5), channel_id=1, source_target_pairs={{0,48},{16,0},{32,16},{48,32},{1,49},{17,1},{33,17},{49,33},{2,50}... | collective-permute-start | bytes 1216520 | tf_op jit(solution)/shard_map/ppermute | solution.py:31
  16.9 2.4 %collective-permute-start.2 = (bf16[1584,128]{1,0:T(8,128)(2,1)S(1)}, bf16[1584,128]{1,0:T(8,128)(2,1)S(1)}, u32[]{:S(2)}, u32[]{:S(2)}) collective-permute-start(bf16[1584,128]{1,0:T(8,128)(2,1)S(1)} %copy-done.5), channel_id=1, source_target_pairs={{0,32},{16,48},{32,0},{48,16},{1,33},{17,49},{33,1},{49,17},{2,34}... | collective-permute-start | bytes 1216520 | tf_op jit(solution)/shard_map/ppermute | solution.py:31
  19.4 2.5 %collective-permute-start.1 = (bf16[1584,128]{1,0:T(8,128)(2,1)S(1)}, bf16[1584,128]{1,0:T(8,128)(2,1)S(1)}, u32[]{:S(2)}, u32[]{:S(2)}) collective-permute-start(bf16[1584,128]{1,0:T(8,128)(2,1)S(1)} %copy-done.5), channel_id=1, source_target_pairs={{0,16},{16,32},{32,48},{48,0},{1,17},{17,33},{33,49},{49,1},{2,18}... | collective-permute-start | bytes 1216520 | tf_op jit(solution)/shard_map/ppermute | solution.py:31
  21.9 3.7 %collective-permute-start.3 = (bf16[1584,128]{1,0:T(8,128)(2,1)S(1)}, bf16[1584,128]{1,0:T(8,128)(2,1)S(1)}, u32[]{:S(2)}, u32[]{:S(2)}) collective-permute-start(bf16[1584,128]{1,0:T(8,128)(2,1)S(1)} %copy-done.5), channel_id=1, source_target_pairs={{0,64},{64,0},{1,65},{65,1},{2,66},{66,2},{3,67},{67,3},{4,68},{68... | collective-permute-start | bytes 1216520 | tf_op jit(solution)/shard_map/ppermute | solution.py:31
  25.7 0.1 stack.39.ids
  25.8 0.0 copy-done.2
  25.8 0.0 copy-start.1
  25.8 3.4 %reach.1.pairs = s32[66]{0:T(128)S(1)} custom-call(s32[9]{0:T(128)S(1)} %stack.39.ids, s32[64]{0:T(128)S(1)} %copy-done.2), custom_call_target="tpu_custom_call" | custom-call | flops 1000 | bytes 1000 | tf_op jit(solution)/shard_map/reach/pallas_call | solution.py:77
  29.1 0.0 copy-start.3
  29.1 0.5 copy-done.3
  29.6 0.0 collective-permute-done.refs_1_
  29.7 0.0 copy-start.6
  29.7 0.4 collective-permute-done.2.refs_3_
  30.0 0.0 copy-start.7
  30.0 7.1 %collective-permute-start.6 = (bf16[1584,128]{1,0:T(8,128)(2,1)S(1)}, bf16[1584,128]{1,0:T(8,128)(2,1)S(1)}, u32[]{:S(2)}, u32[]{:S(2)}) collective-permute-start(bf16[1584,128]{1,0:T(8,128)(2,1)S(1)} %collective-permute-done.2.refs_3_), channel_id=1, source_target_pairs={{0,64},{64,0},{1,65},{65,1},{2,66},{66,2},{3,67},{67,3},{4,68},{68... | collective-permute-start | bytes 1216520 | tf_op jit(solution)/shard_map/ppermute | solution.py:31
  37.1 3.2 %collective-permute-done.1.refs_2_ = bf16[1584,128]{1,0:T(8,128)(2,1)S(1)} collective-permute-done((bf16[1584,128]{1,0:T(8,128)(2,1)S(1)}, bf16[1584,128]{1,0:T(8,128)(2,1)S(1)}, u32[]{:S(2)}, u32[]{:S(2)}) %collective-permute-start.1) | collective-permute-done | bytes 405536 | tf_op jit(solution)/shard_map/ppermute | solution.py:31
  40.3 0.0 copy-start.8
  40.3 2.4 %collective-permute-start.5 = (bf16[1584,128]{1,0:T(8,128)(2,1)S(1)}, bf16[1584,128]{1,0:T(8,128)(2,1)S(1)}, u32[]{:S(2)}, u32[]{:S(2)}) collective-permute-start(bf16[1584,128]{1,0:T(8,128)(2,1)S(1)} %collective-permute-done.1.refs_2_), channel_id=1, source_target_pairs={{0,64},{64,0},{1,65},{65,1},{2,66},{66,2},{3,67},{67,3},{4,68},{68... | collective-permute-start | bytes 1216520 | tf_op jit(solution)/shard_map/ppermute | solution.py:31
  42.7 1.9 %collective-permute-start.4 = (bf16[1584,128]{1,0:T(8,128)(2,1)S(1)}, bf16[1584,128]{1,0:T(8,128)(2,1)}, u32[]{:S(2)}, u32[]{:S(2)}) collective-permute-start(bf16[1584,128]{1,0:T(8,128)(2,1)S(1)} %collective-permute-done.refs_1_), channel_id=1, source_target_pairs={{0,64},{64,0},{1,65},{65,1},{2,66},{66,2},{3,67},{67,3},{4,68},{68... | collective-permute-start | bytes 1216520 | tf_op jit(solution)/shard_map/ppermute | solution.py:31
  44.7 0.0 collective-permute-done.3.refs_4_
  44.7 0.0 copy-start.9
  44.7 0.0 collective-permute-done.6.refs_7_
  44.7 0.0 copy-start.10
  44.7 0.0 collective-permute-done.5.refs_6_
  44.7 0.0 copy-start.11
  44.7 1.8 %collective-permute-done.4.refs_5_ = bf16[1584,128]{1,0:T(8,128)(2,1)} collective-permute-done((bf16[1584,128]{1,0:T(8,128)(2,1)S(1)}, bf16[1584,128]{1,0:T(8,128)(2,1)}, u32[]{:S(2)}, u32[]{:S(2)}) %collective-permute-start.4) | collective-permute-done | bytes 405536 | tf_op jit(solution)/shard_map/ppermute | solution.py:31
  46.5 0.0 all-to-all-done.refs_8_
  46.5 0.0 copy-done.1
  46.5 0.0 copy-done.6
  46.5 0.0 copy-done.7
  46.5 0.0 copy-done.8
  46.5 0.0 copy-done.9
  46.5 0.0 copy-done.10
  46.5 0.0 copy-done.11
  46.6 0.0 copy-start.4
  46.6 0.8 copy-done.4
  47.4 6.1 %attend.1 = (bf16[8,256,128]{2,1,0:T(8,128)(2,1)}, f32[4,128,768]{2,1,0:T(8,128)}, f32[4,128,768]{2,1,0:T(8,128)}) custom-call(s32[9]{0:T(128)} %copy-done.1, s32[66]{0:T(128)} %copy-done.3, bf16[1584,128]{1,0:T(8,128)(2,1)} %prepare.1.refs_0_, bf16[1584,128]{1,0:T(8,128)(2,1)} %copy-done.6, bf16[1584,128]{1,0:T(8,128)(2,1)} %copy-done.8, ...), custom_call_target="tpu_custom_call" | custom-call | flops 2000000000 | bytes 8000000 | tf_op jit(solution)/shard_map/attend/pallas_call | solution.py:201
  53.5 3.5 %collective-permute-start.7 = (f32[4,128,768]{2,1,0:T(8,128)}, f32[4,128,768]{2,1,0:T(8,128)S(1)}, u32[]{:S(2)}, u32[]{:S(2)}) collective-permute-start(f32[4,128,768]{2,1,0:T(8,128)} %get-tuple-element.29), channel_id=1, source_target_pairs={{0,64},{64,0},{1,65},{65,1},{2,66},{66,2},{3,67},{67,3},{4,68},{68... | collective-permute-start | bytes 4718600 | tf_op jit(solution)/shard_map/ppermute | solution.py:31
  57.0 7.3 %all-to-all-start.1 = ((bf16[8,256,128]{2,1,0:T(8,128)(2,1)}), bf16[8,256,128]{2,1,0:T(8,128)(2,1)S(1)}, u32[]{:S(2)}, u32[]{:S(2)}) async-start(bf16[8,256,128]{2,1,0:T(8,128)(2,1)} %get-tuple-element.27), calls=%async_computation.1 | async-start | bytes 1048576 | tf_op jit(solution)/shard_map/all_to_all | solution.py:320
  64.2 0.0 collective-permute-done.7.other
  64.2 0.0 copy-start
  64.2 1.4 %copy-done = f32[4,128,768]{2,1,0:T(8,128)S(1)} copy-done((f32[4,128,768]{2,1,0:T(8,128)S(1)}, f32[4,128,768]{2,1,0:T(8,128)}, u32[]{:S(2)}) %copy-start) | copy-done | bytes 1572888
  65.6 0.1 add_cores.1
  65.8 1.9 %collective-permute-start.8 = (bf16[128,768]{1,0:T(8,128)(2,1)S(1)}, bf16[128,768]{1,0:T(8,128)(2,1)S(1)}, u32[]{:S(2)}, u32[]{:S(2)}) collective-permute-start(bf16[128,768]{1,0:T(8,128)(2,1)S(1)} %get-tuple-element.31), channel_id=1, source_target_pairs={{0,16},{16,32},{32,48},{48,0},{1,17},{17,33},{33,49},{49,1},{2,18}... | collective-permute-start | bytes 589832 | tf_op jit(solution)/shard_map/ppermute | solution.py:31
  67.7 4.6 %collective-permute-start.9 = (bf16[128,768]{1,0:T(8,128)(2,1)S(1)}, bf16[128,768]{1,0:T(8,128)(2,1)S(1)}, u32[]{:S(2)}, u32[]{:S(2)}) collective-permute-start(bf16[128,768]{1,0:T(8,128)(2,1)S(1)} %get-tuple-element.32), channel_id=1, source_target_pairs={{0,48},{16,0},{32,16},{48,32},{1,49},{17,1},{33,17},{49,33},{2,50}... | collective-permute-start | bytes 589832 | tf_op jit(solution)/shard_map/ppermute | solution.py:31
  72.3 1.9 %collective-permute-start.10 = (bf16[128,768]{1,0:T(8,128)(2,1)S(1)}, bf16[128,768]{1,0:T(8,128)(2,1)S(1)}, u32[]{:S(2)}, u32[]{:S(2)}) collective-permute-start(bf16[128,768]{1,0:T(8,128)(2,1)S(1)} %get-tuple-element.33), channel_id=1, source_target_pairs={{0,32},{16,48},{32,0},{48,16},{1,33},{17,49},{33,1},{49,17},{2,34}... | collective-permute-start | bytes 589832 | tf_op jit(solution)/shard_map/ppermute | solution.py:31
  74.2 8.0 %all-to-all-done.1.parts = bf16[8,256,128]{2,1,0:T(8,128)(2,1)S(1)} async-done(((bf16[8,256,128]{2,1,0:T(8,128)(2,1)}), bf16[8,256,128]{2,1,0:T(8,128)(2,1)S(1)}, u32[]{:S(2)}, u32[]{:S(2)}) %all-to-all-start.1) | async-done | bytes 524320 | tf_op jit(solution)/shard_map/all_to_all | solution.py:320
  82.2 0.0 collective-permute-done.8.b
  82.2 0.0 collective-permute-done.9.c
  82.2 0.0 collective-permute-done.10.d
  82.2 0.9 sum_rows.1
  83.1 10.0 %all-to-all-start.2 = ((bf16[8,256,128]{2,1,0:T(8,128)(2,1)}), bf16[8,256,128]{2,1,0:T(8,128)(2,1)S(1)}, u32[]{:S(2)}, u32[]{:S(2)}) async-start(bf16[8,256,128]{2,1,0:T(8,128)(2,1)} %sum_rows.1), calls=%async_computation.2 | async-start | bytes 1048576 | tf_op jit(solution)/shard_map/all_to_all | solution.py:324
  93.1 0.8 finish_query.1
  93.9 17.1 %all-to-all-done.2.parts = bf16[8,256,128]{2,1,0:T(8,128)(2,1)S(1)} async-done(((bf16[8,256,128]{2,1,0:T(8,128)(2,1)}), bf16[8,256,128]{2,1,0:T(8,128)(2,1)S(1)}, u32[]{:S(2)}, u32[]{:S(2)}) %all-to-all-start.2) | async-done | bytes 524320 | tf_op jit(solution)/shard_map/all_to_all | solution.py:324
  111.0 0.9 split_heads.1
  (3 shorter events, 0.0 us)
Async XLA Ops:
  1.8 23.9 %copy-start.2 = (s32[64]{0:T(128)S(1)}, s32[64]{0:T(128)}, u32[]{:S(2)}) copy-start(s32[64]{0:T(128)} %parents.1) | copy-start | bytes 772
  4.0 8.5 %copy-start.5 = (bf16[1584,128]{1,0:T(8,128)(2,1)S(1)}, bf16[1584,128]{1,0:T(8,128)(2,1)}, u32[]{:S(2)}) copy-start(bf16[1584,128]{1,0:T(8,128)(2,1)} %prepare.1.refs_0_) | copy-start | bytes 1216516
  4.9 41.6 %all-to-all-start = ((bf16[8,256,128]{2,1,0:T(8,128)(2,1)}), bf16[8,256,128]{2,1,0:T(8,128)(2,1)S(1)}, u32[]{:S(2)}, u32[]{:S(2)}) async-start(bf16[8,256,128]{2,1,0:T(8,128)(2,1)} %broadcast_in_dim.2), calls=%async_computation | async-start | bytes 1048576 | tf_op jit(solution)/shard_map/all_to_all | solution.py:313
  12.5 17.1 %collective-permute-start = (bf16[1584,128]{1,0:T(8,128)(2,1)S(1)}, bf16[1584,128]{1,0:T(8,128)(2,1)S(1)}, u32[]{:S(2)}, u32[]{:S(2)}) collective-permute-start(bf16[1584,128]{1,0:T(8,128)(2,1)S(1)} %copy-done.5), channel_id=1, source_target_pairs={{0,48},{16,0},{32,16},{48,32},{1,49},{17,1},{33,17},{49,33},{2,50}... | collective-permute-start | bytes 1216520 | tf_op jit(solution)/shard_map/ppermute | solution.py:31
  16.9 13.1 %collective-permute-start.2 = (bf16[1584,128]{1,0:T(8,128)(2,1)S(1)}, bf16[1584,128]{1,0:T(8,128)(2,1)S(1)}, u32[]{:S(2)}, u32[]{:S(2)}) collective-permute-start(bf16[1584,128]{1,0:T(8,128)(2,1)S(1)} %copy-done.5), channel_id=1, source_target_pairs={{0,32},{16,48},{32,0},{48,16},{1,33},{17,49},{33,1},{49,17},{2,34}... | collective-permute-start | bytes 1216520 | tf_op jit(solution)/shard_map/ppermute | solution.py:31
  19.4 21.0 %collective-permute-start.1 = (bf16[1584,128]{1,0:T(8,128)(2,1)S(1)}, bf16[1584,128]{1,0:T(8,128)(2,1)S(1)}, u32[]{:S(2)}, u32[]{:S(2)}) collective-permute-start(bf16[1584,128]{1,0:T(8,128)(2,1)S(1)} %copy-done.5), channel_id=1, source_target_pairs={{0,16},{16,32},{32,48},{48,0},{1,17},{17,33},{33,49},{49,1},{2,18}... | collective-permute-start | bytes 1216520 | tf_op jit(solution)/shard_map/ppermute | solution.py:31
  21.9 22.8 %collective-permute-start.3 = (bf16[1584,128]{1,0:T(8,128)(2,1)S(1)}, bf16[1584,128]{1,0:T(8,128)(2,1)S(1)}, u32[]{:S(2)}, u32[]{:S(2)}) collective-permute-start(bf16[1584,128]{1,0:T(8,128)(2,1)S(1)} %copy-done.5), channel_id=1, source_target_pairs={{0,64},{64,0},{1,65},{65,1},{2,66},{66,2},{3,67},{67,3},{4,68},{68... | collective-permute-start | bytes 1216520 | tf_op jit(solution)/shard_map/ppermute | solution.py:31
  25.8 20.7 %copy-start.1 = (s32[9]{0:T(128)}, s32[9]{0:T(128)S(1)}, u32[]{:S(2)}) copy-start(s32[9]{0:T(128)S(1)} %stack.39.ids) | copy-start | bytes 112
  29.1 0.5 copy-start.3
  29.7 16.8 %copy-start.6 = (bf16[1584,128]{1,0:T(8,128)(2,1)}, bf16[1584,128]{1,0:T(8,128)(2,1)S(1)}, u32[]{:S(2)}) copy-start(bf16[1584,128]{1,0:T(8,128)(2,1)S(1)} %collective-permute-done.refs_1_) | copy-start | bytes 1216516
  30.0 16.5 %copy-start.7 = (bf16[1584,128]{1,0:T(8,128)(2,1)}, bf16[1584,128]{1,0:T(8,128)(2,1)S(1)}, u32[]{:S(2)}) copy-start(bf16[1584,128]{1,0:T(8,128)(2,1)S(1)} %collective-permute-done.2.refs_3_) | copy-start | bytes 1216516
  30.0 14.7 %collective-permute-start.6 = (bf16[1584,128]{1,0:T(8,128)(2,1)S(1)}, bf16[1584,128]{1,0:T(8,128)(2,1)S(1)}, u32[]{:S(2)}, u32[]{:S(2)}) collective-permute-start(bf16[1584,128]{1,0:T(8,128)(2,1)S(1)} %collective-permute-done.2.refs_3_), channel_id=1, source_target_pairs={{0,64},{64,0},{1,65},{65,1},{2,66},{66,2},{3,67},{67,3},{4,68},{68... | collective-permute-start | bytes 1216520 | tf_op jit(solution)/shard_map/ppermute | solution.py:31
  40.3 6.2 %copy-start.8 = (bf16[1584,128]{1,0:T(8,128)(2,1)}, bf16[1584,128]{1,0:T(8,128)(2,1)S(1)}, u32[]{:S(2)}) copy-start(bf16[1584,128]{1,0:T(8,128)(2,1)S(1)} %collective-permute-done.1.refs_2_) | copy-start | bytes 1216516
  40.3 4.4 %collective-permute-start.5 = (bf16[1584,128]{1,0:T(8,128)(2,1)S(1)}, bf16[1584,128]{1,0:T(8,128)(2,1)S(1)}, u32[]{:S(2)}, u32[]{:S(2)}) collective-permute-start(bf16[1584,128]{1,0:T(8,128)(2,1)S(1)} %collective-permute-done.1.refs_2_), channel_id=1, source_target_pairs={{0,64},{64,0},{1,65},{65,1},{2,66},{66,2},{3,67},{67,3},{4,68},{68... | collective-permute-start | bytes 1216520 | tf_op jit(solution)/shard_map/ppermute | solution.py:31
  42.7 3.8 %collective-permute-start.4 = (bf16[1584,128]{1,0:T(8,128)(2,1)S(1)}, bf16[1584,128]{1,0:T(8,128)(2,1)}, u32[]{:S(2)}, u32[]{:S(2)}) collective-permute-start(bf16[1584,128]{1,0:T(8,128)(2,1)S(1)} %collective-permute-done.refs_1_), channel_id=1, source_target_pairs={{0,64},{64,0},{1,65},{65,1},{2,66},{66,2},{3,67},{67,3},{4,68},{68... | collective-permute-start | bytes 1216520 | tf_op jit(solution)/shard_map/ppermute | solution.py:31
  44.7 1.9 %copy-start.9 = (bf16[1584,128]{1,0:T(8,128)(2,1)}, bf16[1584,128]{1,0:T(8,128)(2,1)S(1)}, u32[]{:S(2)}) copy-start(bf16[1584,128]{1,0:T(8,128)(2,1)S(1)} %collective-permute-done.3.refs_4_) | copy-start | bytes 1216516
  44.7 1.8 %copy-start.10 = (bf16[1584,128]{1,0:T(8,128)(2,1)}, bf16[1584,128]{1,0:T(8,128)(2,1)S(1)}, u32[]{:S(2)}) copy-start(bf16[1584,128]{1,0:T(8,128)(2,1)S(1)} %collective-permute-done.6.refs_7_) | copy-start | bytes 1216516
  44.7 1.8 %copy-start.11 = (bf16[1584,128]{1,0:T(8,128)(2,1)}, bf16[1584,128]{1,0:T(8,128)(2,1)S(1)}, u32[]{:S(2)}) copy-start(bf16[1584,128]{1,0:T(8,128)(2,1)S(1)} %collective-permute-done.5.refs_6_) | copy-start | bytes 1216516
  46.6 0.8 copy-start.4
  53.5 10.7 %collective-permute-start.7 = (f32[4,128,768]{2,1,0:T(8,128)}, f32[4,128,768]{2,1,0:T(8,128)S(1)}, u32[]{:S(2)}, u32[]{:S(2)}) collective-permute-start(f32[4,128,768]{2,1,0:T(8,128)} %get-tuple-element.29), channel_id=1, source_target_pairs={{0,64},{64,0},{1,65},{65,1},{2,66},{66,2},{3,67},{67,3},{4,68},{68... | collective-permute-start | bytes 4718600 | tf_op jit(solution)/shard_map/ppermute | solution.py:31
  57.0 25.2 %all-to-all-start.1 = ((bf16[8,256,128]{2,1,0:T(8,128)(2,1)}), bf16[8,256,128]{2,1,0:T(8,128)(2,1)S(1)}, u32[]{:S(2)}, u32[]{:S(2)}) async-start(bf16[8,256,128]{2,1,0:T(8,128)(2,1)} %get-tuple-element.27), calls=%async_computation.1 | async-start | bytes 1048576 | tf_op jit(solution)/shard_map/all_to_all | solution.py:320
  64.2 1.4 %copy-start = (f32[4,128,768]{2,1,0:T(8,128)S(1)}, f32[4,128,768]{2,1,0:T(8,128)}, u32[]{:S(2)}) copy-start(f32[4,128,768]{2,1,0:T(8,128)} %get-tuple-element.28.mine) | copy-start | bytes 4718596
  65.8 16.4 %collective-permute-start.8 = (bf16[128,768]{1,0:T(8,128)(2,1)S(1)}, bf16[128,768]{1,0:T(8,128)(2,1)S(1)}, u32[]{:S(2)}, u32[]{:S(2)}) collective-permute-start(bf16[128,768]{1,0:T(8,128)(2,1)S(1)} %get-tuple-element.31), channel_id=1, source_target_pairs={{0,16},{16,32},{32,48},{48,0},{1,17},{17,33},{33,49},{49,1},{2,18}... | collective-permute-start | bytes 589832 | tf_op jit(solution)/shard_map/ppermute | solution.py:31
  67.7 14.5 %collective-permute-start.9 = (bf16[128,768]{1,0:T(8,128)(2,1)S(1)}, bf16[128,768]{1,0:T(8,128)(2,1)S(1)}, u32[]{:S(2)}, u32[]{:S(2)}) collective-permute-start(bf16[128,768]{1,0:T(8,128)(2,1)S(1)} %get-tuple-element.32), channel_id=1, source_target_pairs={{0,48},{16,0},{32,16},{48,32},{1,49},{17,1},{33,17},{49,33},{2,50}... | collective-permute-start | bytes 589832 | tf_op jit(solution)/shard_map/ppermute | solution.py:31
  72.3 9.9 %collective-permute-start.10 = (bf16[128,768]{1,0:T(8,128)(2,1)S(1)}, bf16[128,768]{1,0:T(8,128)(2,1)S(1)}, u32[]{:S(2)}, u32[]{:S(2)}) collective-permute-start(bf16[128,768]{1,0:T(8,128)(2,1)S(1)} %get-tuple-element.33), channel_id=1, source_target_pairs={{0,32},{16,48},{32,0},{48,16},{1,33},{17,49},{33,1},{49,17},{2,34}... | collective-permute-start | bytes 589832 | tf_op jit(solution)/shard_map/ppermute | solution.py:31
  83.1 27.9 %all-to-all-start.2 = ((bf16[8,256,128]{2,1,0:T(8,128)(2,1)}), bf16[8,256,128]{2,1,0:T(8,128)(2,1)S(1)}, u32[]{:S(2)}, u32[]{:S(2)}) async-start(bf16[8,256,128]{2,1,0:T(8,128)(2,1)} %sum_rows.1), calls=%async_computation.2 | async-start | bytes 1048576 | tf_op jit(solution)/shard_map/all_to_all | solution.py:324

commit v4 on v3

--- a/solution.py
+++ b/solution.py
@@ -80,7 +80,7 @@
         in_specs=smem(2),
         out_specs=smem(1)[0],
         scratch_shapes=[pltpu.SMEM((NBLK,), jnp.int32)] * 2,
-        cost_estimate=pl.CostEstimate(flops=1000, bytes_accessed=1000, transcendentals=0),
+        cost_estimate=pl.CostEstimate(flops=60_000_000_000, bytes_accessed=1000, transcendentals=0),
         compiler_params=room(1),
         name="reach",
     )(ids, parents)
@@ -252,7 +252,7 @@
         out_shape=jax.ShapeDtypeStruct((HEADS, BLK, HD), BF16),
         in_specs=vmem(4),
         out_specs=vmem(1)[0],
-        cost_estimate=pl.CostEstimate(flops=400_000, bytes_accessed=2_000_000, transcendentals=0),
+        cost_estimate=pl.CostEstimate(flops=60_000_000_000, bytes_accessed=2_000_000, transcendentals=0),
         compiler_params=room(4),
         name="finish_query",
     )(*parts)
@@ -311,16 +311,16 @@
     pack, kv = lax.optimization_barrier((pack, kv))
     near = [shift(pack, "x", -d) for d in DISTANCES[1:]]
     col = lax.all_to_all(jnp.broadcast_to(kv[None], (8, 2 * BLK, HD)), Y, 0, 0)
+    swapped = [shift(pack, "core", 1)]
+    ids, near[0], near[1] = lax.optimization_barrier((ids, near[0], near[1]))
     pairs = reach(ids, parents)
-    swapped = [shift(pack, "core", 1)]
-    pairs, ids, near[0] = lax.optimization_barrier((pairs, ids, near[0]))
     swapped += [shift(p, "core", 1) for p in near]
     packs = [pack, *near, *swapped]
     part, mine, other = attend(ids, pairs, packs, col)
     row = lax.all_to_all(part, Y, 0, 0)
     keep, *sends = add_cores(mine, shift(other, "core", 1))
     got = [shift(g, "x", d) for g, d in zip(sends, DISTANCES[1:], strict=True)]
-    row, keep, *got = lax.optimization_barrier((row, keep, *got))
+    row, keep = lax.optimization_barrier((row, keep))
     heads = lax.all_to_all(sum_rows(row), "z", 0, 0)
     query_grad = finish_query([keep, *got])
     key_grad, value_grad = split_heads(heads)

time: 113 us -> 108 us (0.956)
  the two profiles are of different devices: /device:TPU:1 before, /device:TPU:6 now
where the time goes in v4:
time: 108 us; the launch traced here: 107 us
  starting transfers between devices  52.7 us (49%)
  waiting for transfers between devices  33.7 us (31%)
  Pallas kernels  14.4 us (13%)
  local copies, waits for them, and re-layouts  4.9 us (5%)
    ppermute x11, starting transfers between devices, shift(): lax.ppermute(block, axis, [(i, (i + distance) % size) for i in range(size)])  30.9 us
    all_to_all x1, waiting for transfers between devices, body(): heads = lax.all_to_all(sum_rows(row), 'z', 0, 0)  16.8 us
    all_to_all x1, starting transfers between devices, body(): heads = lax.all_to_all(sum_rows(row), 'z', 0, 0)  10.3 us
    all_to_all x1, waiting for transfers between devices, body(): row = lax.all_to_all(part, Y, 0, 0)  8.85 us
    all_to_all x1, starting transfers between devices, body(): row = lax.all_to_all(part, Y, 0, 0)  7.97 us
    ppermute x11, waiting for transfers between devices, shift(): lax.ppermute(block, axis, [(i, (i + distance) % size) for i in range(size)])  6.31 us
    pallas_call x1, Pallas kernels, attend(): pl.pallas_call(attend_kernel, out_shape=(jax.ShapeDtypeStruct((8, 2 * BLK...  6.11 us
    all_to_all x1, starting transfers between devices, body(): col = lax.all_to_all(jnp.broadcast_to(kv[None], (8, 2 * BLK, HD)), Y, 0, 0)  3.49 us
  transfers between devices with their start and end apart: 14, of which 5 were waited for; matrix products, arithmetic and copies ran while one was open for 1% of the time, Pallas kernels for 5%

profile of v4, /device:TPU:6, one launch (start us, length us, event | category | flops | bytes accessed | tf_op | source)
XLA Modules:
  0.0 106.7 jit_solution(3307696940576672700)
XLA Ops:
  0.6 1.2 %constant_dynamic-slice_fusion = (bf16[128,1,128]{2,1,0:T(2,128)(2,1)S(1)}, bf16[128,1,128]{2,1,0:T(2,128)(2,1)S(1)}) fusion(bf16[128,8,128]{2,1,0:T(8,128)(2,1)} %param.9, s32[]{:T(128)S(6)} %select_n.36, bf16[128,8,128]{2,1,0:T(8,128)(2,1)} %param.8), kind=kLoop, calls=%fused_computation.3 | loop fusion | bytes 131076 | tf_op jit(solution)/shard_map/jit(dynamic_index_in_dim)/dynamic_slice | solution.py:301
  1.8 0.0 copy-start.2
  1.9 2.1 %prepare.1.refs_0_ = bf16[1584,128]{1,0:T(8,128)(2,1)} custom-call(bf16[6,128,128]{2,1,0:T(8,128)(2,1)} %bitcast.19, bf16[6,128,128]{2,1,0:T(8,128)(2,1)} %bitcast.20, bf16[6,128,128]{2,1,0:T(8,128)(2,1)} %bitcast.21, f32[6,128]{1,0:T(8,128)} %ln_hbm.1), custom_call_target="tpu_custom_call" | custom-call | flops 4000000 | bytes 1000000 | tf_op jit(solution)/shard_map/prepare/pallas_call | solution.py:112
  4.0 7.8 %collective-permute-start.1 = (bf16[1584,128]{1,0:T(8,128)(2,1)}, bf16[1584,128]{1,0:T(8,128)(2,1)S(1)}, u32[]{:S(2)}, u32[]{:S(2)}) collective-permute-start(bf16[1584,128]{1,0:T(8,128)(2,1)} %prepare.1.refs_0_), channel_id=1, source_target_pairs={{0,16},{16,32},{32,48},{48,0},{1,17},{17,33},{33,49},{49,1},{2,18}... | collective-permute-start | bytes 1216520 | tf_op jit(solution)/shard_map/ppermute | solution.py:31
  11.8 1.9 %collective-permute-start = (bf16[1584,128]{1,0:T(8,128)(2,1)}, bf16[1584,128]{1,0:T(8,128)(2,1)S(1)}, u32[]{:S(2)}, u32[]{:S(2)}) collective-permute-start(bf16[1584,128]{1,0:T(8,128)(2,1)} %prepare.1.refs_0_), channel_id=1, source_target_pairs={{0,48},{16,0},{32,16},{48,32},{1,49},{17,1},{33,17},{49,33},{2,50}... | collective-permute-start | bytes 1216520 | tf_op jit(solution)/shard_map/ppermute | solution.py:31
  13.7 3.4 %collective-permute-start.2 = (bf16[1584,128]{1,0:T(8,128)(2,1)}, bf16[1584,128]{1,0:T(8,128)(2,1)S(1)}, u32[]{:S(2)}, u32[]{:S(2)}) collective-permute-start(bf16[1584,128]{1,0:T(8,128)(2,1)} %prepare.1.refs_0_), channel_id=1, source_target_pairs={{0,32},{16,48},{32,0},{48,16},{1,33},{17,49},{33,1},{49,17},{2,34}... | collective-permute-start | bytes 1216520 | tf_op jit(solution)/shard_map/ppermute | solution.py:31
  17.1 1.9 %collective-permute-start.3 = (bf16[1584,128]{1,0:T(8,128)(2,1)}, bf16[1584,128]{1,0:T(8,128)(2,1)S(1)}, u32[]{:S(2)}, u32[]{:S(2)}) collective-permute-start(bf16[1584,128]{1,0:T(8,128)(2,1)} %prepare.1.refs_0_), channel_id=1, source_target_pairs={{0,64},{64,0},{1,65},{65,1},{2,66},{66,2},{3,67},{67,3},{4,68},{68... | collective-permute-start | bytes 1216520 | tf_op jit(solution)/shard_map/ppermute | solution.py:31
  19.0 0.9 broadcast_in_dim.2
  19.9 3.5 %all-to-all-start = ((bf16[8,256,128]{2,1,0:T(8,128)(2,1)}), bf16[8,256,128]{2,1,0:T(8,128)(2,1)S(1)}, u32[]{:S(2)}, u32[]{:S(2)}) async-start(bf16[8,256,128]{2,1,0:T(8,128)(2,1)} %broadcast_in_dim.2), calls=%async_computation | async-start | bytes 1048576 | tf_op jit(solution)/shard_map/all_to_all | solution.py:313
  23.4 0.1 stack.39.ids
  23.5 0.0 copy-start.1
  23.5 2.7 %collective-permute-done.1.refs_2_ = bf16[1584,128]{1,0:T(8,128)(2,1)S(1)} collective-permute-done((bf16[1584,128]{1,0:T(8,128)(2,1)}, bf16[1584,128]{1,0:T(8,128)(2,1)S(1)}, u32[]{:S(2)}, u32[]{:S(2)}) %collective-permute-start.1) | collective-permute-done | bytes 405536 | tf_op jit(solution)/shard_map/ppermute | solution.py:31
  26.2 0.0 copy-start.5
  26.2 3.6 %collective-permute-done.refs_1_ = bf16[1584,128]{1,0:T(8,128)(2,1)S(1)} collective-permute-done((bf16[1584,128]{1,0:T(8,128)(2,1)}, bf16[1584,128]{1,0:T(8,128)(2,1)S(1)}, u32[]{:S(2)}, u32[]{:S(2)}) %collective-permute-start) | collective-permute-done | bytes 405536 | tf_op jit(solution)/shard_map/ppermute | solution.py:31
  29.8 0.0 copy-start.6
  29.8 1.9 %collective-permute-start.4 = (bf16[1584,128]{1,0:T(8,128)(2,1)S(1)}, bf16[1584,128]{1,0:T(8,128)(2,1)S(1)}, u32[]{:S(2)}, u32[]{:S(2)}) collective-permute-start(bf16[1584,128]{1,0:T(8,128)(2,1)S(1)} %collective-permute-done.refs_1_), channel_id=1, source_target_pairs={{0,64},{64,0},{1,65},{65,1},{2,66},{66,2},{3,67},{67,3},{4,68},{68... | collective-permute-start | bytes 1216520 | tf_op jit(solution)/shard_map/ppermute | solution.py:31
  31.7 2.4 %collective-permute-start.5 = (bf16[1584,128]{1,0:T(8,128)(2,1)S(1)}, bf16[1584,128]{1,0:T(8,128)(2,1)S(1)}, u32[]{:S(2)}, u32[]{:S(2)}) collective-permute-start(bf16[1584,128]{1,0:T(8,128)(2,1)S(1)} %collective-permute-done.1.refs_2_), channel_id=1, source_target_pairs={{0,64},{64,0},{1,65},{65,1},{2,66},{66,2},{3,67},{67,3},{4,68},{68... | collective-permute-start | bytes 1216520 | tf_op jit(solution)/shard_map/ppermute | solution.py:31
  34.2 0.0 collective-permute-done.2.refs_3_
  34.2 0.0 copy-start.7
  34.2 1.9 %collective-permute-start.6 = (bf16[1584,128]{1,0:T(8,128)(2,1)S(1)}, bf16[1584,128]{1,0:T(8,128)(2,1)S(1)}, u32[]{:S(2)}, u32[]{:S(2)}) collective-permute-start(bf16[1584,128]{1,0:T(8,128)(2,1)S(1)} %collective-permute-done.2.refs_3_), channel_id=1, source_target_pairs={{0,64},{64,0},{1,65},{65,1},{2,66},{66,2},{3,67},{67,3},{4,68},{68... | collective-permute-start | bytes 1216520 | tf_op jit(solution)/shard_map/ppermute | solution.py:31
  36.1 0.0 copy-done.2
  36.1 3.4 %reach.1.pairs = s32[66]{0:T(128)S(1)} custom-call(s32[9]{0:T(128)S(1)} %stack.39.ids, s32[64]{0:T(128)S(1)} %copy-done.2), custom_call_target="tpu_custom_call" | custom-call | flops 60000002048 | bytes 1000 | tf_op jit(solution)/shard_map/reach/pallas_call | solution.py:77
  39.5 0.0 copy-done.1
  39.5 0.0 copy-done.5
  39.5 0.0 copy-done.6
  39.5 0.0 copy-done.7
  39.5 0.0 copy-start.3
  39.5 0.5 copy-done.3
  40.0 0.0 collective-permute-done.3.refs_4_
  40.0 0.0 copy-start.8
  40.0 0.0 collective-permute-done.6.refs_7_
  40.0 0.0 copy-start.11
  40.1 0.0 collective-permute-done.4.refs_5_
  40.1 0.0 copy-start.9
  40.1 0.0 collective-permute-done.5.refs_6_
  40.1 0.0 copy-start.10
  40.1 1.7 %all-to-all-done.refs_8_ = bf16[8,256,128]{2,1,0:T(8,128)(2,1)S(1)} async-done(((bf16[8,256,128]{2,1,0:T(8,128)(2,1)}), bf16[8,256,128]{2,1,0:T(8,128)(2,1)S(1)}, u32[]{:S(2)}, u32[]{:S(2)}) %all-to-all-start) | async-done | bytes 524320 | tf_op jit(solution)/shard_map/all_to_all | solution.py:313
  41.8 0.0 copy-done.8
  41.8 0.0 copy-done.11
  41.8 0.0 copy-done.9
  41.8 0.0 copy-done.10
  41.8 0.0 copy-start.4
  41.8 0.8 copy-done.4
  42.6 6.1 %attend.1 = (bf16[8,256,128]{2,1,0:T(8,128)(2,1)}, f32[4,128,768]{2,1,0:T(8,128)}, f32[4,128,768]{2,1,0:T(8,128)}) custom-call(s32[9]{0:T(128)} %copy-done.1, s32[66]{0:T(128)} %copy-done.3, bf16[1584,128]{1,0:T(8,128)(2,1)} %prepare.1.refs_0_, bf16[1584,128]{1,0:T(8,128)(2,1)} %copy-done.6, bf16[1584,128]{1,0:T(8,128)(2,1)} %copy-done.5, ...), custom_call_target="tpu_custom_call" | custom-call | flops 2000000000 | bytes 8000000 | tf_op jit(solution)/shard_map/attend/pallas_call | solution.py:201
  48.7 1.9 %collective-permute-start.7 = (f32[4,128,768]{2,1,0:T(8,128)}, f32[4,128,768]{2,1,0:T(8,128)S(1)}, u32[]{:S(2)}, u32[]{:S(2)}) collective-permute-start(f32[4,128,768]{2,1,0:T(8,128)} %get-tuple-element.26), channel_id=1, source_target_pairs={{0,64},{64,0},{1,65},{65,1},{2,66},{66,2},{3,67},{67,3},{4,68},{68... | collective-permute-start | bytes 4718600 | tf_op jit(solution)/shard_map/ppermute | solution.py:31
  50.6 8.0 %all-to-all-start.1 = ((bf16[8,256,128]{2,1,0:T(8,128)(2,1)}), bf16[8,256,128]{2,1,0:T(8,128)(2,1)S(1)}, u32[]{:S(2)}, u32[]{:S(2)}) async-start(bf16[8,256,128]{2,1,0:T(8,128)(2,1)} %get-tuple-element.24), calls=%async_computation.1 | async-start | bytes 1048576 | tf_op jit(solution)/shard_map/all_to_all | solution.py:320
  58.6 0.0 collective-permute-done.7.other
  58.6 0.0 copy-start
  58.6 1.4 %copy-done = f32[4,128,768]{2,1,0:T(8,128)S(1)} copy-done((f32[4,128,768]{2,1,0:T(8,128)S(1)}, f32[4,128,768]{2,1,0:T(8,128)}, u32[]{:S(2)}) %copy-start) | copy-done | bytes 1572888
  60.0 0.1 add_cores.1
  60.2 1.9 %collective-permute-start.8 = (bf16[128,768]{1,0:T(8,128)(2,1)S(1)}, bf16[128,768]{1,0:T(8,128)(2,1)S(1)}, u32[]{:S(2)}, u32[]{:S(2)}) collective-permute-start(bf16[128,768]{1,0:T(8,128)(2,1)S(1)} %get-tuple-element.29), channel_id=1, source_target_pairs={{0,16},{16,32},{32,48},{48,0},{1,17},{17,33},{33,49},{49,1},{2,18}... | collective-permute-start | bytes 589832 | tf_op jit(solution)/shard_map/ppermute | solution.py:31
  62.1 3.9 %collective-permute-start.9 = (bf16[128,768]{1,0:T(8,128)(2,1)S(1)}, bf16[128,768]{1,0:T(8,128)(2,1)S(1)}, u32[]{:S(2)}, u32[]{:S(2)}) collective-permute-start(bf16[128,768]{1,0:T(8,128)(2,1)S(1)} %get-tuple-element.30), channel_id=1, source_target_pairs={{0,48},{16,0},{32,16},{48,32},{1,49},{17,1},{33,17},{49,33},{2,50}... | collective-permute-start | bytes 589832 | tf_op jit(solution)/shard_map/ppermute | solution.py:31
  66.0 1.9 %collective-permute-start.10 = (bf16[128,768]{1,0:T(8,128)(2,1)S(1)}, bf16[128,768]{1,0:T(8,128)(2,1)S(1)}, u32[]{:S(2)}, u32[]{:S(2)}) collective-permute-start(bf16[128,768]{1,0:T(8,128)(2,1)S(1)} %get-tuple-element.31), channel_id=1, source_target_pairs={{0,32},{16,48},{32,0},{48,16},{1,33},{17,49},{33,1},{49,17},{2,34}... | collective-permute-start | bytes 589832 | tf_op jit(solution)/shard_map/ppermute | solution.py:31
  68.0 8.9 %all-to-all-done.1.parts = bf16[8,256,128]{2,1,0:T(8,128)(2,1)S(1)} async-done(((bf16[8,256,128]{2,1,0:T(8,128)(2,1)}), bf16[8,256,128]{2,1,0:T(8,128)(2,1)S(1)}, u32[]{:S(2)}, u32[]{:S(2)}) %all-to-all-start.1) | async-done | bytes 524320 | tf_op jit(solution)/shard_map/all_to_all | solution.py:320
  76.8 0.9 sum_rows.1
  77.7 10.3 %all-to-all-start.2 = ((bf16[8,256,128]{2,1,0:T(8,128)(2,1)}), bf16[8,256,128]{2,1,0:T(8,128)(2,1)S(1)}, u32[]{:S(2)}, u32[]{:S(2)}) async-start(bf16[8,256,128]{2,1,0:T(8,128)(2,1)} %sum_rows.1), calls=%async_computation.2 | async-start | bytes 1048576 | tf_op jit(solution)/shard_map/all_to_all | solution.py:324
  88.0 0.0 collective-permute-done.8.b
  88.0 0.0 collective-permute-done.9.c
  88.0 0.0 collective-permute-done.10.d
  88.0 0.9 finish_query.1
  88.9 16.8 %all-to-all-done.2.parts = bf16[8,256,128]{2,1,0:T(8,128)(2,1)S(1)} async-done(((bf16[8,256,128]{2,1,0:T(8,128)(2,1)}), bf16[8,256,128]{2,1,0:T(8,128)(2,1)S(1)}, u32[]{:S(2)}, u32[]{:S(2)}) %all-to-all-start.2) | async-done | bytes 524320 | tf_op jit(solution)/shard_map/all_to_all | solution.py:324
  105.7 0.9 split_heads.1
  (3 shorter events, 0.0 us)
Async XLA Ops:
  1.8 34.3 %copy-start.2 = (s32[64]{0:T(128)S(1)}, s32[64]{0:T(128)}, u32[]{:S(2)}) copy-start(s32[64]{0:T(128)} %parents.1) | copy-start | bytes 772
  4.0 22.2 %collective-permute-start.1 = (bf16[1584,128]{1,0:T(8,128)(2,1)}, bf16[1584,128]{1,0:T(8,128)(2,1)S(1)}, u32[]{:S(2)}, u32[]{:S(2)}) collective-permute-start(bf16[1584,128]{1,0:T(8,128)(2,1)} %prepare.1.refs_0_), channel_id=1, source_target_pairs={{0,16},{16,32},{32,48},{48,0},{1,17},{17,33},{33,49},{49,1},{2,18}... | collective-permute-start | bytes 1216520 | tf_op jit(solution)/shard_map/ppermute | solution.py:31
  11.8 18.1 %collective-permute-start = (bf16[1584,128]{1,0:T(8,128)(2,1)}, bf16[1584,128]{1,0:T(8,128)(2,1)S(1)}, u32[]{:S(2)}, u32[]{:S(2)}) collective-permute-start(bf16[1584,128]{1,0:T(8,128)(2,1)} %prepare.1.refs_0_), channel_id=1, source_target_pairs={{0,48},{16,0},{32,16},{48,32},{1,49},{17,1},{33,17},{49,33},{2,50}... | collective-permute-start | bytes 1216520 | tf_op jit(solution)/shard_map/ppermute | solution.py:31
  13.7 20.5 %collective-permute-start.2 = (bf16[1584,128]{1,0:T(8,128)(2,1)}, bf16[1584,128]{1,0:T(8,128)(2,1)S(1)}, u32[]{:S(2)}, u32[]{:S(2)}) collective-permute-start(bf16[1584,128]{1,0:T(8,128)(2,1)} %prepare.1.refs_0_), channel_id=1, source_target_pairs={{0,32},{16,48},{32,0},{48,16},{1,33},{17,49},{33,1},{49,17},{2,34}... | collective-permute-start | bytes 1216520 | tf_op jit(solution)/shard_map/ppermute | solution.py:31
  17.1 23.0 %collective-permute-start.3 = (bf16[1584,128]{1,0:T(8,128)(2,1)}, bf16[1584,128]{1,0:T(8,128)(2,1)S(1)}, u32[]{:S(2)}, u32[]{:S(2)}) collective-permute-start(bf16[1584,128]{1,0:T(8,128)(2,1)} %prepare.1.refs_0_), channel_id=1, source_target_pairs={{0,64},{64,0},{1,65},{65,1},{2,66},{66,2},{3,67},{67,3},{4,68},{68... | collective-permute-start | bytes 1216520 | tf_op jit(solution)/shard_map/ppermute | solution.py:31
  19.9 21.9 %all-to-all-start = ((bf16[8,256,128]{2,1,0:T(8,128)(2,1)}), bf16[8,256,128]{2,1,0:T(8,128)(2,1)S(1)}, u32[]{:S(2)}, u32[]{:S(2)}) async-start(bf16[8,256,128]{2,1,0:T(8,128)(2,1)} %broadcast_in_dim.2), calls=%async_computation | async-start | bytes 1048576 | tf_op jit(solution)/shard_map/all_to_all | solution.py:313
  23.5 16.0 %copy-start.1 = (s32[9]{0:T(128)}, s32[9]{0:T(128)S(1)}, u32[]{:S(2)}) copy-start(s32[9]{0:T(128)S(1)} %stack.39.ids) | copy-start | bytes 112
  26.2 13.3 %copy-start.5 = (bf16[1584,128]{1,0:T(8,128)(2,1)}, bf16[1584,128]{1,0:T(8,128)(2,1)S(1)}, u32[]{:S(2)}) copy-start(bf16[1584,128]{1,0:T(8,128)(2,1)S(1)} %collective-permute-done.1.refs_2_) | copy-start | bytes 1216516
  29.8 9.7 %copy-start.6 = (bf16[1584,128]{1,0:T(8,128)(2,1)}, bf16[1584,128]{1,0:T(8,128)(2,1)S(1)}, u32[]{:S(2)}) copy-start(bf16[1584,128]{1,0:T(8,128)(2,1)S(1)} %collective-permute-done.refs_1_) | copy-start | bytes 1216516
  29.8 10.2 %collective-permute-start.4 = (bf16[1584,128]{1,0:T(8,128)(2,1)S(1)}, bf16[1584,128]{1,0:T(8,128)(2,1)S(1)}, u32[]{:S(2)}, u32[]{:S(2)}) collective-permute-start(bf16[1584,128]{1,0:T(8,128)(2,1)S(1)} %collective-permute-done.refs_1_), channel_id=1, source_target_pairs={{0,64},{64,0},{1,65},{65,1},{2,66},{66,2},{3,67},{67,3},{4,68},{68... | collective-permute-start | bytes 1216520 | tf_op jit(solution)/shard_map/ppermute | solution.py:31
  31.7 8.3 %collective-permute-start.5 = (bf16[1584,128]{1,0:T(8,128)(2,1)S(1)}, bf16[1584,128]{1,0:T(8,128)(2,1)S(1)}, u32[]{:S(2)}, u32[]{:S(2)}) collective-permute-start(bf16[1584,128]{1,0:T(8,128)(2,1)S(1)} %collective-permute-done.1.refs_2_), channel_id=1, source_target_pairs={{0,64},{64,0},{1,65},{65,1},{2,66},{66,2},{3,67},{67,3},{4,68},{68... | collective-permute-start | bytes 1216520 | tf_op jit(solution)/shard_map/ppermute | solution.py:31
  34.2 5.3 %copy-start.7 = (bf16[1584,128]{1,0:T(8,128)(2,1)}, bf16[1584,128]{1,0:T(8,128)(2,1)S(1)}, u32[]{:S(2)}) copy-start(bf16[1584,128]{1,0:T(8,128)(2,1)S(1)} %collective-permute-done.2.refs_3_) | copy-start | bytes 1216516
  34.2 5.9 %collective-permute-start.6 = (bf16[1584,128]{1,0:T(8,128)(2,1)S(1)}, bf16[1584,128]{1,0:T(8,128)(2,1)S(1)}, u32[]{:S(2)}, u32[]{:S(2)}) collective-permute-start(bf16[1584,128]{1,0:T(8,128)(2,1)S(1)} %collective-permute-done.2.refs_3_), channel_id=1, source_target_pairs={{0,64},{64,0},{1,65},{65,1},{2,66},{66,2},{3,67},{67,3},{4,68},{68... | collective-permute-start | bytes 1216520 | tf_op jit(solution)/shard_map/ppermute | solution.py:31
  39.5 0.5 copy-start.3
  40.0 1.7 %copy-start.8 = (bf16[1584,128]{1,0:T(8,128)(2,1)}, bf16[1584,128]{1,0:T(8,128)(2,1)S(1)}, u32[]{:S(2)}) copy-start(bf16[1584,128]{1,0:T(8,128)(2,1)S(1)} %collective-permute-done.3.refs_4_) | copy-start | bytes 1216516
  40.0 1.7 %copy-start.11 = (bf16[1584,128]{1,0:T(8,128)(2,1)}, bf16[1584,128]{1,0:T(8,128)(2,1)S(1)}, u32[]{:S(2)}) copy-start(bf16[1584,128]{1,0:T(8,128)(2,1)S(1)} %collective-permute-done.6.refs_7_) | copy-start | bytes 1216516
  40.1 1.7 %copy-start.9 = (bf16[1584,128]{1,0:T(8,128)(2,1)}, bf16[1584,128]{1,0:T(8,128)(2,1)S(1)}, u32[]{:S(2)}) copy-start(bf16[1584,128]{1,0:T(8,128)(2,1)S(1)} %collective-permute-done.4.refs_5_) | copy-start | bytes 1216516
  40.1 1.7 %copy-start.10 = (bf16[1584,128]{1,0:T(8,128)(2,1)}, bf16[1584,128]{1,0:T(8,128)(2,1)S(1)}, u32[]{:S(2)}) copy-start(bf16[1584,128]{1,0:T(8,128)(2,1)S(1)} %collective-permute-done.5.refs_6_) | copy-start | bytes 1216516
  41.8 0.8 copy-start.4
  48.7 9.9 %collective-permute-start.7 = (f32[4,128,768]{2,1,0:T(8,128)}, f32[4,128,768]{2,1,0:T(8,128)S(1)}, u32[]{:S(2)}, u32[]{:S(2)}) collective-permute-start(f32[4,128,768]{2,1,0:T(8,128)} %get-tuple-element.26), channel_id=1, source_target_pairs={{0,64},{64,0},{1,65},{65,1},{2,66},{66,2},{3,67},{67,3},{4,68},{68... | collective-permute-start | bytes 4718600 | tf_op jit(solution)/shard_map/ppermute | solution.py:31
  50.6 26.2 %all-to-all-start.1 = ((bf16[8,256,128]{2,1,0:T(8,128)(2,1)}), bf16[8,256,128]{2,1,0:T(8,128)(2,1)S(1)}, u32[]{:S(2)}, u32[]{:S(2)}) async-start(bf16[8,256,128]{2,1,0:T(8,128)(2,1)} %get-tuple-element.24), calls=%async_computation.1 | async-start | bytes 1048576 | tf_op jit(solution)/shard_map/all_to_all | solution.py:320
  58.6 1.4 %copy-start = (f32[4,128,768]{2,1,0:T(8,128)S(1)}, f32[4,128,768]{2,1,0:T(8,128)}, u32[]{:S(2)}) copy-start(f32[4,128,768]{2,1,0:T(8,128)} %get-tuple-element.25.mine) | copy-start | bytes 4718596
  60.2 27.8 %collective-permute-start.8 = (bf16[128,768]{1,0:T(8,128)(2,1)S(1)}, bf16[128,768]{1,0:T(8,128)(2,1)S(1)}, u32[]{:S(2)}, u32[]{:S(2)}) collective-permute-start(bf16[128,768]{1,0:T(8,128)(2,1)S(1)} %get-tuple-element.29), channel_id=1, source_target_pairs={{0,16},{16,32},{32,48},{48,0},{1,17},{17,33},{33,49},{49,1},{2,18}... | collective-permute-start | bytes 589832 | tf_op jit(solution)/shard_map/ppermute | solution.py:31
  62.1 25.9 %collective-permute-start.9 = (bf16[128,768]{1,0:T(8,128)(2,1)S(1)}, bf16[128,768]{1,0:T(8,128)(2,1)S(1)}, u32[]{:S(2)}, u32[]{:S(2)}) collective-permute-start(bf16[128,768]{1,0:T(8,128)(2,1)S(1)} %get-tuple-element.30), channel_id=1, source_target_pairs={{0,48},{16,0},{32,16},{48,32},{1,49},{17,1},{33,17},{49,33},{2,50}... | collective-permute-start | bytes 589832 | tf_op jit(solution)/shard_map/ppermute | solution.py:31
  66.0 22.0 %collective-permute-start.10 = (bf16[128,768]{1,0:T(8,128)(2,1)S(1)}, bf16[128,768]{1,0:T(8,128)(2,1)S(1)}, u32[]{:S(2)}, u32[]{:S(2)}) collective-permute-start(bf16[128,768]{1,0:T(8,128)(2,1)S(1)} %get-tuple-element.31), channel_id=1, source_target_pairs={{0,32},{16,48},{32,0},{48,16},{1,33},{17,49},{33,1},{49,17},{2,34}... | collective-permute-start | bytes 589832 | tf_op jit(solution)/shard_map/ppermute | solution.py:31
  77.7 28.0 %all-to-all-start.2 = ((bf16[8,256,128]{2,1,0:T(8,128)(2,1)}), bf16[8,256,128]{2,1,0:T(8,128)(2,1)S(1)}, u32[]{:S(2)}, u32[]{:S(2)}) async-start(bf16[8,256,128]{2,1,0:T(8,128)(2,1)} %sum_rows.1), calls=%async_computation.2 | async-start | bytes 1048576 | tf_op jit(solution)/shard_map/all_to_all | solution.py:324

commit v5 on v4

--- a/solution.py
+++ b/solution.py
@@ -14,8 +14,8 @@
 NBLK = 64
 KVH = 8
 SIDES = 8
-DISTANCES = (0, 1, -1, 2)
-Y = ("yh", "yl")
+COLUMN = ("yh", "xh")
+SQUARE = ("xl", "yl")
 STAT_ROWS = 16
 PACK_ROWS = 2 * ROWS + 3 * STAT_ROWS
 DOTS = 8
@@ -26,9 +26,12 @@
 BF16 = jnp.bfloat16
 
 
-def shift(block, axis, distance):
-    size = lax.axis_size(axis)
-    return lax.ppermute(block, axis, [(i, (i + distance) % size) for i in range(size)])
+def swap_cores(block):
+    return lax.ppermute(block, "core", [(0, 1), (1, 0)])
+
+
+def exchange(block, flip):
+    return lax.ppermute(block, SQUARE, [(i, i ^ flip) for i in range(4)])
 
 
 def room(mebibytes):
@@ -56,27 +59,29 @@
         high[block] = jnp.where(root, 0, high[above]) | jnp.where(block < 32, 0, bit)
         return carry
 
-    lax.fori_loop(0, NBLK, step, 0)
+    lax.fori_loop(0, NBLK, step, 0, unroll=True)
     first = ids[SIDES]
 
     def look(k, count):
-        side, j = k // 8, k % 8
-        block = first + 16 * (j // 2) + j % 2
+        side, j = (k // 8 + 4) % SIDES, k % 8
+        block = first + 16 * (j // 2) + 4 * (j % 2)
         mine = ids[side]
         word = jnp.where(block < 32, low[mine], high[mine])
         take = ((jnp.right_shift(word, block % 32) & 1) == 1) & (block != mine)
-        pairs[1 + count] = k
+        pairs[2 + count] = 8 * side + j
         return count + take.astype(jnp.int32)
 
-    count = lax.fori_loop(0, SIDES * 8, look, 0)
-    pairs[0] = count
-    pairs[1 + count] = 0
+    others = lax.fori_loop(0, SIDES * 4, look, 0, unroll=True)
+    count = lax.fori_loop(SIDES * 4, SIDES * 8, look, others, unroll=True)
+    pairs[0] = others
+    pairs[1] = count - others
+    pairs[2 + count] = 0
 
 
 def reach(ids, parents):
     return pl.pallas_call(
         reach_kernel,
-        out_shape=jax.ShapeDtypeStruct((SIDES * 8 + 2,), jnp.int32),
+        out_shape=jax.ShapeDtypeStruct((SIDES * 8 + 3,), jnp.int32),
         in_specs=smem(2),
         out_specs=smem(1)[0],
         scratch_shapes=[pltpu.SMEM((NBLK,), jnp.int32)] * 2,
@@ -86,8 +91,16 @@
     )(ids, parents)
 
 
-def prepare_kernel(q_hbm, do_hbm, o_hbm, ln_hbm, pack_ref, q_ref, do_ref, o_ref, ln_ref, stat, sems):
-    routes = ((do_hbm, do_ref), (o_hbm, o_ref), (ln_hbm, ln_ref), (q_hbm, q_ref))
+def prepare_kernel(head, q_hbm, do_hbm, o_hbm, ln_hbm, k_hbm, v_hbm, pack_ref, kv_ref, *scratch):
+    q_ref, do_ref, o_ref, ln_ref, k_ref, v_ref, stat, heads, sems = scratch
+    routes = (
+        (do_hbm, do_ref),
+        (o_hbm, o_ref),
+        (ln_hbm, ln_ref),
+        (q_hbm, q_ref),
+        (k_hbm, k_ref),
+        (v_hbm, v_ref),
+    )
     copies = [pltpu.make_async_copy(src, dst, sems.at[i]) for i, (src, dst) in enumerate(routes)]
     for copy in copies:
         copy.start()
@@ -106,20 +119,30 @@
         start = 2 * ROWS + part * STAT_ROWS
         pack_ref[start : start + STAT_ROWS] = high
         rest = rest - high.astype(F32)
-
-
-def prepare(queries, out_grad, outputs, log_norm):
+    for i, ref in enumerate((k_ref, v_ref)):
+        heads[...] = jnp.swapaxes(ref[...].astype(F32), 0, 1)
+        one = heads[head[0]].astype(BF16)
+        for j in range(8):
+            kv_ref[j, i * BLK : (i + 1) * BLK] = one
+
+
+def prepare(head, queries, out_grad, outputs, log_norm, keys, values):
     return pl.pallas_call(
         prepare_kernel,
-        out_shape=jax.ShapeDtypeStruct((PACK_ROWS, HD), BF16),
-        in_specs=anywhere(4),
-        out_specs=vmem(1)[0],
+        out_shape=(
+            jax.ShapeDtypeStruct((PACK_ROWS, HD), BF16),
+            jax.ShapeDtypeStruct((8, 2 * BLK, HD), BF16),
+        ),
+        in_specs=smem(1) + anywhere(6),
+        out_specs=tuple(vmem(2)),
         scratch_shapes=[pltpu.VMEM((HEADS, BLK, HD), BF16)] * 3
-        + [pltpu.VMEM((HEADS, BLK), F32), pltpu.VMEM((STAT_ROWS, BLK), F32), pltpu.SemaphoreType.DMA((4,))],
+        + [pltpu.VMEM((HEADS, BLK), F32)]
+        + [pltpu.VMEM((BLK, KVH, HD), BF16)] * 2
+        + [pltpu.VMEM((STAT_ROWS, BLK), F32), pltpu.VMEM((KVH, BLK, HD), F32), pltpu.SemaphoreType.DMA((6,))],
         cost_estimate=pl.CostEstimate(flops=4_000_000, bytes_accessed=1_000_000, transcendentals=0),
         compiler_params=room(60),
         name="prepare",
-    )(queries, out_grad, outputs, log_norm)
+    )(head, queries, out_grad, outputs, log_norm, keys, values)
 
 
 NT = (((1,), (1,)), ((), ()))
@@ -148,6 +171,7 @@
             for side, _, _ in work
         ]
         norms = [jnp.concatenate([r[h : h + 1] for h in range(HEADS)], 1) * LOG2E for r in rows]
+        norms = [n if use is None else jnp.where(use, n, jnp.inf) for n, (_, _, use) in zip(norms, work, strict=True)]
         dots = [jnp.concatenate([r[DOTS + h : DOTS + h + 1] for h in range(HEADS)], 1) for r in rows]
         probs = [
             jnp.exp2(mm(col[j, 0:BLK], packs[side, 0:ROWS], NT) * (SCALING * LOG2E) - norm)
@@ -158,7 +182,6 @@
             token = lax.broadcasted_iota(jnp.int32, (BLK, ROWS), 1) % BLK
             place = lax.broadcasted_iota(jnp.int32, (BLK, ROWS), 0)
             probs = [jnp.where(token >= place, p, 0.0) for p in probs]
-        probs = [p if use is None else jnp.where(use, p, 0.0) for p, (_, _, use) in zip(probs, work, strict=True)]
         dscores = [(p * (d - dot) * SCALING).astype(BF16) for p, d, dot in zip(probs, dprobs, dots, strict=True)]
         dv = [mm(p.astype(BF16), packs[side, ROWS : 2 * ROWS], NN) for p, (side, _, _) in zip(probs, work, strict=True)]
         dk = [mm(d, packs[side, 0:ROWS], NN) for d, (side, _, _) in zip(dscores, work, strict=True)]
@@ -171,29 +194,31 @@
     own = ids[0]
     copies[SIDES].wait()
     copies[0].wait()
-    visit([(0, 2 * (own // 16) + own % 2, None)], diagonal=True)
+    visit([(0, 2 * (own // 16) + own // 4 % 2, None)], diagonal=True)
     for copy in copies[1:SIDES]:
         copy.wait()
 
-    def step(i, carry):
-        work = []
-        for k in range(PER_STEP):
-            at = PER_STEP * i + k
-            code = pairs[1 + jnp.minimum(at, SIDES * 8)]
-            work.append((code // 8, code % 8, (at < pairs[0]) if k else None))
-        visit(work)
-        return carry
-
-    lax.fori_loop(0, (pairs[0] + PER_STEP - 1) // PER_STEP, step, 0)
+    def visit_all(start, count):
+        def step(i, carry):
+            work = []
+            for k in range(PER_STEP):
+                at = PER_STEP * i + k
+                code = pairs[start + jnp.minimum(at, count)]
+                work.append((code // 8, code % 8, (at < count) if k else None))
+            visit(work)
+            return carry
+
+        lax.fori_loop(0, (count + PER_STEP - 1) // PER_STEP, step, 0)
+
+    visit_all(2, pairs[0])
+    sent = pltpu.make_async_copy(both.at[4:8], other, outs.at[1])
+    sent.start()
+    visit_all(2 + pairs[0], pairs[1])
     low[...] = sums[...].astype(BF16)
-    copies = [
-        pltpu.make_async_copy(low, part, outs.at[0]),
-        pltpu.make_async_copy(both.at[4:8], other, outs.at[1]),
-        pltpu.make_async_copy(both.at[0:4], mine, outs.at[2]),
-    ]
+    copies = [pltpu.make_async_copy(low, part, outs.at[0]), pltpu.make_async_copy(both.at[0:4], mine, outs.at[2])]
     for copy in copies:
         copy.start()
-    for copy in copies:
+    for copy in [sent, *copies]:
         copy.wait()
 
 
@@ -296,30 +321,27 @@
 
 
 def body(queries, keys, values, outputs, out_grad, log_norm, parents):
-    yh, core, x, yl, z = (lax.axis_index(a) for a in ("yh", "core", "x", "yl", "z"))
-    kv = jnp.concatenate(
-        [lax.dynamic_index_in_dim(keys, z, 1, False), lax.dynamic_index_in_dim(values, z, 1, False)], 0
-    )
+    yh, core, xh, xl, yl, z = (lax.axis_index(a) for a in ("yh", "core", "xh", "xl", "yl", "z"))
+    place = 2 * xl + yl
     ids = [
-        16 * yh + 8 * (core if side < 4 else 1 - core) + 2 * ((x + DISTANCES[side % 4]) % 4) + yl
+        16 * yh + 8 * (core if side < 4 else 1 - core) + 4 * xh + jnp.bitwise_xor(place, side % 4)
         for side in range(SIDES)
     ]
-    ids = jnp.stack([*ids, 8 * core + 2 * x]).astype(jnp.int32)
+    ids = jnp.stack([*ids, 8 * core + place]).astype(jnp.int32)
 
     queries, out_grad, outputs = (jnp.swapaxes(a, 0, 1) for a in (queries, out_grad, outputs))
-    pack = prepare(queries, out_grad, outputs, log_norm)
-    pack, kv = lax.optimization_barrier((pack, kv))
-    near = [shift(pack, "x", -d) for d in DISTANCES[1:]]
-    col = lax.all_to_all(jnp.broadcast_to(kv[None], (8, 2 * BLK, HD)), Y, 0, 0)
-    swapped = [shift(pack, "core", 1)]
-    ids, near[0], near[1] = lax.optimization_barrier((ids, near[0], near[1]))
+    head = jnp.reshape(z, (1,)).astype(jnp.int32)
+    pack, kv = prepare(head, queries, out_grad, outputs, log_norm, keys, values)
+    near = [exchange(pack, flip) for flip in (1, 2, 3)]
+    col = lax.all_to_all(kv, COLUMN, 0, 0)
+    ids, near[0], near[1], again = lax.optimization_barrier((ids, near[0], near[1], pack))
     pairs = reach(ids, parents)
-    swapped += [shift(p, "core", 1) for p in near]
+    swapped = [swap_cores(p) for p in [again, *near]]
     packs = [pack, *near, *swapped]
     part, mine, other = attend(ids, pairs, packs, col)
-    row = lax.all_to_all(part, Y, 0, 0)
-    keep, *sends = add_cores(mine, shift(other, "core", 1))
-    got = [shift(g, "x", d) for g, d in zip(sends, DISTANCES[1:], strict=True)]
+    row = lax.all_to_all(part, COLUMN, 0, 0)
+    keep, *sends = add_cores(mine, swap_cores(other))
+    got = [exchange(send, flip) for flip, send in enumerate(sends, 1)]
     row, keep = lax.optimization_barrier((row, keep))
     heads = lax.all_to_all(sum_rows(row), "z", 0, 0)
     query_grad = finish_query([keep, *got])
@@ -328,8 +350,8 @@
 
 
 def solution(mesh):
-    fine = Mesh(mesh.devices.reshape(4, 2, 4, 2, 8), ("yh", "core", "x", "yl", "z"))
-    tokens = ("yh", "core", "x", "yl")
+    fine = Mesh(mesh.devices.reshape(4, 2, 2, 2, 2, 8), ("yh", "core", "xh", "xl", "yl", "z"))
+    tokens = ("yh", "core", "xh", "xl", "yl")
     in_specs = (
         P(tokens, "z", None),
         P(tokens, None, None),

time: 108 us -> 110 us (1.019)
  starting transfers between devices: 52.7 us -> 57.3 us
  waiting for transfers between devices: 33.7 us -> 30.3 us
  local copies, waits for them, and re-layouts: 4.9 us -> 2.83 us
  Pallas kernels: 14.4 us -> 16.4 us
    all_to_all x2, starting transfers between devices: 11.5 us -> 18.4 us  [the longest x1 10.1 us: body(): col = lax.all_to_all(kv, COLUMN, 0, 0)]
    pallas_call x1, Pallas kernels: 6.11 us -> 9.29 us  [attend(): pl.pallas_call(attend_kernel, out_shape=(jax.ShapeDtypeStruct((8, 2 * BLK...]
    ppermute x11, starting transfers between devices: 30.9 us -> 28.5 us  [the longest x6 18.4 us: exchange(): return lax.ppermute(block, SQUARE, [(i, i ^ flip) for i in range(4)])]
    ppermute x11, waiting for transfers between devices: 6.31 us -> 4.39 us  [the longest x6 4.37 us: exchange(): return lax.ppermute(block, SQUARE, [(i, i ^ flip) for i in range(4)])]
    all_to_all x1, waiting for transfers between devices: 16.8 us -> 15 us  [body(): heads = lax.all_to_all(sum_rows(row), 'z', 0, 0)]
    pallas_call x1, Pallas kernels: 3.36 us -> 1.71 us  [reach(): pl.pallas_call(reach_kernel, out_shape=jax.ShapeDtypeStruct((SIDES * 8 +...]
    dynamic_slice x1 -> x0, local copies, waits for them, and re-layouts: 1.17 us -> none  [body(): lax.dynamic_index_in_dim(values, z, 1, False)]
    unnamed x26 -> x24, local copies, waits for them, and re-layouts: 2.76 us -> 2.75 us
  transfers between devices with their start and end apart: 14 -> 14, of which waited for: 5 -> 4; matrix products, arithmetic and copies ran while one was open for 1% -> 0% of each run, Pallas kernels for 5% -> 3%
where the time goes in v5:
time: 110 us; the launch traced here: 108 us
  starting transfers between devices  57.3 us (52%)
  waiting for transfers between devices  30.3 us (28%)
  Pallas kernels  16.4 us (15%)
  local copies, waits for them, and re-layouts  2.83 us (3%)
    ppermute x6, starting transfers between devices, exchange(): return lax.ppermute(block, SQUARE, [(i, i ^ flip) for i in range(4)])  18.4 us
    all_to_all x1, waiting for transfers between devices, body(): heads = lax.all_to_all(sum_rows(row), 'z', 0, 0)  15 us
    all_to_all x1, starting transfers between devices, body(): heads = lax.all_to_all(sum_rows(row), 'z', 0, 0)  10.4 us
    ppermute x5, starting transfers between devices, swap_cores(): return lax.ppermute(block, 'core', [(0, 1), (1, 0)])  10.1 us
    all_to_all x1, starting transfers between devices, body(): col = lax.all_to_all(kv, COLUMN, 0, 0)  10.1 us
    pallas_call x1, Pallas kernels, attend(): pl.pallas_call(attend_kernel, out_shape=(jax.ShapeDtypeStruct((8, 2 * BLK...  9.29 us
    all_to_all x1, starting transfers between devices, body(): row = lax.all_to_all(part, COLUMN, 0, 0)  8.35 us
    all_to_all x1, waiting for transfers between devices, body(): row = lax.all_to_all(part, COLUMN, 0, 0)  5.91 us
  transfers between devices with their start and end apart: 14, of which 4 were waited for; matrix products, arithmetic and copies ran while one was open for 0% of the time, Pallas kernels for 3%

profile of v5, /device:TPU:6, one launch (start us, length us, event | category | flops | bytes accessed | tf_op | source)
XLA Modules:
  0.0 107.8 jit_solution(16010668892987541664)
XLA Ops:
  0.6 0.0 copy-start.2
  0.6 2.6 %prepare.1 = (bf16[1584,128]{1,0:T(8,128)(2,1)}, bf16[8,256,128]{2,1,0:T(8,128)(2,1)}) custom-call(s32[1]{0:T(128)} %bitcast.9.head, bf16[6,128,128]{2,1,0:T(8,128)(2,1)} %bitcast.14, bf16[6,128,128]{2,1,0:T(8,128)(2,1)} %bitcast.15, bf16[6,128,128]{2,1,0:T(8,128)(2,1)} %bitcast.16, f32[6,128]{1,0:T(8,128)} %ln_hbm.1, bf16[128,8,128]{2,1,0:T(8,128)(2,1)} %k_hbm.1, ...), custom_call_target="tpu_custom_call" | custom-call | flops 4000000 | bytes 1000000 | tf_op jit(solution)/shard_map/prepare/pallas_call | solution.py:130
  3.3 2.7 %collective-permute-start.1 = (bf16[1584,128]{1,0:T(8,128)(2,1)}, bf16[1584,128]{1,0:T(8,128)(2,1)S(1)}, u32[]{:S(2)}, u32[]{:S(2)}) collective-permute-start(bf16[1584,128]{1,0:T(8,128)(2,1)} %get-tuple-element.24.refs_0_), channel_id=1, source_target_pairs={{0,16},{8,24},{16,0},{24,8},{1,17},{9,25},{17,1},{25,9},{2,18},{10... | collective-permute-start | bytes 1216520 | tf_op jit(solution)/shard_map/ppermute | solution.py:34
  6.0 3.5 %collective-permute-start = (bf16[1584,128]{1,0:T(8,128)(2,1)}, bf16[1584,128]{1,0:T(8,128)(2,1)S(1)}, u32[]{:S(2)}, u32[]{:S(2)}) collective-permute-start(bf16[1584,128]{1,0:T(8,128)(2,1)} %get-tuple-element.24.refs_0_), channel_id=1, source_target_pairs={{0,8},{8,0},{16,24},{24,16},{1,9},{9,1},{17,25},{25,17},{2,10},{10... | collective-permute-start | bytes 1216520 | tf_op jit(solution)/shard_map/ppermute | solution.py:34
  9.5 3.0 %collective-permute-start.2 = (bf16[1584,128]{1,0:T(8,128)(2,1)}, bf16[1584,128]{1,0:T(8,128)(2,1)S(1)}, u32[]{:S(2)}, u32[]{:S(2)}) collective-permute-start(bf16[1584,128]{1,0:T(8,128)(2,1)} %get-tuple-element.24.refs_0_), channel_id=1, source_target_pairs={{0,24},{8,16},{16,8},{24,0},{1,25},{9,17},{17,9},{25,1},{2,26},{10... | collective-permute-start | bytes 1216520 | tf_op jit(solution)/shard_map/ppermute | solution.py:34
  12.5 10.1 %all-to-all-start = ((bf16[8,256,128]{2,1,0:T(8,128)(2,1)}), bf16[8,256,128]{2,1,0:T(8,128)(2,1)S(1)}, u32[]{:S(2)}, u32[]{:S(2)}) async-start(bf16[8,256,128]{2,1,0:T(8,128)(2,1)} %get-tuple-element.25), calls=%async_computation | async-start | bytes 1048576 | tf_op jit(solution)/shard_map/all_to_all | solution.py:336
  22.6 0.1 stack.39.ids
  22.7 0.0 copy-start.1
  22.7 0.0 collective-permute-done.1.refs_2_
  22.7 0.0 copy-start.5
  22.7 0.0 collective-permute-done.refs_1_
  22.7 0.0 copy-start.6
  22.7 1.9 %collective-permute-start.3 = (bf16[1584,128]{1,0:T(8,128)(2,1)}, bf16[1584,128]{1,0:T(8,128)(2,1)S(1)}, u32[]{:S(2)}, u32[]{:S(2)}) collective-permute-start(bf16[1584,128]{1,0:T(8,128)(2,1)} %get-tuple-element.24.refs_0_), channel_id=1, source_target_pairs={{0,64},{64,0},{1,65},{65,1},{2,66},{66,2},{3,67},{67,3},{4,68},{68... | collective-permute-start | bytes 1216520 | tf_op jit(solution)/shard_map/ppermute | solution.py:30
  24.6 2.4 %collective-permute-start.4 = (bf16[1584,128]{1,0:T(8,128)(2,1)S(1)}, bf16[1584,128]{1,0:T(8,128)(2,1)S(1)}, u32[]{:S(2)}, u32[]{:S(2)}) collective-permute-start(bf16[1584,128]{1,0:T(8,128)(2,1)S(1)} %collective-permute-done.refs_1_), channel_id=1, source_target_pairs={{0,64},{64,0},{1,65},{65,1},{2,66},{66,2},{3,67},{67,3},{4,68},{68... | collective-permute-start | bytes 1216520 | tf_op jit(solution)/shard_map/ppermute | solution.py:30
  27.0 1.9 %collective-permute-start.5 = (bf16[1584,128]{1,0:T(8,128)(2,1)S(1)}, bf16[1584,128]{1,0:T(8,128)(2,1)S(1)}, u32[]{:S(2)}, u32[]{:S(2)}) collective-permute-start(bf16[1584,128]{1,0:T(8,128)(2,1)S(1)} %collective-permute-done.1.refs_2_), channel_id=1, source_target_pairs={{0,64},{64,0},{1,65},{65,1},{2,66},{66,2},{3,67},{67,3},{4,68},{68... | collective-permute-start | bytes 1216520 | tf_op jit(solution)/shard_map/ppermute | solution.py:30
  29.0 4.4 %collective-permute-done.2.refs_3_ = bf16[1584,128]{1,0:T(8,128)(2,1)S(1)} collective-permute-done((bf16[1584,128]{1,0:T(8,128)(2,1)}, bf16[1584,128]{1,0:T(8,128)(2,1)S(1)}, u32[]{:S(2)}, u32[]{:S(2)}) %collective-permute-start.2) | collective-permute-done | bytes 405536 | tf_op jit(solution)/shard_map/ppermute | solution.py:34
  33.3 0.0 copy-start.7
  33.3 1.9 %collective-permute-start.6 = (bf16[1584,128]{1,0:T(8,128)(2,1)S(1)}, bf16[1584,128]{1,0:T(8,128)(2,1)S(1)}, u32[]{:S(2)}, u32[]{:S(2)}) collective-permute-start(bf16[1584,128]{1,0:T(8,128)(2,1)S(1)} %collective-permute-done.2.refs_3_), channel_id=1, source_target_pairs={{0,64},{64,0},{1,65},{65,1},{2,66},{66,2},{3,67},{67,3},{4,68},{68... | collective-permute-start | bytes 1216520 | tf_op jit(solution)/shard_map/ppermute | solution.py:30
  35.3 0.0 copy-done.2
  35.3 1.7 %reach.1.pairs = s32[67]{0:T(128)S(1)} custom-call(s32[9]{0:T(128)S(1)} %stack.39.ids, s32[64]{0:T(128)S(1)} %copy-done.2), custom_call_target="tpu_custom_call" | custom-call | flops 60000002048 | bytes 1000 | tf_op jit(solution)/shard_map/reach/pallas_call | solution.py:82
  37.0 0.0 copy-done.1
  37.0 0.0 copy-done.5
  37.0 0.0 copy-done.6
  37.0 0.0 copy-done.7
  37.0 0.0 copy-start.3
  37.0 0.5 copy-done.3
  37.5 0.0 collective-permute-done.6.refs_7_
  37.5 0.0 copy-start.11
  37.5 0.0 collective-permute-done.3.refs_4_
  37.5 0.0 copy-start.8
  37.6 0.0 collective-permute-done.4.refs_5_
  37.6 0.0 copy-start.9
  37.6 0.0 collective-permute-done.5.refs_6_
  37.6 0.0 copy-start.10
  37.6 5.1 %all-to-all-done.refs_8_ = bf16[8,256,128]{2,1,0:T(8,128)(2,1)S(1)} async-done(((bf16[8,256,128]{2,1,0:T(8,128)(2,1)}), bf16[8,256,128]{2,1,0:T(8,128)(2,1)S(1)}, u32[]{:S(2)}, u32[]{:S(2)}) %all-to-all-start) | async-done | bytes 524320 | tf_op jit(solution)/shard_map/all_to_all | solution.py:336
  42.7 0.0 copy-done.11
  42.7 0.0 copy-done.8
  42.7 0.0 copy-done.9
  42.7 0.0 copy-done.10
  42.7 0.0 copy-start.4
  42.7 0.8 copy-done.4
  43.5 9.3 %attend.1 = (bf16[8,256,128]{2,1,0:T(8,128)(2,1)}, f32[4,128,768]{2,1,0:T(8,128)}, f32[4,128,768]{2,1,0:T(8,128)}) custom-call(s32[9]{0:T(128)} %copy-done.1, s32[67]{0:T(128)} %copy-done.3, bf16[1584,128]{1,0:T(8,128)(2,1)} %get-tuple-element.24.refs_0_, bf16[1584,128]{1,0:T(8,128)(2,1)} %copy-done.6, bf16[1584,128]{1,0:T(8,128)(2,1)} %copy-done.5, ...), custom_call_target="tpu_custom_call" | custom-call | flops 2000000000 | bytes 8000000 | tf_op jit(solution)/shard_map/attend/pallas_call | solution.py:226
  52.8 1.9 %collective-permute-start.7 = (f32[4,128,768]{2,1,0:T(8,128)}, f32[4,128,768]{2,1,0:T(8,128)S(1)}, u32[]{:S(2)}, u32[]{:S(2)}) collective-permute-start(f32[4,128,768]{2,1,0:T(8,128)} %get-tuple-element.28), channel_id=1, source_target_pairs={{0,64},{64,0},{1,65},{65,1},{2,66},{66,2},{3,67},{67,3},{4,68},{68... | collective-permute-start | bytes 4718600 | tf_op jit(solution)/shard_map/ppermute | solution.py:30
  54.7 8.4 %all-to-all-start.1 = ((bf16[8,256,128]{2,1,0:T(8,128)(2,1)}), bf16[8,256,128]{2,1,0:T(8,128)(2,1)S(1)}, u32[]{:S(2)}, u32[]{:S(2)}) async-start(bf16[8,256,128]{2,1,0:T(8,128)(2,1)} %get-tuple-element.26), calls=%async_computation.1 | async-start | bytes 1048576 | tf_op jit(solution)/shard_map/all_to_all | solution.py:342
  63.1 0.0 collective-permute-done.7.other
  63.1 0.0 copy-start
  63.1 1.4 %copy-done = f32[4,128,768]{2,1,0:T(8,128)S(1)} copy-done((f32[4,128,768]{2,1,0:T(8,128)S(1)}, f32[4,128,768]{2,1,0:T(8,128)}, u32[]{:S(2)}) %copy-start) | copy-done | bytes 1572888
  64.5 0.1 add_cores.1
  64.6 1.9 %collective-permute-start.8 = (bf16[128,768]{1,0:T(8,128)(2,1)S(1)}, bf16[128,768]{1,0:T(8,128)(2,1)S(1)}, u32[]{:S(2)}, u32[]{:S(2)}) collective-permute-start(bf16[128,768]{1,0:T(8,128)(2,1)S(1)} %get-tuple-element.31), channel_id=1, source_target_pairs={{0,8},{8,0},{16,24},{24,16},{1,9},{9,1},{17,25},{25,17},{2,10},{10... | collective-permute-start | bytes 589832 | tf_op jit(solution)/shard_map/ppermute | solution.py:34
  66.6 1.9 %collective-permute-start.9 = (bf16[128,768]{1,0:T(8,128)(2,1)S(1)}, bf16[128,768]{1,0:T(8,128)(2,1)S(1)}, u32[]{:S(2)}, u32[]{:S(2)}) collective-permute-start(bf16[128,768]{1,0:T(8,128)(2,1)S(1)} %get-tuple-element.32), channel_id=1, source_target_pairs={{0,16},{8,24},{16,0},{24,8},{1,17},{9,25},{17,1},{25,9},{2,18},{10... | collective-permute-start | bytes 589832 | tf_op jit(solution)/shard_map/ppermute | solution.py:34
  68.5 5.4 %collective-permute-start.10 = (bf16[128,768]{1,0:T(8,128)(2,1)S(1)}, bf16[128,768]{1,0:T(8,128)(2,1)S(1)}, u32[]{:S(2)}, u32[]{:S(2)}) collective-permute-start(bf16[128,768]{1,0:T(8,128)(2,1)S(1)} %get-tuple-element.33), channel_id=1, source_target_pairs={{0,24},{8,16},{16,8},{24,0},{1,25},{9,17},{17,9},{25,1},{2,26},{10... | collective-permute-start | bytes 589832 | tf_op jit(solution)/shard_map/ppermute | solution.py:34
  73.9 5.9 %all-to-all-done.1.parts = bf16[8,256,128]{2,1,0:T(8,128)(2,1)S(1)} async-done(((bf16[8,256,128]{2,1,0:T(8,128)(2,1)}), bf16[8,256,128]{2,1,0:T(8,128)(2,1)S(1)}, u32[]{:S(2)}, u32[]{:S(2)}) %all-to-all-start.1) | async-done | bytes 524320 | tf_op jit(solution)/shard_map/all_to_all | solution.py:342
  79.8 0.9 sum_rows.1
  80.7 10.4 %all-to-all-start.2 = ((bf16[8,256,128]{2,1,0:T(8,128)(2,1)}), bf16[8,256,128]{2,1,0:T(8,128)(2,1)S(1)}, u32[]{:S(2)}, u32[]{:S(2)}) async-start(bf16[8,256,128]{2,1,0:T(8,128)(2,1)} %sum_rows.1), calls=%async_computation.2 | async-start | bytes 1048576 | tf_op jit(solution)/shard_map/all_to_all | solution.py:346
  91.0 0.0 collective-permute-done.8.b
  91.0 0.0 collective-permute-done.9.c
  91.0 0.0 collective-permute-done.10.d
  91.1 0.9 finish_query.1
  91.9 15.0 %all-to-all-done.2.parts = bf16[8,256,128]{2,1,0:T(8,128)(2,1)S(1)} async-done(((bf16[8,256,128]{2,1,0:T(8,128)(2,1)}), bf16[8,256,128]{2,1,0:T(8,128)(2,1)S(1)}, u32[]{:S(2)}, u32[]{:S(2)}) %all-to-all-start.2) | async-done | bytes 524320 | tf_op jit(solution)/shard_map/all_to_all | solution.py:346
  106.9 0.9 split_heads.1
Async XLA Ops:
  0.6 34.6 %copy-start.2 = (s32[64]{0:T(128)S(1)}, s32[64]{0:T(128)}, u32[]{:S(2)}) copy-start(s32[64]{0:T(128)} %parents.1) | copy-start | bytes 772
  3.3 19.4 %collective-permute-start.1 = (bf16[1584,128]{1,0:T(8,128)(2,1)}, bf16[1584,128]{1,0:T(8,128)(2,1)S(1)}, u32[]{:S(2)}, u32[]{:S(2)}) collective-permute-start(bf16[1584,128]{1,0:T(8,128)(2,1)} %get-tuple-element.24.refs_0_), channel_id=1, source_target_pairs={{0,16},{8,24},{16,0},{24,8},{1,17},{9,25},{17,1},{25,9},{2,18},{10... | collective-permute-start | bytes 1216520 | tf_op jit(solution)/shard_map/ppermute | solution.py:34
  6.0 16.7 %collective-permute-start = (bf16[1584,128]{1,0:T(8,128)(2,1)}, bf16[1584,128]{1,0:T(8,128)(2,1)S(1)}, u32[]{:S(2)}, u32[]{:S(2)}) collective-permute-start(bf16[1584,128]{1,0:T(8,128)(2,1)} %get-tuple-element.24.refs_0_), channel_id=1, source_target_pairs={{0,8},{8,0},{16,24},{24,16},{1,9},{9,1},{17,25},{25,17},{2,10},{10... | collective-permute-start | bytes 1216520 | tf_op jit(solution)/shard_map/ppermute | solution.py:34
  9.5 23.8 %collective-permute-start.2 = (bf16[1584,128]{1,0:T(8,128)(2,1)}, bf16[1584,128]{1,0:T(8,128)(2,1)S(1)}, u32[]{:S(2)}, u32[]{:S(2)}) collective-permute-start(bf16[1584,128]{1,0:T(8,128)(2,1)} %get-tuple-element.24.refs_0_), channel_id=1, source_target_pairs={{0,24},{8,16},{16,8},{24,0},{1,25},{9,17},{17,9},{25,1},{2,26},{10... | collective-permute-start | bytes 1216520 | tf_op jit(solution)/shard_map/ppermute | solution.py:34
  12.5 30.1 %all-to-all-start = ((bf16[8,256,128]{2,1,0:T(8,128)(2,1)}), bf16[8,256,128]{2,1,0:T(8,128)(2,1)S(1)}, u32[]{:S(2)}, u32[]{:S(2)}) async-start(bf16[8,256,128]{2,1,0:T(8,128)(2,1)} %get-tuple-element.25), calls=%async_computation | async-start | bytes 1048576 | tf_op jit(solution)/shard_map/all_to_all | solution.py:336
  22.7 14.3 %copy-start.1 = (s32[9]{0:T(128)}, s32[9]{0:T(128)S(1)}, u32[]{:S(2)}) copy-start(s32[9]{0:T(128)S(1)} %stack.39.ids) | copy-start | bytes 112
  22.7 14.3 %copy-start.5 = (bf16[1584,128]{1,0:T(8,128)(2,1)}, bf16[1584,128]{1,0:T(8,128)(2,1)S(1)}, u32[]{:S(2)}) copy-start(bf16[1584,128]{1,0:T(8,128)(2,1)S(1)} %collective-permute-done.1.refs_2_) | copy-start | bytes 1216516
  22.7 14.3 %copy-start.6 = (bf16[1584,128]{1,0:T(8,128)(2,1)}, bf16[1584,128]{1,0:T(8,128)(2,1)S(1)}, u32[]{:S(2)}) copy-start(bf16[1584,128]{1,0:T(8,128)(2,1)S(1)} %collective-permute-done.refs_1_) | copy-start | bytes 1216516
  22.7 14.8 %collective-permute-start.3 = (bf16[1584,128]{1,0:T(8,128)(2,1)}, bf16[1584,128]{1,0:T(8,128)(2,1)S(1)}, u32[]{:S(2)}, u32[]{:S(2)}) collective-permute-start(bf16[1584,128]{1,0:T(8,128)(2,1)} %get-tuple-element.24.refs_0_), channel_id=1, source_target_pairs={{0,64},{64,0},{1,65},{65,1},{2,66},{66,2},{3,67},{67,3},{4,68},{68... | collective-permute-start | bytes 1216520 | tf_op jit(solution)/shard_map/ppermute | solution.py:30
  24.6 12.9 %collective-permute-start.4 = (bf16[1584,128]{1,0:T(8,128)(2,1)S(1)}, bf16[1584,128]{1,0:T(8,128)(2,1)S(1)}, u32[]{:S(2)}, u32[]{:S(2)}) collective-permute-start(bf16[1584,128]{1,0:T(8,128)(2,1)S(1)} %collective-permute-done.refs_1_), channel_id=1, source_target_pairs={{0,64},{64,0},{1,65},{65,1},{2,66},{66,2},{3,67},{67,3},{4,68},{68... | collective-permute-start | bytes 1216520 | tf_op jit(solution)/shard_map/ppermute | solution.py:30
  27.0 10.5 %collective-permute-start.5 = (bf16[1584,128]{1,0:T(8,128)(2,1)S(1)}, bf16[1584,128]{1,0:T(8,128)(2,1)S(1)}, u32[]{:S(2)}, u32[]{:S(2)}) collective-permute-start(bf16[1584,128]{1,0:T(8,128)(2,1)S(1)} %collective-permute-done.1.refs_2_), channel_id=1, source_target_pairs={{0,64},{64,0},{1,65},{65,1},{2,66},{66,2},{3,67},{67,3},{4,68},{68... | collective-permute-start | bytes 1216520 | tf_op jit(solution)/shard_map/ppermute | solution.py:30
  33.3 3.7 %copy-start.7 = (bf16[1584,128]{1,0:T(8,128)(2,1)}, bf16[1584,128]{1,0:T(8,128)(2,1)S(1)}, u32[]{:S(2)}) copy-start(bf16[1584,128]{1,0:T(8,128)(2,1)S(1)} %collective-permute-done.2.refs_3_) | copy-start | bytes 1216516
  33.3 4.2 %collective-permute-start.6 = (bf16[1584,128]{1,0:T(8,128)(2,1)S(1)}, bf16[1584,128]{1,0:T(8,128)(2,1)S(1)}, u32[]{:S(2)}, u32[]{:S(2)}) collective-permute-start(bf16[1584,128]{1,0:T(8,128)(2,1)S(1)} %collective-permute-done.2.refs_3_), channel_id=1, source_target_pairs={{0,64},{64,0},{1,65},{65,1},{2,66},{66,2},{3,67},{67,3},{4,68},{68... | collective-permute-start | bytes 1216520 | tf_op jit(solution)/shard_map/ppermute | solution.py:30
  37.0 0.5 copy-start.3
  37.5 5.1 %copy-start.11 = (bf16[1584,128]{1,0:T(8,128)(2,1)}, bf16[1584,128]{1,0:T(8,128)(2,1)S(1)}, u32[]{:S(2)}) copy-start(bf16[1584,128]{1,0:T(8,128)(2,1)S(1)} %collective-permute-done.6.refs_7_) | copy-start | bytes 1216516
  37.5 5.1 %copy-start.8 = (bf16[1584,128]{1,0:T(8,128)(2,1)}, bf16[1584,128]{1,0:T(8,128)(2,1)S(1)}, u32[]{:S(2)}) copy-start(bf16[1584,128]{1,0:T(8,128)(2,1)S(1)} %collective-permute-done.3.refs_4_) | copy-start | bytes 1216516
  37.6 5.1 %copy-start.9 = (bf16[1584,128]{1,0:T(8,128)(2,1)}, bf16[1584,128]{1,0:T(8,128)(2,1)S(1)}, u32[]{:S(2)}) copy-start(bf16[1584,128]{1,0:T(8,128)(2,1)S(1)} %collective-permute-done.4.refs_5_) | copy-start | bytes 1216516
  37.6 5.1 %copy-start.10 = (bf16[1584,128]{1,0:T(8,128)(2,1)}, bf16[1584,128]{1,0:T(8,128)(2,1)S(1)}, u32[]{:S(2)}) copy-start(bf16[1584,128]{1,0:T(8,128)(2,1)S(1)} %collective-permute-done.5.refs_6_) | copy-start | bytes 1216516
  42.7 0.8 copy-start.4
  52.8 10.3 %collective-permute-start.7 = (f32[4,128,768]{2,1,0:T(8,128)}, f32[4,128,768]{2,1,0:T(8,128)S(1)}, u32[]{:S(2)}, u32[]{:S(2)}) collective-permute-start(f32[4,128,768]{2,1,0:T(8,128)} %get-tuple-element.28), channel_id=1, source_target_pairs={{0,64},{64,0},{1,65},{65,1},{2,66},{66,2},{3,67},{67,3},{4,68},{68... | collective-permute-start | bytes 4718600 | tf_op jit(solution)/shard_map/ppermute | solution.py:30
  54.7 25.1 %all-to-all-start.1 = ((bf16[8,256,128]{2,1,0:T(8,128)(2,1)}), bf16[8,256,128]{2,1,0:T(8,128)(2,1)S(1)}, u32[]{:S(2)}, u32[]{:S(2)}) async-start(bf16[8,256,128]{2,1,0:T(8,128)(2,1)} %get-tuple-element.26), calls=%async_computation.1 | async-start | bytes 1048576 | tf_op jit(solution)/shard_map/all_to_all | solution.py:342
  63.1 1.4 %copy-start = (f32[4,128,768]{2,1,0:T(8,128)S(1)}, f32[4,128,768]{2,1,0:T(8,128)}, u32[]{:S(2)}) copy-start(f32[4,128,768]{2,1,0:T(8,128)} %get-tuple-element.27.mine) | copy-start | bytes 4718596
  64.6 26.4 %collective-permute-start.8 = (bf16[128,768]{1,0:T(8,128)(2,1)S(1)}, bf16[128,768]{1,0:T(8,128)(2,1)S(1)}, u32[]{:S(2)}, u32[]{:S(2)}) collective-permute-start(bf16[128,768]{1,0:T(8,128)(2,1)S(1)} %get-tuple-element.31), channel_id=1, source_target_pairs={{0,8},{8,0},{16,24},{24,16},{1,9},{9,1},{17,25},{25,17},{2,10},{10... | collective-permute-start | bytes 589832 | tf_op jit(solution)/shard_map/ppermute | solution.py:34
  66.6 24.5 %collective-permute-start.9 = (bf16[128,768]{1,0:T(8,128)(2,1)S(1)}, bf16[128,768]{1,0:T(8,128)(2,1)S(1)}, u32[]{:S(2)}, u32[]{:S(2)}) collective-permute-start(bf16[128,768]{1,0:T(8,128)(2,1)S(1)} %get-tuple-element.32), channel_id=1, source_target_pairs={{0,16},{8,24},{16,0},{24,8},{1,17},{9,25},{17,1},{25,9},{2,18},{10... | collective-permute-start | bytes 589832 | tf_op jit(solution)/shard_map/ppermute | solution.py:34
  68.5 22.5 %collective-permute-start.10 = (bf16[128,768]{1,0:T(8,128)(2,1)S(1)}, bf16[128,768]{1,0:T(8,128)(2,1)S(1)}, u32[]{:S(2)}, u32[]{:S(2)}) collective-permute-start(bf16[128,768]{1,0:T(8,128)(2,1)S(1)} %get-tuple-element.33), channel_id=1, source_target_pairs={{0,24},{8,16},{16,8},{24,0},{1,25},{9,17},{17,9},{25,1},{2,26},{10... | collective-permute-start | bytes 589832 | tf_op jit(solution)/shard_map/ppermute | solution.py:34
  80.7 26.2 %all-to-all-start.2 = ((bf16[8,256,128]{2,1,0:T(8,128)(2,1)}), bf16[8,256,128]{2,1,0:T(8,128)(2,1)S(1)}, u32[]{:S(2)}, u32[]{:S(2)}) async-start(bf16[8,256,128]{2,1,0:T(8,128)(2,1)} %sum_rows.1), calls=%async_computation.2 | async-start | bytes 1048576 | tf_op jit(solution)/shard_map/all_to_all | solution.py:346

commit v6 on v5

--- a/solution.py
+++ b/solution.py
@@ -332,11 +332,14 @@
     queries, out_grad, outputs = (jnp.swapaxes(a, 0, 1) for a in (queries, out_grad, outputs))
     head = jnp.reshape(z, (1,)).astype(jnp.int32)
     pack, kv = prepare(head, queries, out_grad, outputs, log_norm, keys, values)
-    near = [exchange(pack, flip) for flip in (1, 2, 3)]
+    near = [exchange(pack, 1), exchange(pack, 2)]
     col = lax.all_to_all(kv, COLUMN, 0, 0)
     ids, near[0], near[1], again = lax.optimization_barrier((ids, near[0], near[1], pack))
     pairs = reach(ids, parents)
-    swapped = [swap_cores(p) for p in [again, *near]]
+    near.append(exchange(near[0], 2))
+    swapped = [swap_cores(p) for p in [again, *near[:2]]]
+    far, pairs, *swapped = lax.optimization_barrier((near[2], pairs, *swapped))
+    swapped.append(swap_cores(far))
     packs = [pack, *near, *swapped]
     part, mine, other = attend(ids, pairs, packs, col)
     row = lax.all_to_all(part, COLUMN, 0, 0)

time: 110 us -> 108 us (0.982)
  the two profiles are of different devices: /device:TPU:6 before, /device:TPU:9 now
where the time goes in v6:
time: 108 us; the launch traced here: 107 us
  starting transfers between devices  64 us (59%)
  waiting for transfers between devices  27.9 us (26%)
  Pallas kernels  11.7 us (11%)
  local copies, waits for them, and re-layouts  2.77 us (3%)
    ppermute x6, starting transfers between devices, exchange(): return lax.ppermute(block, SQUARE, [(i, i ^ flip) for i in range(4)])  22.2 us
    all_to_all x1, waiting for transfers between devices, body(): heads = lax.all_to_all(sum_rows(row), 'z', 0, 0)  17.1 us
    ppermute x5, starting transfers between devices, swap_cores(): return lax.ppermute(block, 'core', [(0, 1), (1, 0)])  15.2 us
    all_to_all x1, starting transfers between devices, body(): heads = lax.all_to_all(sum_rows(row), 'z', 0, 0)  10 us
    all_to_all x1, starting transfers between devices, body(): col = lax.all_to_all(kv, COLUMN, 0, 0)  9 us
    all_to_all x1, starting transfers between devices, body(): row = lax.all_to_all(part, COLUMN, 0, 0)  7.59 us
    all_to_all x1, waiting for transfers between devices, body(): row = lax.all_to_all(part, COLUMN, 0, 0)  5.84 us
    pallas_call x1, Pallas kernels, attend(): pl.pallas_call(attend_kernel, out_shape=(jax.ShapeDtypeStruct((8, 2 * BLK...  4.61 us
  transfers between devices with their start and end apart: 14, of which 4 were waited for; matrix products, arithmetic and copies ran while one was open for 0% of the time, Pallas kernels for 3%

profile of v6, /device:TPU:9, one launch (start us, length us, event | category | flops | bytes accessed | tf_op | source)
XLA Modules:
  0.0 107.3 jit_solution(1464233162470348594)
XLA Ops:
  0.6 0.0 copy-start.2
  0.6 2.6 %prepare.1 = (bf16[1584,128]{1,0:T(8,128)(2,1)}, bf16[8,256,128]{2,1,0:T(8,128)(2,1)}) custom-call(s32[1]{0:T(128)} %bitcast.9.head, bf16[6,128,128]{2,1,0:T(8,128)(2,1)} %bitcast.14, bf16[6,128,128]{2,1,0:T(8,128)(2,1)} %bitcast.15, bf16[6,128,128]{2,1,0:T(8,128)(2,1)} %bitcast.16, f32[6,128]{1,0:T(8,128)} %ln_hbm.1, bf16[128,8,128]{2,1,0:T(8,128)(2,1)} %k_hbm.1, ...), custom_call_target="tpu_custom_call" | custom-call | flops 4000000 | bytes 1000000 | tf_op jit(solution)/shard_map/prepare/pallas_call | solution.py:130
  3.3 3.1 %collective-permute-start.1 = (bf16[1584,128]{1,0:T(8,128)(2,1)}, bf16[1584,128]{1,0:T(8,128)(2,1)S(1)}, u32[]{:S(2)}, u32[]{:S(2)}) collective-permute-start(bf16[1584,128]{1,0:T(8,128)(2,1)} %get-tuple-element.28.refs_0_), channel_id=1, source_target_pairs={{0,16},{8,24},{16,0},{24,8},{1,17},{9,25},{17,1},{25,9},{2,18},{10... | collective-permute-start | bytes 1216520 | tf_op jit(solution)/shard_map/ppermute | solution.py:34
  6.4 2.1 %collective-permute-start = (bf16[1584,128]{1,0:T(8,128)(2,1)}, bf16[1584,128]{1,0:T(8,128)(2,1)S(1)}, u32[]{:S(2)}, u32[]{:S(2)}) collective-permute-start(bf16[1584,128]{1,0:T(8,128)(2,1)} %get-tuple-element.28.refs_0_), channel_id=1, source_target_pairs={{0,8},{8,0},{16,24},{24,16},{1,9},{9,1},{17,25},{25,17},{2,10},{10... | collective-permute-start | bytes 1216520 | tf_op jit(solution)/shard_map/ppermute | solution.py:34
  8.5 9.0 %all-to-all-start = ((bf16[8,256,128]{2,1,0:T(8,128)(2,1)}), bf16[8,256,128]{2,1,0:T(8,128)(2,1)S(1)}, u32[]{:S(2)}, u32[]{:S(2)}) async-start(bf16[8,256,128]{2,1,0:T(8,128)(2,1)} %get-tuple-element.35), calls=%async_computation | async-start | bytes 1048576 | tf_op jit(solution)/shard_map/all_to_all | solution.py:336
  17.5 0.1 stack.39.ids
  17.6 0.0 copy-start.1
  17.6 0.0 collective-permute-done.1.refs_2_
  17.6 0.0 copy-start.5
  17.6 0.0 collective-permute-done.refs_1_
  17.6 0.0 copy-start.6
  17.6 5.1 %collective-permute-start.4 = (bf16[1584,128]{1,0:T(8,128)(2,1)S(1)}, bf16[1584,128]{1,0:T(8,128)(2,1)S(1)}, u32[]{:S(2)}, u32[]{:S(2)}) collective-permute-start(bf16[1584,128]{1,0:T(8,128)(2,1)S(1)} %collective-permute-done.refs_1_), channel_id=1, source_target_pairs={{0,64},{64,0},{1,65},{65,1},{2,66},{66,2},{3,67},{67,3},{4,68},{68... | collective-permute-start | bytes 1216520 | tf_op jit(solution)/shard_map/ppermute | solution.py:30
  22.7 8.6 %collective-permute-start.2 = (bf16[1584,128]{1,0:T(8,128)(2,1)S(1)}, bf16[1584,128]{1,0:T(8,128)(2,1)S(1)}, u32[]{:S(2)}, u32[]{:S(2)}) collective-permute-start(bf16[1584,128]{1,0:T(8,128)(2,1)S(1)} %collective-permute-done.refs_1_), channel_id=1, source_target_pairs={{0,16},{8,24},{16,0},{24,8},{1,17},{9,25},{17,1},{25,9},{2,18},{10... | collective-permute-start | bytes 1216520 | tf_op jit(solution)/shard_map/ppermute | solution.py:34
  31.3 2.2 %collective-permute-start.3 = (bf16[1584,128]{1,0:T(8,128)(2,1)}, bf16[1584,128]{1,0:T(8,128)(2,1)S(1)}, u32[]{:S(2)}, u32[]{:S(2)}) collective-permute-start(bf16[1584,128]{1,0:T(8,128)(2,1)} %get-tuple-element.28.refs_0_), channel_id=1, source_target_pairs={{0,64},{64,0},{1,65},{65,1},{2,66},{66,2},{3,67},{67,3},{4,68},{68... | collective-permute-start | bytes 1216520 | tf_op jit(solution)/shard_map/ppermute | solution.py:30
  33.5 2.1 %collective-permute-start.5 = (bf16[1584,128]{1,0:T(8,128)(2,1)S(1)}, bf16[1584,128]{1,0:T(8,128)(2,1)S(1)}, u32[]{:S(2)}, u32[]{:S(2)}) collective-permute-start(bf16[1584,128]{1,0:T(8,128)(2,1)S(1)} %collective-permute-done.1.refs_2_), channel_id=1, source_target_pairs={{0,64},{64,0},{1,65},{65,1},{2,66},{66,2},{3,67},{67,3},{4,68},{68... | collective-permute-start | bytes 1216520 | tf_op jit(solution)/shard_map/ppermute | solution.py:30
  35.7 0.0 copy-done.2
  35.7 1.7 %reach.1.pairs = s32[67]{0:T(128)S(1)} custom-call(s32[9]{0:T(128)S(1)} %stack.39.ids, s32[64]{0:T(128)S(1)} %copy-done.2), custom_call_target="tpu_custom_call" | custom-call | flops 60000002048 | bytes 1000 | tf_op jit(solution)/shard_map/reach/pallas_call | solution.py:82
  37.4 0.0 copy-done.1
  37.4 0.0 copy-done.5
  37.4 0.0 copy-done.6
  37.4 0.0 copy-start.3
  37.4 0.5 copy-done.3
  37.9 0.0 collective-permute-done.3.refs_4_
  37.9 0.0 copy-start.9
  37.9 0.0 collective-permute-done.5.refs_6_
  37.9 0.0 copy-start.10
  38.0 0.0 collective-permute-done.4.refs_5_
  38.0 0.0 copy-start.7
  38.0 3.7 %collective-permute-done.2.refs_3_ = bf16[1584,128]{1,0:T(8,128)(2,1)S(1)} collective-permute-done((bf16[1584,128]{1,0:T(8,128)(2,1)S(1)}, bf16[1584,128]{1,0:T(8,128)(2,1)S(1)}, u32[]{:S(2)}, u32[]{:S(2)}) %collective-permute-start.2) | collective-permute-done | bytes 405536 | tf_op jit(solution)/shard_map/ppermute | solution.py:34
  41.6 0.0 copy-start.8
  41.6 2.4 %collective-permute-start.6 = (bf16[1584,128]{1,0:T(8,128)(2,1)S(1)}, bf16[1584,128]{1,0:T(8,128)(2,1)S(1)}, u32[]{:S(2)}, u32[]{:S(2)}) collective-permute-start(bf16[1584,128]{1,0:T(8,128)(2,1)S(1)} %collective-permute-done.2.refs_3_), channel_id=1, source_target_pairs={{0,64},{64,0},{1,65},{65,1},{2,66},{66,2},{3,67},{67,3},{4,68},{68... | collective-permute-start | bytes 1216520 | tf_op jit(solution)/shard_map/ppermute | solution.py:30
  44.1 0.0 all-to-all-done.refs_8_
  44.1 0.0 copy-start.4
  44.1 1.3 %collective-permute-done.6.refs_7_ = bf16[1584,128]{1,0:T(8,128)(2,1)S(1)} collective-permute-done((bf16[1584,128]{1,0:T(8,128)(2,1)S(1)}, bf16[1584,128]{1,0:T(8,128)(2,1)S(1)}, u32[]{:S(2)}, u32[]{:S(2)}) %collective-permute-start.6) | collective-permute-done | bytes 405536 | tf_op jit(solution)/shard_map/ppermute | solution.py:30
  45.4 0.0 copy-done.9
  45.4 0.0 copy-done.10
  45.4 0.0 copy-done.7
  45.4 0.0 copy-done.8
  45.4 0.0 copy-done.4
  45.4 0.0 copy-start.11
  45.5 0.7 copy-done.11
  46.2 4.6 %attend.1 = (bf16[8,256,128]{2,1,0:T(8,128)(2,1)}, f32[4,128,768]{2,1,0:T(8,128)}, f32[4,128,768]{2,1,0:T(8,128)}) custom-call(s32[9]{0:T(128)} %copy-done.1, s32[67]{0:T(128)} %copy-done.3, bf16[1584,128]{1,0:T(8,128)(2,1)} %get-tuple-element.28.refs_0_, bf16[1584,128]{1,0:T(8,128)(2,1)} %copy-done.6, bf16[1584,128]{1,0:T(8,128)(2,1)} %copy-done.5, ...), custom_call_target="tpu_custom_call" | custom-call | flops 2000000000 | bytes 8000000 | tf_op jit(solution)/shard_map/attend/pallas_call | solution.py:226
  50.8 3.3 %collective-permute-start.7 = (f32[4,128,768]{2,1,0:T(8,128)}, f32[4,128,768]{2,1,0:T(8,128)S(1)}, u32[]{:S(2)}, u32[]{:S(2)}) collective-permute-start(f32[4,128,768]{2,1,0:T(8,128)} %get-tuple-element.38), channel_id=1, source_target_pairs={{0,64},{64,0},{1,65},{65,1},{2,66},{66,2},{3,67},{67,3},{4,68},{68... | collective-permute-start | bytes 4718600 | tf_op jit(solution)/shard_map/ppermute | solution.py:30
  54.1 7.6 %all-to-all-start.1 = ((bf16[8,256,128]{2,1,0:T(8,128)(2,1)}), bf16[8,256,128]{2,1,0:T(8,128)(2,1)S(1)}, u32[]{:S(2)}, u32[]{:S(2)}) async-start(bf16[8,256,128]{2,1,0:T(8,128)(2,1)} %get-tuple-element.36), calls=%async_computation.1 | async-start | bytes 1048576 | tf_op jit(solution)/shard_map/all_to_all | solution.py:345
  61.7 0.0 collective-permute-done.7.other
  61.7 0.0 copy-start
  61.8 1.4 %copy-done = f32[4,128,768]{2,1,0:T(8,128)S(1)} copy-done((f32[4,128,768]{2,1,0:T(8,128)S(1)}, f32[4,128,768]{2,1,0:T(8,128)}, u32[]{:S(2)}) %copy-start) | copy-done | bytes 1572888
  63.1 0.1 add_cores.1
  63.3 1.9 %collective-permute-start.8 = (bf16[128,768]{1,0:T(8,128)(2,1)S(1)}, bf16[128,768]{1,0:T(8,128)(2,1)S(1)}, u32[]{:S(2)}, u32[]{:S(2)}) collective-permute-start(bf16[128,768]{1,0:T(8,128)(2,1)S(1)} %get-tuple-element.41), channel_id=1, source_target_pairs={{0,8},{8,0},{16,24},{24,16},{1,9},{9,1},{17,25},{25,17},{2,10},{10... | collective-permute-start | bytes 589832 | tf_op jit(solution)/shard_map/ppermute | solution.py:34
  65.2 1.9 %collective-permute-start.9 = (bf16[128,768]{1,0:T(8,128)(2,1)S(1)}, bf16[128,768]{1,0:T(8,128)(2,1)S(1)}, u32[]{:S(2)}, u32[]{:S(2)}) collective-permute-start(bf16[128,768]{1,0:T(8,128)(2,1)S(1)} %get-tuple-element.42), channel_id=1, source_target_pairs={{0,16},{8,24},{16,0},{24,8},{1,17},{9,25},{17,1},{25,9},{2,18},{10... | collective-permute-start | bytes 589832 | tf_op jit(solution)/shard_map/ppermute | solution.py:34
  67.2 4.5 %collective-permute-start.10 = (bf16[128,768]{1,0:T(8,128)(2,1)S(1)}, bf16[128,768]{1,0:T(8,128)(2,1)S(1)}, u32[]{:S(2)}, u32[]{:S(2)}) collective-permute-start(bf16[128,768]{1,0:T(8,128)(2,1)S(1)} %get-tuple-element.43), channel_id=1, source_target_pairs={{0,24},{8,16},{16,8},{24,0},{1,25},{9,17},{17,9},{25,1},{2,26},{10... | collective-permute-start | bytes 589832 | tf_op jit(solution)/shard_map/ppermute | solution.py:34
  71.7 5.8 %all-to-all-done.1.parts = bf16[8,256,128]{2,1,0:T(8,128)(2,1)S(1)} async-done(((bf16[8,256,128]{2,1,0:T(8,128)(2,1)}), bf16[8,256,128]{2,1,0:T(8,128)(2,1)S(1)}, u32[]{:S(2)}, u32[]{:S(2)}) %all-to-all-start.1) | async-done | bytes 524320 | tf_op jit(solution)/shard_map/all_to_all | solution.py:345
  77.5 0.9 sum_rows.1
  78.4 10.0 %all-to-all-start.2 = ((bf16[8,256,128]{2,1,0:T(8,128)(2,1)}), bf16[8,256,128]{2,1,0:T(8,128)(2,1)S(1)}, u32[]{:S(2)}, u32[]{:S(2)}) async-start(bf16[8,256,128]{2,1,0:T(8,128)(2,1)} %sum_rows.1), calls=%async_computation.2 | async-start | bytes 1048576 | tf_op jit(solution)/shard_map/all_to_all | solution.py:349
  88.5 0.0 collective-permute-done.8.b
  88.5 0.0 collective-permute-done.9.c
  88.5 0.0 collective-permute-done.10.d
  88.5 0.9 finish_query.1
  89.3 17.1 %all-to-all-done.2.parts = bf16[8,256,128]{2,1,0:T(8,128)(2,1)S(1)} async-done(((bf16[8,256,128]{2,1,0:T(8,128)(2,1)}), bf16[8,256,128]{2,1,0:T(8,128)(2,1)S(1)}, u32[]{:S(2)}, u32[]{:S(2)}) %all-to-all-start.2) | async-done | bytes 524320 | tf_op jit(solution)/shard_map/all_to_all | solution.py:349
  106.4 0.9 split_heads.1
Async XLA Ops:
  0.6 35.0 %copy-start.2 = (s32[64]{0:T(128)S(1)}, s32[64]{0:T(128)}, u32[]{:S(2)}) copy-start(s32[64]{0:T(128)} %parents.1) | copy-start | bytes 772
  3.3 14.3 %collective-permute-start.1 = (bf16[1584,128]{1,0:T(8,128)(2,1)}, bf16[1584,128]{1,0:T(8,128)(2,1)S(1)}, u32[]{:S(2)}, u32[]{:S(2)}) collective-permute-start(bf16[1584,128]{1,0:T(8,128)(2,1)} %get-tuple-element.28.refs_0_), channel_id=1, source_target_pairs={{0,16},{8,24},{16,0},{24,8},{1,17},{9,25},{17,1},{25,9},{2,18},{10... | collective-permute-start | bytes 1216520 | tf_op jit(solution)/shard_map/ppermute | solution.py:34
  6.4 11.2 %collective-permute-start = (bf16[1584,128]{1,0:T(8,128)(2,1)}, bf16[1584,128]{1,0:T(8,128)(2,1)S(1)}, u32[]{:S(2)}, u32[]{:S(2)}) collective-permute-start(bf16[1584,128]{1,0:T(8,128)(2,1)} %get-tuple-element.28.refs_0_), channel_id=1, source_target_pairs={{0,8},{8,0},{16,24},{24,16},{1,9},{9,1},{17,25},{25,17},{2,10},{10... | collective-permute-start | bytes 1216520 | tf_op jit(solution)/shard_map/ppermute | solution.py:34
  8.5 35.6 %all-to-all-start = ((bf16[8,256,128]{2,1,0:T(8,128)(2,1)}), bf16[8,256,128]{2,1,0:T(8,128)(2,1)S(1)}, u32[]{:S(2)}, u32[]{:S(2)}) async-start(bf16[8,256,128]{2,1,0:T(8,128)(2,1)} %get-tuple-element.35), calls=%async_computation | async-start | bytes 1048576 | tf_op jit(solution)/shard_map/all_to_all | solution.py:336
  17.6 19.8 %copy-start.1 = (s32[9]{0:T(128)}, s32[9]{0:T(128)S(1)}, u32[]{:S(2)}) copy-start(s32[9]{0:T(128)S(1)} %stack.39.ids) | copy-start | bytes 112
  17.6 19.8 %copy-start.5 = (bf16[1584,128]{1,0:T(8,128)(2,1)}, bf16[1584,128]{1,0:T(8,128)(2,1)S(1)}, u32[]{:S(2)}) copy-start(bf16[1584,128]{1,0:T(8,128)(2,1)S(1)} %collective-permute-done.1.refs_2_) | copy-start | bytes 1216516
  17.6 19.8 %copy-start.6 = (bf16[1584,128]{1,0:T(8,128)(2,1)}, bf16[1584,128]{1,0:T(8,128)(2,1)S(1)}, u32[]{:S(2)}) copy-start(bf16[1584,128]{1,0:T(8,128)(2,1)S(1)} %collective-permute-done.refs_1_) | copy-start | bytes 1216516
  17.6 20.4 %collective-permute-start.4 = (bf16[1584,128]{1,0:T(8,128)(2,1)S(1)}, bf16[1584,128]{1,0:T(8,128)(2,1)S(1)}, u32[]{:S(2)}, u32[]{:S(2)}) collective-permute-start(bf16[1584,128]{1,0:T(8,128)(2,1)S(1)} %collective-permute-done.refs_1_), channel_id=1, source_target_pairs={{0,64},{64,0},{1,65},{65,1},{2,66},{66,2},{3,67},{67,3},{4,68},{68... | collective-permute-start | bytes 1216520 | tf_op jit(solution)/shard_map/ppermute | solution.py:30
  22.7 18.9 %collective-permute-start.2 = (bf16[1584,128]{1,0:T(8,128)(2,1)S(1)}, bf16[1584,128]{1,0:T(8,128)(2,1)S(1)}, u32[]{:S(2)}, u32[]{:S(2)}) collective-permute-start(bf16[1584,128]{1,0:T(8,128)(2,1)S(1)} %collective-permute-done.refs_1_), channel_id=1, source_target_pairs={{0,16},{8,24},{16,0},{24,8},{1,17},{9,25},{17,1},{25,9},{2,18},{10... | collective-permute-start | bytes 1216520 | tf_op jit(solution)/shard_map/ppermute | solution.py:34
  31.3 6.6 %collective-permute-start.3 = (bf16[1584,128]{1,0:T(8,128)(2,1)}, bf16[1584,128]{1,0:T(8,128)(2,1)S(1)}, u32[]{:S(2)}, u32[]{:S(2)}) collective-permute-start(bf16[1584,128]{1,0:T(8,128)(2,1)} %get-tuple-element.28.refs_0_), channel_id=1, source_target_pairs={{0,64},{64,0},{1,65},{65,1},{2,66},{66,2},{3,67},{67,3},{4,68},{68... | collective-permute-start | bytes 1216520 | tf_op jit(solution)/shard_map/ppermute | solution.py:30
  33.5 4.4 %collective-permute-start.5 = (bf16[1584,128]{1,0:T(8,128)(2,1)S(1)}, bf16[1584,128]{1,0:T(8,128)(2,1)S(1)}, u32[]{:S(2)}, u32[]{:S(2)}) collective-permute-start(bf16[1584,128]{1,0:T(8,128)(2,1)S(1)} %collective-permute-done.1.refs_2_), channel_id=1, source_target_pairs={{0,64},{64,0},{1,65},{65,1},{2,66},{66,2},{3,67},{67,3},{4,68},{68... | collective-permute-start | bytes 1216520 | tf_op jit(solution)/shard_map/ppermute | solution.py:30
  37.4 0.5 copy-start.3
  37.9 7.5 %copy-start.9 = (bf16[1584,128]{1,0:T(8,128)(2,1)}, bf16[1584,128]{1,0:T(8,128)(2,1)S(1)}, u32[]{:S(2)}) copy-start(bf16[1584,128]{1,0:T(8,128)(2,1)S(1)} %collective-permute-done.3.refs_4_) | copy-start | bytes 1216516
  37.9 7.5 %copy-start.10 = (bf16[1584,128]{1,0:T(8,128)(2,1)}, bf16[1584,128]{1,0:T(8,128)(2,1)S(1)}, u32[]{:S(2)}) copy-start(bf16[1584,128]{1,0:T(8,128)(2,1)S(1)} %collective-permute-done.5.refs_6_) | copy-start | bytes 1216516
  38.0 7.5 %copy-start.7 = (bf16[1584,128]{1,0:T(8,128)(2,1)}, bf16[1584,128]{1,0:T(8,128)(2,1)S(1)}, u32[]{:S(2)}) copy-start(bf16[1584,128]{1,0:T(8,128)(2,1)S(1)} %collective-permute-done.4.refs_5_) | copy-start | bytes 1216516
  41.6 3.8 %copy-start.8 = (bf16[1584,128]{1,0:T(8,128)(2,1)}, bf16[1584,128]{1,0:T(8,128)(2,1)S(1)}, u32[]{:S(2)}) copy-start(bf16[1584,128]{1,0:T(8,128)(2,1)S(1)} %collective-permute-done.2.refs_3_) | copy-start | bytes 1216516
  41.6 3.8 %collective-permute-start.6 = (bf16[1584,128]{1,0:T(8,128)(2,1)S(1)}, bf16[1584,128]{1,0:T(8,128)(2,1)S(1)}, u32[]{:S(2)}, u32[]{:S(2)}) collective-permute-start(bf16[1584,128]{1,0:T(8,128)(2,1)S(1)} %collective-permute-done.2.refs_3_), channel_id=1, source_target_pairs={{0,64},{64,0},{1,65},{65,1},{2,66},{66,2},{3,67},{67,3},{4,68},{68... | collective-permute-start | bytes 1216520 | tf_op jit(solution)/shard_map/ppermute | solution.py:30
  44.1 1.4 %copy-start.4 = (bf16[8,256,128]{2,1,0:T(8,128)(2,1)}, bf16[8,256,128]{2,1,0:T(8,128)(2,1)S(1)}, u32[]{:S(2)}) copy-start(bf16[8,256,128]{2,1,0:T(8,128)(2,1)S(1)} %all-to-all-done.refs_8_) | copy-start | bytes 1572868
  45.4 0.8 copy-start.11
  50.8 10.9 %collective-permute-start.7 = (f32[4,128,768]{2,1,0:T(8,128)}, f32[4,128,768]{2,1,0:T(8,128)S(1)}, u32[]{:S(2)}, u32[]{:S(2)}) collective-permute-start(f32[4,128,768]{2,1,0:T(8,128)} %get-tuple-element.38), channel_id=1, source_target_pairs={{0,64},{64,0},{1,65},{65,1},{2,66},{66,2},{3,67},{67,3},{4,68},{68... | collective-permute-start | bytes 4718600 | tf_op jit(solution)/shard_map/ppermute | solution.py:30
  54.1 23.4 %all-to-all-start.1 = ((bf16[8,256,128]{2,1,0:T(8,128)(2,1)}), bf16[8,256,128]{2,1,0:T(8,128)(2,1)S(1)}, u32[]{:S(2)}, u32[]{:S(2)}) async-start(bf16[8,256,128]{2,1,0:T(8,128)(2,1)} %get-tuple-element.36), calls=%async_computation.1 | async-start | bytes 1048576 | tf_op jit(solution)/shard_map/all_to_all | solution.py:345
  61.7 1.4 %copy-start = (f32[4,128,768]{2,1,0:T(8,128)S(1)}, f32[4,128,768]{2,1,0:T(8,128)}, u32[]{:S(2)}) copy-start(f32[4,128,768]{2,1,0:T(8,128)} %get-tuple-element.37.mine) | copy-start | bytes 4718596
  63.3 25.2 %collective-permute-start.8 = (bf16[128,768]{1,0:T(8,128)(2,1)S(1)}, bf16[128,768]{1,0:T(8,128)(2,1)S(1)}, u32[]{:S(2)}, u32[]{:S(2)}) collective-permute-start(bf16[128,768]{1,0:T(8,128)(2,1)S(1)} %get-tuple-element.41), channel_id=1, source_target_pairs={{0,8},{8,0},{16,24},{24,16},{1,9},{9,1},{17,25},{25,17},{2,10},{10... | collective-permute-start | bytes 589832 | tf_op jit(solution)/shard_map/ppermute | solution.py:34
  65.2 23.2 %collective-permute-start.9 = (bf16[128,768]{1,0:T(8,128)(2,1)S(1)}, bf16[128,768]{1,0:T(8,128)(2,1)S(1)}, u32[]{:S(2)}, u32[]{:S(2)}) collective-permute-start(bf16[128,768]{1,0:T(8,128)(2,1)S(1)} %get-tuple-element.42), channel_id=1, source_target_pairs={{0,16},{8,24},{16,0},{24,8},{1,17},{9,25},{17,1},{25,9},{2,18},{10... | collective-permute-start | bytes 589832 | tf_op jit(solution)/shard_map/ppermute | solution.py:34
  67.2 21.3 %collective-permute-start.10 = (bf16[128,768]{1,0:T(8,128)(2,1)S(1)}, bf16[128,768]{1,0:T(8,128)(2,1)S(1)}, u32[]{:S(2)}, u32[]{:S(2)}) collective-permute-start(bf16[128,768]{1,0:T(8,128)(2,1)S(1)} %get-tuple-element.43), channel_id=1, source_target_pairs={{0,24},{8,16},{16,8},{24,0},{1,25},{9,17},{17,9},{25,1},{2,26},{10... | collective-permute-start | bytes 589832 | tf_op jit(solution)/shard_map/ppermute | solution.py:34
  78.4 28.0 %all-to-all-start.2 = ((bf16[8,256,128]{2,1,0:T(8,128)(2,1)}), bf16[8,256,128]{2,1,0:T(8,128)(2,1)S(1)}, u32[]{:S(2)}, u32[]{:S(2)}) async-start(bf16[8,256,128]{2,1,0:T(8,128)(2,1)} %sum_rows.1), calls=%async_computation.2 | async-start | bytes 1048576 | tf_op jit(solution)/shard_map/all_to_all | solution.py:349

commit v7 on v6

--- a/solution.py
+++ b/solution.py
@@ -332,11 +332,10 @@
     queries, out_grad, outputs = (jnp.swapaxes(a, 0, 1) for a in (queries, out_grad, outputs))
     head = jnp.reshape(z, (1,)).astype(jnp.int32)
     pack, kv = prepare(head, queries, out_grad, outputs, log_norm, keys, values)
-    near = [exchange(pack, 1), exchange(pack, 2)]
+    near = [exchange(pack, flip) for flip in (1, 2, 3)]
     col = lax.all_to_all(kv, COLUMN, 0, 0)
     ids, near[0], near[1], again = lax.optimization_barrier((ids, near[0], near[1], pack))
     pairs = reach(ids, parents)
-    near.append(exchange(near[0], 2))
     swapped = [swap_cores(p) for p in [again, *near[:2]]]
     far, pairs, *swapped = lax.optimization_barrier((near[2], pairs, *swapped))
     swapped.append(swap_cores(far))

time: 108 us -> 108 us (level)
  the two profiles are of different devices: /device:TPU:9 before, /device:TPU:17 now
where the time goes in v7:
time: 108 us
  starting transfers between devices  62 us (57%)
  waiting for transfers between devices  28.7 us (27%)
  Pallas kernels  12.8 us (12%)
  local copies, waits for them, and re-layouts  3.55 us (3%)
    ppermute x5, starting transfers between devices, swap_cores(): return lax.ppermute(block, 'core', [(0, 1), (1, 0)])  20.4 us
    all_to_all x1, waiting for transfers between devices, body(): heads = lax.all_to_all(sum_rows(row), 'z', 0, 0)  17.1 us
    ppermute x6, starting transfers between devices, exchange(): return lax.ppermute(block, SQUARE, [(i, i ^ flip) for i in range(4)])  16.7 us
    all_to_all x1, starting transfers between devices, body(): heads = lax.all_to_all(sum_rows(row), 'z', 0, 0)  10 us
    all_to_all x1, starting transfers between devices, body(): col = lax.all_to_all(kv, COLUMN, 0, 0)  9.34 us
    all_to_all x1, waiting for transfers between devices, body(): row = lax.all_to_all(part, COLUMN, 0, 0)  7.67 us
    pallas_call x1, Pallas kernels, attend(): pl.pallas_call(attend_kernel, out_shape=(jax.ShapeDtypeStruct((8, 2 * BLK...  5.65 us
    all_to_all x1, starting transfers between devices, body(): row = lax.all_to_all(part, COLUMN, 0, 0)  5.5 us
  transfers between devices with their start and end apart: 14, of which 3 were waited for; matrix products, arithmetic and copies ran while one was open for 0% of the time, Pallas kernels for 3%

profile of v7, /device:TPU:17, one launch (start us, length us, event | category | flops | bytes accessed | tf_op | source)
XLA Modules:
  0.0 107.9 jit_solution(5886490465247310409)
XLA Ops:
  0.6 0.0 copy-start.2
  0.6 2.6 %prepare.1 = (bf16[1584,128]{1,0:T(8,128)(2,1)}, bf16[8,256,128]{2,1,0:T(8,128)(2,1)}) custom-call(s32[1]{0:T(128)} %bitcast.9.head, bf16[6,128,128]{2,1,0:T(8,128)(2,1)} %bitcast.14, bf16[6,128,128]{2,1,0:T(8,128)(2,1)} %bitcast.15, bf16[6,128,128]{2,1,0:T(8,128)(2,1)} %bitcast.16, f32[6,128]{1,0:T(8,128)} %ln_hbm.1, bf16[128,8,128]{2,1,0:T(8,128)(2,1)} %k_hbm.1, ...), custom_call_target="tpu_custom_call" | custom-call | flops 4000000 | bytes 1000000 | tf_op jit(solution)/shard_map/prepare/pallas_call | solution.py:130
  3.3 3.1 %collective-permute-start.1 = (bf16[1584,128]{1,0:T(8,128)(2,1)}, bf16[1584,128]{1,0:T(8,128)(2,1)S(1)}, u32[]{:S(2)}, u32[]{:S(2)}) collective-permute-start(bf16[1584,128]{1,0:T(8,128)(2,1)} %get-tuple-element.27.refs_0_), channel_id=1, source_target_pairs={{0,16},{8,24},{16,0},{24,8},{1,17},{9,25},{17,1},{25,9},{2,18},{10... | collective-permute-start | bytes 1216520 | tf_op jit(solution)/shard_map/ppermute | solution.py:34
  6.4 3.2 %collective-permute-start = (bf16[1584,128]{1,0:T(8,128)(2,1)}, bf16[1584,128]{1,0:T(8,128)(2,1)S(1)}, u32[]{:S(2)}, u32[]{:S(2)}) collective-permute-start(bf16[1584,128]{1,0:T(8,128)(2,1)} %get-tuple-element.27.refs_0_), channel_id=1, source_target_pairs={{0,8},{8,0},{16,24},{24,16},{1,9},{9,1},{17,25},{25,17},{2,10},{10... | collective-permute-start | bytes 1216520 | tf_op jit(solution)/shard_map/ppermute | solution.py:34
  9.6 2.0 %collective-permute-start.2 = (bf16[1584,128]{1,0:T(8,128)(2,1)}, bf16[1584,128]{1,0:T(8,128)(2,1)S(1)}, u32[]{:S(2)}, u32[]{:S(2)}) collective-permute-start(bf16[1584,128]{1,0:T(8,128)(2,1)} %get-tuple-element.27.refs_0_), channel_id=1, source_target_pairs={{0,24},{8,16},{16,8},{24,0},{1,25},{9,17},{17,9},{25,1},{2,26},{10... | collective-permute-start | bytes 1216520 | tf_op jit(solution)/shard_map/ppermute | solution.py:34
  11.7 9.3 %all-to-all-start = ((bf16[8,256,128]{2,1,0:T(8,128)(2,1)}), bf16[8,256,128]{2,1,0:T(8,128)(2,1)S(1)}, u32[]{:S(2)}, u32[]{:S(2)}) async-start(bf16[8,256,128]{2,1,0:T(8,128)(2,1)} %get-tuple-element.35), calls=%async_computation | async-start | bytes 1048576 | tf_op jit(solution)/shard_map/all_to_all | solution.py:336
  21.0 0.1 stack.39.ids
  21.1 0.0 copy-start.1
  21.1 0.0 collective-permute-done.1.refs_2_
  21.1 0.0 copy-start.5
  21.1 0.0 collective-permute-done.refs_1_
  21.1 0.0 copy-start.6
  21.1 4.0 %collective-permute-start.3 = (bf16[1584,128]{1,0:T(8,128)(2,1)}, bf16[1584,128]{1,0:T(8,128)(2,1)S(1)}, u32[]{:S(2)}, u32[]{:S(2)}) collective-permute-start(bf16[1584,128]{1,0:T(8,128)(2,1)} %get-tuple-element.27.refs_0_), channel_id=1, source_target_pairs={{0,64},{64,0},{1,65},{65,1},{2,66},{66,2},{3,67},{67,3},{4,68},{68... | collective-permute-start | bytes 1216520 | tf_op jit(solution)/shard_map/ppermute | solution.py:30
  25.1 1.9 %collective-permute-start.4 = (bf16[1584,128]{1,0:T(8,128)(2,1)S(1)}, bf16[1584,128]{1,0:T(8,128)(2,1)S(1)}, u32[]{:S(2)}, u32[]{:S(2)}) collective-permute-start(bf16[1584,128]{1,0:T(8,128)(2,1)S(1)} %collective-permute-done.refs_1_), channel_id=1, source_target_pairs={{0,64},{64,0},{1,65},{65,1},{2,66},{66,2},{3,67},{67,3},{4,68},{68... | collective-permute-start | bytes 1216520 | tf_op jit(solution)/shard_map/ppermute | solution.py:30
  27.1 2.4 %collective-permute-start.5 = (bf16[1584,128]{1,0:T(8,128)(2,1)S(1)}, bf16[1584,128]{1,0:T(8,128)(2,1)S(1)}, u32[]{:S(2)}, u32[]{:S(2)}) collective-permute-start(bf16[1584,128]{1,0:T(8,128)(2,1)S(1)} %collective-permute-done.1.refs_2_), channel_id=1, source_target_pairs={{0,64},{64,0},{1,65},{65,1},{2,66},{66,2},{3,67},{67,3},{4,68},{68... | collective-permute-start | bytes 1216520 | tf_op jit(solution)/shard_map/ppermute | solution.py:30
  29.5 0.0 copy-done.2
  29.5 1.7 %reach.1.pairs = s32[67]{0:T(128)S(1)} custom-call(s32[9]{0:T(128)S(1)} %stack.39.ids, s32[64]{0:T(128)S(1)} %copy-done.2), custom_call_target="tpu_custom_call" | custom-call | flops 60000002048 | bytes 1000 | tf_op jit(solution)/shard_map/reach/pallas_call | solution.py:82
  31.2 0.0 copy-done.1
  31.2 0.0 copy-done.5
  31.2 0.0 copy-done.6
  31.2 0.0 copy-start.3
  31.2 0.5 copy-done.3
  31.7 0.0 collective-permute-done.2.refs_3_
  31.7 0.0 copy-start.7
  31.7 0.0 collective-permute-done.3.refs_4_
  31.7 0.0 copy-start.8
  31.8 0.0 collective-permute-done.4.refs_5_
  31.8 0.0 copy-start.9
  31.8 0.0 collective-permute-done.5.refs_6_
  31.8 0.0 copy-start.10
  31.8 4.2 %collective-permute-start.6 = (bf16[1584,128]{1,0:T(8,128)(2,1)S(1)}, bf16[1584,128]{1,0:T(8,128)(2,1)S(1)}, u32[]{:S(2)}, u32[]{:S(2)}) collective-permute-start(bf16[1584,128]{1,0:T(8,128)(2,1)S(1)} %collective-permute-done.2.refs_3_), channel_id=1, source_target_pairs={{0,64},{64,0},{1,65},{65,1},{2,66},{66,2},{3,67},{67,3},{4,68},{68... | collective-permute-start | bytes 1216520 | tf_op jit(solution)/shard_map/ppermute | solution.py:30
  36.0 3.9 %all-to-all-done.refs_8_ = bf16[8,256,128]{2,1,0:T(8,128)(2,1)S(1)} async-done(((bf16[8,256,128]{2,1,0:T(8,128)(2,1)}), bf16[8,256,128]{2,1,0:T(8,128)(2,1)S(1)}, u32[]{:S(2)}, u32[]{:S(2)}) %all-to-all-start) | async-done | bytes 524320 | tf_op jit(solution)/shard_map/all_to_all | solution.py:336
  39.9 0.0 copy-start.4
  39.9 0.0 collective-permute-done.6.refs_7_
  39.9 0.0 copy-done.7
  39.9 0.0 copy-done.8
  39.9 0.0 copy-done.9
  39.9 0.0 copy-done.10
  39.9 0.8 copy-done.4
  40.7 0.0 copy-start.11
  40.7 0.7 copy-done.11
  41.5 5.7 %attend.1 = (bf16[8,256,128]{2,1,0:T(8,128)(2,1)}, f32[4,128,768]{2,1,0:T(8,128)}, f32[4,128,768]{2,1,0:T(8,128)}) custom-call(s32[9]{0:T(128)} %copy-done.1, s32[67]{0:T(128)} %copy-done.3, bf16[1584,128]{1,0:T(8,128)(2,1)} %get-tuple-element.27.refs_0_, bf16[1584,128]{1,0:T(8,128)(2,1)} %copy-done.6, bf16[1584,128]{1,0:T(8,128)(2,1)} %copy-done.5, ...), custom_call_target="tpu_custom_call" | custom-call | flops 2000000000 | bytes 8000000 | tf_op jit(solution)/shard_map/attend/pallas_call | solution.py:226
  47.1 7.9 %collective-permute-start.7 = (f32[4,128,768]{2,1,0:T(8,128)}, f32[4,128,768]{2,1,0:T(8,128)S(1)}, u32[]{:S(2)}, u32[]{:S(2)}) collective-permute-start(f32[4,128,768]{2,1,0:T(8,128)} %get-tuple-element.38), channel_id=1, source_target_pairs={{0,64},{64,0},{1,65},{65,1},{2,66},{66,2},{3,67},{67,3},{4,68},{68... | collective-permute-start | bytes 4718600 | tf_op jit(solution)/shard_map/ppermute | solution.py:30
  55.0 5.5 %all-to-all-start.1 = ((bf16[8,256,128]{2,1,0:T(8,128)(2,1)}), bf16[8,256,128]{2,1,0:T(8,128)(2,1)S(1)}, u32[]{:S(2)}, u32[]{:S(2)}) async-start(bf16[8,256,128]{2,1,0:T(8,128)(2,1)} %get-tuple-element.36), calls=%async_computation.1 | async-start | bytes 1048576 | tf_op jit(solution)/shard_map/all_to_all | solution.py:344
  60.5 0.0 collective-permute-done.7.other
  60.5 0.0 copy-start
  60.5 1.4 %copy-done = f32[4,128,768]{2,1,0:T(8,128)S(1)} copy-done((f32[4,128,768]{2,1,0:T(8,128)S(1)}, f32[4,128,768]{2,1,0:T(8,128)}, u32[]{:S(2)}) %copy-start) | copy-done | bytes 1572888
  61.9 0.1 add_cores.1
  62.1 1.9 %collective-permute-start.8 = (bf16[128,768]{1,0:T(8,128)(2,1)S(1)}, bf16[128,768]{1,0:T(8,128)(2,1)S(1)}, u32[]{:S(2)}, u32[]{:S(2)}) collective-permute-start(bf16[128,768]{1,0:T(8,128)(2,1)S(1)} %get-tuple-element.41), channel_id=1, source_target_pairs={{0,8},{8,0},{16,24},{24,16},{1,9},{9,1},{17,25},{25,17},{2,10},{10... | collective-permute-start | bytes 589832 | tf_op jit(solution)/shard_map/ppermute | solution.py:34
  64.0 3.3 %collective-permute-start.9 = (bf16[128,768]{1,0:T(8,128)(2,1)S(1)}, bf16[128,768]{1,0:T(8,128)(2,1)S(1)}, u32[]{:S(2)}, u32[]{:S(2)}) collective-permute-start(bf16[128,768]{1,0:T(8,128)(2,1)S(1)} %get-tuple-element.42), channel_id=1, source_target_pairs={{0,16},{8,24},{16,0},{24,8},{1,17},{9,25},{17,1},{25,9},{2,18},{10... | collective-permute-start | bytes 589832 | tf_op jit(solution)/shard_map/ppermute | solution.py:34
  67.3 3.1 %collective-permute-start.10 = (bf16[128,768]{1,0:T(8,128)(2,1)S(1)}, bf16[128,768]{1,0:T(8,128)(2,1)S(1)}, u32[]{:S(2)}, u32[]{:S(2)}) collective-permute-start(bf16[128,768]{1,0:T(8,128)(2,1)S(1)} %get-tuple-element.43), channel_id=1, source_target_pairs={{0,24},{8,16},{16,8},{24,0},{1,25},{9,17},{17,9},{25,1},{2,26},{10... | collective-permute-start | bytes 589832 | tf_op jit(solution)/shard_map/ppermute | solution.py:34
  70.5 7.7 %all-to-all-done.1.parts = bf16[8,256,128]{2,1,0:T(8,128)(2,1)S(1)} async-done(((bf16[8,256,128]{2,1,0:T(8,128)(2,1)}), bf16[8,256,128]{2,1,0:T(8,128)(2,1)S(1)}, u32[]{:S(2)}, u32[]{:S(2)}) %all-to-all-start.1) | async-done | bytes 524320 | tf_op jit(solution)/shard_map/all_to_all | solution.py:344
  78.1 0.9 sum_rows.1
  79.0 10.0 %all-to-all-start.2 = ((bf16[8,256,128]{2,1,0:T(8,128)(2,1)}), bf16[8,256,128]{2,1,0:T(8,128)(2,1)S(1)}, u32[]{:S(2)}, u32[]{:S(2)}) async-start(bf16[8,256,128]{2,1,0:T(8,128)(2,1)} %sum_rows.1), calls=%async_computation.2 | async-start | bytes 1048576 | tf_op jit(solution)/shard_map/all_to_all | solution.py:348
  89.0 0.0 collective-permute-done.8.b
  89.1 0.0 collective-permute-done.9.c
  89.1 0.0 collective-permute-done.10.d
  89.1 0.9 finish_query.1
  89.9 17.1 %all-to-all-done.2.parts = bf16[8,256,128]{2,1,0:T(8,128)(2,1)S(1)} async-done(((bf16[8,256,128]{2,1,0:T(8,128)(2,1)}), bf16[8,256,128]{2,1,0:T(8,128)(2,1)S(1)}, u32[]{:S(2)}, u32[]{:S(2)}) %all-to-all-start.2) | async-done | bytes 524320 | tf_op jit(solution)/shard_map/all_to_all | solution.py:348
  107.0 0.9 split_heads.1
Async XLA Ops:
  0.6 28.8 %copy-start.2 = (s32[64]{0:T(128)S(1)}, s32[64]{0:T(128)}, u32[]{:S(2)}) copy-start(s32[64]{0:T(128)} %parents.1) | copy-start | bytes 772
  3.3 17.8 %collective-permute-start.1 = (bf16[1584,128]{1,0:T(8,128)(2,1)}, bf16[1584,128]{1,0:T(8,128)(2,1)S(1)}, u32[]{:S(2)}, u32[]{:S(2)}) collective-permute-start(bf16[1584,128]{1,0:T(8,128)(2,1)} %get-tuple-element.27.refs_0_), channel_id=1, source_target_pairs={{0,16},{8,24},{16,0},{24,8},{1,17},{9,25},{17,1},{25,9},{2,18},{10... | collective-permute-start | bytes 1216520 | tf_op jit(solution)/shard_map/ppermute | solution.py:34
  6.4 14.7 %collective-permute-start = (bf16[1584,128]{1,0:T(8,128)(2,1)}, bf16[1584,128]{1,0:T(8,128)(2,1)S(1)}, u32[]{:S(2)}, u32[]{:S(2)}) collective-permute-start(bf16[1584,128]{1,0:T(8,128)(2,1)} %get-tuple-element.27.refs_0_), channel_id=1, source_target_pairs={{0,8},{8,0},{16,24},{24,16},{1,9},{9,1},{17,25},{25,17},{2,10},{10... | collective-permute-start | bytes 1216520 | tf_op jit(solution)/shard_map/ppermute | solution.py:34
  9.6 22.1 %collective-permute-start.2 = (bf16[1584,128]{1,0:T(8,128)(2,1)}, bf16[1584,128]{1,0:T(8,128)(2,1)S(1)}, u32[]{:S(2)}, u32[]{:S(2)}) collective-permute-start(bf16[1584,128]{1,0:T(8,128)(2,1)} %get-tuple-element.27.refs_0_), channel_id=1, source_target_pairs={{0,24},{8,16},{16,8},{24,0},{1,25},{9,17},{17,9},{25,1},{2,26},{10... | collective-permute-start | bytes 1216520 | tf_op jit(solution)/shard_map/ppermute | solution.py:34
  11.7 28.2 %all-to-all-start = ((bf16[8,256,128]{2,1,0:T(8,128)(2,1)}), bf16[8,256,128]{2,1,0:T(8,128)(2,1)S(1)}, u32[]{:S(2)}, u32[]{:S(2)}) async-start(bf16[8,256,128]{2,1,0:T(8,128)(2,1)} %get-tuple-element.35), calls=%async_computation | async-start | bytes 1048576 | tf_op jit(solution)/shard_map/all_to_all | solution.py:336
  21.1 10.1 %copy-start.1 = (s32[9]{0:T(128)}, s32[9]{0:T(128)S(1)}, u32[]{:S(2)}) copy-start(s32[9]{0:T(128)S(1)} %stack.39.ids) | copy-start | bytes 112
  21.1 10.1 %copy-start.5 = (bf16[1584,128]{1,0:T(8,128)(2,1)}, bf16[1584,128]{1,0:T(8,128)(2,1)S(1)}, u32[]{:S(2)}) copy-start(bf16[1584,128]{1,0:T(8,128)(2,1)S(1)} %collective-permute-done.1.refs_2_) | copy-start | bytes 1216516
  21.1 10.1 %copy-start.6 = (bf16[1584,128]{1,0:T(8,128)(2,1)}, bf16[1584,128]{1,0:T(8,128)(2,1)S(1)}, u32[]{:S(2)}) copy-start(bf16[1584,128]{1,0:T(8,128)(2,1)S(1)} %collective-permute-done.refs_1_) | copy-start | bytes 1216516
  21.1 10.6 %collective-permute-start.3 = (bf16[1584,128]{1,0:T(8,128)(2,1)}, bf16[1584,128]{1,0:T(8,128)(2,1)S(1)}, u32[]{:S(2)}, u32[]{:S(2)}) collective-permute-start(bf16[1584,128]{1,0:T(8,128)(2,1)} %get-tuple-element.27.refs_0_), channel_id=1, source_target_pairs={{0,64},{64,0},{1,65},{65,1},{2,66},{66,2},{3,67},{67,3},{4,68},{68... | collective-permute-start | bytes 1216520 | tf_op jit(solution)/shard_map/ppermute | solution.py:30
  25.1 6.6 %collective-permute-start.4 = (bf16[1584,128]{1,0:T(8,128)(2,1)S(1)}, bf16[1584,128]{1,0:T(8,128)(2,1)S(1)}, u32[]{:S(2)}, u32[]{:S(2)}) collective-permute-start(bf16[1584,128]{1,0:T(8,128)(2,1)S(1)} %collective-permute-done.refs_1_), channel_id=1, source_target_pairs={{0,64},{64,0},{1,65},{65,1},{2,66},{66,2},{3,67},{67,3},{4,68},{68... | collective-permute-start | bytes 1216520 | tf_op jit(solution)/shard_map/ppermute | solution.py:30
  27.1 4.7 %collective-permute-start.5 = (bf16[1584,128]{1,0:T(8,128)(2,1)S(1)}, bf16[1584,128]{1,0:T(8,128)(2,1)S(1)}, u32[]{:S(2)}, u32[]{:S(2)}) collective-permute-start(bf16[1584,128]{1,0:T(8,128)(2,1)S(1)} %collective-permute-done.1.refs_2_), channel_id=1, source_target_pairs={{0,64},{64,0},{1,65},{65,1},{2,66},{66,2},{3,67},{67,3},{4,68},{68... | collective-permute-start | bytes 1216520 | tf_op jit(solution)/shard_map/ppermute | solution.py:30
  31.2 0.5 copy-start.3
  31.7 8.2 %copy-start.7 = (bf16[1584,128]{1,0:T(8,128)(2,1)}, bf16[1584,128]{1,0:T(8,128)(2,1)S(1)}, u32[]{:S(2)}) copy-start(bf16[1584,128]{1,0:T(8,128)(2,1)S(1)} %collective-permute-done.2.refs_3_) | copy-start | bytes 1216516
  31.7 8.2 %copy-start.8 = (bf16[1584,128]{1,0:T(8,128)(2,1)}, bf16[1584,128]{1,0:T(8,128)(2,1)S(1)}, u32[]{:S(2)}) copy-start(bf16[1584,128]{1,0:T(8,128)(2,1)S(1)} %collective-permute-done.3.refs_4_) | copy-start | bytes 1216516
  31.8 8.1 %copy-start.9 = (bf16[1584,128]{1,0:T(8,128)(2,1)}, bf16[1584,128]{1,0:T(8,128)(2,1)S(1)}, u32[]{:S(2)}) copy-start(bf16[1584,128]{1,0:T(8,128)(2,1)S(1)} %collective-permute-done.4.refs_5_) | copy-start | bytes 1216516
  31.8 8.1 %copy-start.10 = (bf16[1584,128]{1,0:T(8,128)(2,1)}, bf16[1584,128]{1,0:T(8,128)(2,1)S(1)}, u32[]{:S(2)}) copy-start(bf16[1584,128]{1,0:T(8,128)(2,1)S(1)} %collective-permute-done.5.refs_6_) | copy-start | bytes 1216516
  31.8 8.1 %collective-permute-start.6 = (bf16[1584,128]{1,0:T(8,128)(2,1)S(1)}, bf16[1584,128]{1,0:T(8,128)(2,1)S(1)}, u32[]{:S(2)}, u32[]{:S(2)}) collective-permute-start(bf16[1584,128]{1,0:T(8,128)(2,1)S(1)} %collective-permute-done.2.refs_3_), channel_id=1, source_target_pairs={{0,64},{64,0},{1,65},{65,1},{2,66},{66,2},{3,67},{67,3},{4,68},{68... | collective-permute-start | bytes 1216520 | tf_op jit(solution)/shard_map/ppermute | solution.py:30
  39.9 0.8 copy-start.4
  40.7 0.8 copy-start.11
  47.1 13.4 %collective-permute-start.7 = (f32[4,128,768]{2,1,0:T(8,128)}, f32[4,128,768]{2,1,0:T(8,128)S(1)}, u32[]{:S(2)}, u32[]{:S(2)}) collective-permute-start(f32[4,128,768]{2,1,0:T(8,128)} %get-tuple-element.38), channel_id=1, source_target_pairs={{0,64},{64,0},{1,65},{65,1},{2,66},{66,2},{3,67},{67,3},{4,68},{68... | collective-permute-start | bytes 4718600 | tf_op jit(solution)/shard_map/ppermute | solution.py:30
  55.0 23.1 %all-to-all-start.1 = ((bf16[8,256,128]{2,1,0:T(8,128)(2,1)}), bf16[8,256,128]{2,1,0:T(8,128)(2,1)S(1)}, u32[]{:S(2)}, u32[]{:S(2)}) async-start(bf16[8,256,128]{2,1,0:T(8,128)(2,1)} %get-tuple-element.36), calls=%async_computation.1 | async-start | bytes 1048576 | tf_op jit(solution)/shard_map/all_to_all | solution.py:344
  60.5 1.4 %copy-start = (f32[4,128,768]{2,1,0:T(8,128)S(1)}, f32[4,128,768]{2,1,0:T(8,128)}, u32[]{:S(2)}) copy-start(f32[4,128,768]{2,1,0:T(8,128)} %get-tuple-element.37.mine) | copy-start | bytes 4718596
  62.1 27.0 %collective-permute-start.8 = (bf16[128,768]{1,0:T(8,128)(2,1)S(1)}, bf16[128,768]{1,0:T(8,128)(2,1)S(1)}, u32[]{:S(2)}, u32[]{:S(2)}) collective-permute-start(bf16[128,768]{1,0:T(8,128)(2,1)S(1)} %get-tuple-element.41), channel_id=1, source_target_pairs={{0,8},{8,0},{16,24},{24,16},{1,9},{9,1},{17,25},{25,17},{2,10},{10... | collective-permute-start | bytes 589832 | tf_op jit(solution)/shard_map/ppermute | solution.py:34
  64.0 25.1 %collective-permute-start.9 = (bf16[128,768]{1,0:T(8,128)(2,1)S(1)}, bf16[128,768]{1,0:T(8,128)(2,1)S(1)}, u32[]{:S(2)}, u32[]{:S(2)}) collective-permute-start(bf16[128,768]{1,0:T(8,128)(2,1)S(1)} %get-tuple-element.42), channel_id=1, source_target_pairs={{0,16},{8,24},{16,0},{24,8},{1,17},{9,25},{17,1},{25,9},{2,18},{10... | collective-permute-start | bytes 589832 | tf_op jit(solution)/shard_map/ppermute | solution.py:34
  67.3 21.8 %collective-permute-start.10 = (bf16[128,768]{1,0:T(8,128)(2,1)S(1)}, bf16[128,768]{1,0:T(8,128)(2,1)S(1)}, u32[]{:S(2)}, u32[]{:S(2)}) collective-permute-start(bf16[128,768]{1,0:T(8,128)(2,1)S(1)} %get-tuple-element.43), channel_id=1, source_target_pairs={{0,24},{8,16},{16,8},{24,0},{1,25},{9,17},{17,9},{25,1},{2,26},{10... | collective-permute-start | bytes 589832 | tf_op jit(solution)/shard_map/ppermute | solution.py:34
  79.0 28.0 %all-to-all-start.2 = ((bf16[8,256,128]{2,1,0:T(8,128)(2,1)}), bf16[8,256,128]{2,1,0:T(8,128)(2,1)S(1)}, u32[]{:S(2)}, u32[]{:S(2)}) async-start(bf16[8,256,128]{2,1,0:T(8,128)(2,1)} %sum_rows.1), calls=%async_computation.2 | async-start | bytes 1048576 | tf_op jit(solution)/shard_map/all_to_all | solution.py:348
